TPU v7x, 32 devices: a whole 2x2x4 slice. The times are simulated.
32 devices in a mesh: seq: 16 (over z, x, core), tp: 2 (over y).
Axes of the slice: x: 2, y: 2, z: 4, core: 2. Of those that a mesh axis runs over, the one named last changes fastest.
Arguments:
- block_in: bfloat16 [2048, 2048], P(('seq', 'tp')), may hold values from -6 to 6
- cotangent: bfloat16 [2048, 2048], P('seq'), may hold values from -6 to 6
- segment_ids: int32 [2048], replicated, may hold values from 0 to 7, never falling along the last dimension, each value on 1 to 1024 neighbouring positions
- norm_gain: float32 [2048], replicated, may hold values from 0.5 to 1.5
- in_weight: float32 [2048, 2, 4096], P('seq', None, 'tp'), may hold values from -0.125 to 0.125
- out_weight: float32 [2048, 4096], P('seq', 'tp'), may hold values from -0.1875 to 0.1875
- conv_weight: float32 [4, 4096], P(None, 'tp'), may hold values from -3 to 3
- conv_bias: float32 [4096], P('tp'), may hold values from -0.5 to 0.5
- select_weight: float32 [160, 4096], P(None, 'tp'), may hold values from -0.09375 to 0.09375
- step_weight: float32 [128, 4096], P(None, 'tp'), may hold values from -0.5 to 0.5
- step_bias: float32 [4096], P('tp'), may hold values from -6 to -2
- decay_log: float32 [16, 4096], P(None, 'tp'), may hold values from -5 to 2
- skip_gain: float32 [4096], P('tp'), may hold values from 0.5 to 1.5
- norm_moment: float32 [2048], replicated, may hold values from 1000 to 30000
- in_rows: float32 [2048], P('seq'), may hold values from 3000 to 30000
- in_cols: float32 [2, 4096], P(None, 'tp'), may hold values from 3000 to 30000
- out_rows: float32 [2048], P('seq'), may hold values from 3000 to 30000
- out_cols: float32 [4096], P('tp'), may hold values from 3000 to 30000
- conv_rows: float32 [4], replicated, may hold values from 1000 to 30000
- conv_cols: float32 [4096], P('tp'), may hold values from 1000 to 30000
- bias_moment: float32 [4096], P('tp'), may hold values from 100 to 10000
- select_rows: float32 [160], replicated, may hold values from 10 to 10000
- select_cols: float32 [4096], P('tp'), may hold values from 30000 to 30000000
- step_rows: float32 [128], replicated, may hold values from 10 to 10000
- step_cols: float32 [4096], P('tp'), may hold values from 10 to 10000
- step_moment: float32 [4096], P('tp'), may hold values from 10 to 10000
- decay_rows: float32 [16], replicated, may hold values from 10 to 10000
- decay_cols: float32 [4096], P('tp'), may hold values from 10 to 10000
- skip_moment: float32 [4096], P('tp'), may hold values from 100 to 10000
Outputs:
- block_out: float32 [2048, 2048], P(('seq', 'tp'))
- input_grad: float32 [2048, 2048], P(('seq', 'tp'))
- norm_gain_grad: float32 [2048], replicated
- norm_gain_new: float32 [2048], replicated
- norm_gain_copy: bfloat16 [2048], replicated
- norm_moment_new: float32 [2048], replicated
- in_weight_grad: float32 [2048, 2, 4096], P('seq', None, 'tp')
- in_weight_new: float32 [2048, 2, 4096], P('seq', None, 'tp')
- in_weight_copy: bfloat16 [2048, 2, 4096], P('seq', None, 'tp')
- in_rows_new: float32 [2048], P('seq')
- in_cols_new: float32 [2, 4096], P(None, 'tp')
- out_weight_grad: float32 [2048, 4096], P('seq', 'tp')
- out_weight_new: float32 [2048, 4096], P('seq', 'tp')
- out_weight_copy: bfloat16 [2048, 4096], P('seq', 'tp')
- out_rows_new: float32 [2048], P('seq')
- out_cols_new: float32 [4096], P('tp')
- conv_weight_grad: float32 [4, 4096], P(None, 'tp')
- conv_weight_new: float32 [4, 4096], P(None, 'tp')
- conv_weight_copy: bfloat16 [4, 4096], P(None, 'tp')
- conv_rows_new: float32 [4], replicated
- conv_cols_new: float32 [4096], P('tp')
- conv_bias_grad: float32 [4096], P('tp')
- conv_bias_new: float32 [4096], P('tp')
- conv_bias_copy: bfloat16 [4096], P('tp')
- bias_moment_new: float32 [4096], P('tp')
- select_weight_grad: float32 [160, 4096], P(None, 'tp')
- select_weight_new: float32 [160, 4096], P(None, 'tp')
- select_weight_copy: bfloat16 [160, 4096], P(None, 'tp')
- select_rows_new: float32 [160], replicated
- select_cols_new: float32 [4096], P('tp')
- step_weight_grad: float32 [128, 4096], P(None, 'tp')
- step_weight_new: float32 [128, 4096], P(None, 'tp')
- step_weight_copy: bfloat16 [128, 4096], P(None, 'tp')
- step_rows_new: float32 [128], replicated
- step_cols_new: float32 [4096], P('tp')
- step_bias_grad: float32 [4096], P('tp')
- step_bias_new: float32 [4096], P('tp')
- step_bias_copy: bfloat16 [4096], P('tp')
- step_moment_new: float32 [4096], P('tp')
- decay_log_grad: float32 [16, 4096], P(None, 'tp')
- decay_log_new: float32 [16, 4096], P(None, 'tp')
- decay_log_copy: bfloat16 [16, 4096], P(None, 'tp')
- decay_rows_new: float32 [16], replicated
- decay_cols_new: float32 [4096], P('tp')
- skip_gain_grad: float32 [4096], P('tp')
- skip_gain_new: float32 [4096], P('tp')
- skip_gain_copy: bfloat16 [4096], P('tp')
- skip_moment_new: float32 [4096], P('tp')
Inputs may be any that keep to these rules, and one draw needn't show every extreme that they name: `segment_ids`: never falling along the stream; each document has 1 to 1024 tokens and one has exactly 1024.
All inputs are finite; a program needn't handle non-finite values.
Results may differ from a plain program's by a relative error of at most 0.0075.
The roundings to bfloat16 on the way count: a program that leaves them out, or rounds other values in their place, can miss the bound.
Values may be sent and summed in bfloat16 or wider, within the bound.
A program may use at most 112 MiB of HBM per device.

v0:
```python
import jax
import jax.numpy as jnp
from jax import lax
from jax.sharding import PartitionSpec as P

EPS_NORM = 1e-05
EPS_FACTOR = 1e-30
DECAY = 0.5
CLIP = 0.5
RATES = (0.45, 0.02, 0.03, 0.1, 0.05, 0.016, 0.09, 1.8, 0.3, 0.45)
highest = lax.Precision.HIGHEST


def passed_along(value, axis, steps):
    count = lax.axis_size(axis)
    initial, last = (max(0, -steps), min(count, count - steps))
    return lax.ppermute(value, axis, [(source, source + steps) for source in range(initial, last)])


def prefix(value, axis, join, neutral, backward):
    count, mine = (lax.axis_size(axis), lax.axis_index(axis))
    pieces = jax.tree.map(lambda part: lax.all_gather(part, axis), value)
    if backward:
        pieces = jax.tree.map(lambda part: part[::-1], pieces)
        mine = count - 1 - mine
    subtotal = jax.tree.map(
        lambda part, zero: jnp.full_like(part, 0) + jnp.asarray(zero, part.dtype), value, neutral
    )

    def step(position, subtotal):
        longer = join(subtotal, jax.tree.map(lambda part: part[position], pieces))
        return jax.tree.map(lambda new, old: jnp.where(position < mine, new, old), longer, subtotal)

    return lax.fori_loop(0, count - 1, step, subtotal)


def silu_slope(values):
    sigmoid_v = jax.nn.sigmoid(values)
    return sigmoid_v * (1.0 + values * (1.0 - sigmoid_v))


def compose(earlier, later):
    return (later[0] * earlier[0], later[0] * earlier[1] + later[1])


def widen_last(piece_in, index_of, total_len):
    zero_block = jnp.zeros(piece_in.shape[:-1] + (total_len,), jnp.float32)
    return lax.dynamic_update_slice_in_dim(
        zero_block, piece_in, index_of * piece_in.shape[-1], piece_in.ndim - 1
    )


def narrow(full_array, index_of, size_of):
    return lax.dynamic_slice_in_dim(full_array, index_of * size_of, size_of, full_array.ndim - 1)


def factor_update(full_grad, local_grad, rows_old, cols_old):
    rows_new = DECAY * rows_old + (1.0 - DECAY) * (
        jnp.mean(full_grad * full_grad, axis=1) + EPS_FACTOR
    )
    cols_new = DECAY * cols_old + (1.0 - DECAY) * (
        jnp.mean(local_grad * local_grad, axis=0) + EPS_FACTOR
    )
    scale_sq = rows_new[:, None] * cols_new[None, :] / jnp.mean(rows_new)
    return (rows_new, cols_new, local_grad * lax.rsqrt(scale_sq))


def moment_update(grad_in, moment_old):
    moment_new = DECAY * moment_old + (1.0 - DECAY) * (grad_in * grad_in + EPS_FACTOR)
    return (moment_new, grad_in * lax.rsqrt(moment_new))


def sum_squares(update):
    return jnp.sum(update * update)


def apply_step(weight, update, total_sum, count_all, step_rate):
    root_mean = jnp.sqrt(total_sum / count_all)
    return weight - step_rate * update / jnp.maximum(1.0, root_mean / CLIP)


def block_masks(lower_blk, step_b, keep_b):
    cum_b = jnp.dot(lower_blk, step_b, precision=highest)
    resets_b = jnp.dot(lower_blk, 1.0 - keep_b, precision=highest)
    same_b = (resets_b[:, None] == resets_b[None, :]).astype(jnp.float32) * lower_blk
    head_b = (resets_b == 0.0).astype(jnp.float32)
    tail_b = (resets_b == resets_b[-1]).astype(jnp.float32)
    return (cum_b, same_b, head_b, tail_b)


def decay_matrix(rate_row, cum_b, same_b):
    live = same_b[:, :, None] > 0.0
    spread = jnp.where(live, cum_b[:, None, :] - cum_b[None, :, :], 0.0)
    return jnp.where(live, jnp.exp(rate_row[None, None, :] * spread), 0.0)


def on_device(
    block_in,
    cotangent,
    segment_ids,
    norm_gain,
    in_weight,
    out_weight,
    conv_weight,
    conv_bias,
    select_weight,
    step_weight,
    step_bias,
    decay_log,
    skip_gain,
    norm_moment,
    in_rows,
    in_cols,
    out_rows,
    out_cols,
    conv_rows,
    conv_cols,
    bias_moment,
    select_rows,
    select_cols,
    step_rows,
    step_cols,
    step_moment,
    decay_rows,
    decay_cols,
    skip_moment,
):
    tp_count = lax.axis_size("tp")
    seq_index = lax.axis_index("seq")
    tp_index = lax.axis_index("tp")
    seq_first = (seq_index == 0).astype(jnp.float32)
    tp_first = (tp_index == 0).astype(jnp.float32)
    half_rows, model_dim = block_in.shape
    row_count = cotangent.shape[0]
    inner_dim = in_weight.shape[2]
    channels = inner_dim * tp_count
    conv_taps = conv_weight.shape[0]
    states = decay_log.shape[0]
    step_rank = step_weight.shape[0]
    row_share = in_weight.shape[0]
    block_len = min(row_count, max(32, row_count // 16))
    blocks = row_count // block_len
    id_padded = jnp.concatenate(
        [
            jnp.full((conv_taps - 1,), -1, jnp.int32),
            segment_ids,
            jnp.full((conv_taps - 1,), -2, jnp.int32),
        ]
    )
    window = lax.dynamic_slice_in_dim(
        id_padded, seq_index * row_count, row_count + 2 * (conv_taps - 1)
    )
    local_ids = window[conv_taps - 1 : conv_taps - 1 + row_count]
    keep_mask = (local_ids == window[conv_taps - 2 : conv_taps - 2 + row_count]).astype(jnp.float32)
    lower_tri = (
        lax.broadcasted_iota(jnp.int32, (row_count, row_count), 0)
        >= lax.broadcasted_iota(jnp.int32, (row_count, row_count), 1)
    ).astype(jnp.float32)
    lower_blk = lower_tri[:block_len, :block_len]
    resets = jnp.dot(lower_tri, 1.0 - keep_mask, precision=highest)
    keep_pre = (resets == 0.0).astype(jnp.float32)
    keep_suf = (resets == resets[-1]).astype(jnp.float32)
    keep_all = (resets[-1] == 0.0).astype(jnp.float32)
    residual = block_in.astype(jnp.float32)
    mean_sq = jnp.mean(residual * residual, axis=1, keepdims=True)
    inv_rms = lax.rsqrt(mean_sq + EPS_NORM)
    normed = residual * inv_rms
    hidden = lax.all_gather(
        (normed * norm_gain[None, :]).astype(jnp.bfloat16), "tp", axis=0, tiled=True
    )
    in_full, out_full = (
        lax.all_gather(in_weight.astype(jnp.bfloat16), "seq", axis=0, tiled=True),
        lax.all_gather(out_weight.astype(jnp.bfloat16), "seq", axis=0, tiled=True),
    )
    projected = jnp.einsum("td,dke->tke", hidden, in_full, preferred_element_type=jnp.float32)
    conv_in = projected[:, 0].astype(jnp.bfloat16)
    gate_pre = projected[:, 1]
    rim_rows = passed_along(conv_in[row_count - (conv_taps - 1) :], "seq", 1)
    ext_rows = jnp.concatenate([rim_rows, conv_in], axis=0).astype(jnp.float32)
    same_docs = []
    conv_pre = jnp.zeros_like(gate_pre) + conv_bias[None, :]
    for shift_lag in range(conv_taps):
        first_row = conv_taps - 1 - shift_lag
        same_doc = (window[first_row : first_row + row_count] == local_ids).astype(jnp.float32)[
            :, None
        ]
        same_docs.append(same_doc)
        conv_pre = (
            conv_pre
            + conv_weight[shift_lag][None, :]
            * ext_rows[first_row : first_row + row_count]
            * same_doc
        )
    conv_out = jax.nn.silu(conv_pre).astype(jnp.bfloat16)
    conv_value = conv_out.astype(jnp.float32)
    select_low = select_weight.astype(jnp.bfloat16)
    select_out = lax.psum(
        jnp.einsum("te,ke->tk", conv_out, select_low, preferred_element_type=jnp.float32), "tp"
    )
    step_in = select_out[:, :step_rank].astype(jnp.bfloat16)
    state_in = select_out[:, step_rank : step_rank + states]
    state_out = select_out[:, step_rank + states :]
    step_low = step_weight.astype(jnp.bfloat16)
    step_pre = jnp.dot(step_in, step_low, preferred_element_type=jnp.float32) + step_bias[None, :]
    step_size = jax.nn.softplus(step_pre)
    decay_rate = -jnp.exp(decay_log)
    drive = step_size * conv_value
    cum_pre = jnp.dot(lower_tri, step_size, precision=highest)
    total_step = cum_pre[-1]
    cum_suf = total_step[None, :] - cum_pre
    masked_drive = drive * keep_suf[:, None]

    def state_term(pair_in):
        rate_row, column = pair_in
        return jnp.sum(
            jnp.exp(rate_row[None, :] * cum_suf) * masked_drive * column[:, None], axis=0
        )

    local_state = lax.map(state_term, (decay_rate, state_in.T))
    product = jnp.exp(decay_rate * total_step[None, :]) * keep_all
    identity = (jnp.ones_like(product), jnp.zeros_like(product))
    _, incoming = prefix((product, local_state), "seq", compose, identity, False)
    step_blocks = step_size.reshape(blocks, block_len, inner_dim)
    drive_blocks = drive.reshape(blocks, block_len, inner_dim)
    enter_blocks = state_in.reshape(blocks, block_len, states)
    leave_blocks = state_out.reshape(blocks, block_len, states)
    keep_blocks = keep_mask.reshape(blocks, block_len)

    def block_forward(state_now, inputs):
        step_b, drive_b, enter_b, keep_b, leave_b = inputs
        cum_b, same_b, head_b, _ = block_masks(lower_blk, step_b, keep_b)

        def per_state(args):
            rate_row, enter_col, leave_col, start_row = args
            weights_b = decay_matrix(rate_row, cum_b, same_b)
            rows_b = jnp.sum(weights_b * (drive_b * enter_col[:, None])[None], axis=1)
            rows_b = (
                rows_b + jnp.exp(rate_row[None, :] * cum_b) * head_b[:, None] * start_row[None, :]
            )
            return (leave_col[:, None] * rows_b, rows_b[-1])

        terms, ends = lax.map(per_state, (decay_rate, enter_b.T, leave_b.T, state_now))
        return (ends, (jnp.sum(terms, axis=0), state_now))

    _, (scanned, block_starts) = lax.scan(
        block_forward,
        incoming,
        (step_blocks, drive_blocks, enter_blocks, keep_blocks, leave_blocks),
    )
    scanned = scanned.reshape(row_count, inner_dim)
    mixed = scanned + skip_gain[None, :] * conv_value
    gate_act = jax.nn.silu(gate_pre)
    gated = (mixed * gate_act).astype(jnp.bfloat16)
    branch = jnp.einsum("te,de->td", gated, out_full, preferred_element_type=jnp.float32)
    block_out = residual + lax.psum_scatter(
        branch.astype(jnp.bfloat16), "tp", scatter_dimension=0, tiled=True
    ).astype(jnp.float32)
    in_back, out_back = (
        lax.all_gather(in_weight.astype(jnp.bfloat16), "seq", axis=0, tiled=True),
        lax.all_gather(out_weight.astype(jnp.bfloat16), "seq", axis=0, tiled=True),
    )
    d_gated = jnp.einsum("td,de->te", cotangent, out_back, preferred_element_type=jnp.float32)
    d_out_w = jnp.einsum("td,te->de", cotangent, gated, preferred_element_type=jnp.float32)
    d_mixed = d_gated * gate_act
    d_gate = (d_gated * mixed * silu_slope(gate_pre)).astype(jnp.bfloat16)
    skip_grad = jnp.sum(d_mixed * conv_value, axis=0)
    masked_grad = d_mixed * keep_pre[:, None]

    def adjoint_term(pair_in):
        rate_row, column = pair_in
        return jnp.sum(jnp.exp(rate_row[None, :] * cum_pre) * masked_grad * column[:, None], axis=0)

    local_adjoint = lax.map(adjoint_term, (decay_rate, state_out.T))
    _, later_adjoint = prefix((product, local_adjoint), "seq", compose, identity, True)

    def block_backward(carry_in, inputs):
        following, decay_acc = carry_in
        step_b, drive_b, enter_b, keep_b, leave_b, grad_b, block_start = inputs
        cum_b, same_b, head_b, tail_b = block_masks(lower_blk, step_b, keep_b)

        def per_state(args):
            rate_row, enter_col, leave_col, start_row, follow_row = args
            weights_b = decay_matrix(rate_row, cum_b, same_b)
            rows_b = jnp.sum(weights_b * (drive_b * enter_col[:, None])[None], axis=1)
            rows_b = (
                rows_b + jnp.exp(rate_row[None, :] * cum_b) * head_b[:, None] * start_row[None, :]
            )
            previous = jnp.concatenate([start_row[None], rows_b[:-1]], axis=0)
            factor_b = jnp.exp(rate_row[None, :] * step_b) * keep_b[:, None]
            source = grad_b * leave_col[:, None]
            adjoint = jnp.sum(weights_b * source[:, None, :], axis=0)
            adjoint = (
                adjoint
                + jnp.exp(rate_row[None, :] * (cum_b[-1][None, :] - cum_b))
                * tail_b[:, None]
                * follow_row[None, :]
            )
            decay_part = adjoint * previous * factor_b
            return (
                adjoint * enter_col[:, None],
                decay_part * rate_row[None, :],
                jnp.sum(decay_part * step_b, axis=0),
                jnp.sum(adjoint * drive_b, axis=1),
                jnp.sum(rows_b * grad_b, axis=1),
                factor_b[0] * adjoint[0],
            )

        drive_parts, step_parts, decay_parts, enter_cols, leave_cols, follow_out = lax.map(
            per_state, (decay_rate, enter_b.T, leave_b.T, block_start, following)
        )
        return (
            (follow_out, decay_acc + decay_parts),
            (jnp.sum(drive_parts, axis=0), jnp.sum(step_parts, axis=0), enter_cols.T, leave_cols.T),
        )

    (_, decay_acc), (drive_grad, step_grad, enter_grad, leave_grad) = lax.scan(
        block_backward,
        (later_adjoint, jnp.zeros_like(decay_rate)),
        (
            step_blocks,
            drive_blocks,
            enter_blocks,
            keep_blocks,
            leave_blocks,
            d_mixed.reshape(blocks, block_len, inner_dim),
            block_starts,
        ),
        reverse=True,
    )
    drive_grad = drive_grad.reshape(row_count, inner_dim)
    d_step = drive_grad * conv_value + step_grad.reshape(row_count, inner_dim)
    decay_grad = decay_acc * decay_rate
    d_step_pre = (d_step * jax.nn.sigmoid(step_pre)).astype(jnp.bfloat16)
    step_bias_grad = jnp.sum(d_step_pre.astype(jnp.float32), axis=0)
    step_w_grad = jnp.einsum("tr,te->re", step_in, d_step_pre, preferred_element_type=jnp.float32)
    d_step_in = jnp.einsum("te,re->tr", d_step_pre, step_low, preferred_element_type=jnp.float32)
    select_grads = jnp.concatenate(
        [d_step_in, enter_grad.reshape(row_count, states), leave_grad.reshape(row_count, states)],
        axis=1,
    )
    d_select = lax.psum(select_grads, "tp").astype(jnp.bfloat16)
    select_w_grad = jnp.einsum("tk,te->ke", d_select, conv_out, preferred_element_type=jnp.float32)
    d_conv = (
        drive_grad * step_size
        + d_mixed * skip_gain[None, :]
        + jnp.einsum("tk,ke->te", d_select, select_low, preferred_element_type=jnp.float32)
    )
    d_conv_pre = d_conv * silu_slope(conv_pre)
    rim_next = passed_along(d_conv_pre[: conv_taps - 1], "seq", -1)
    ext_grads = jnp.concatenate([d_conv_pre, rim_next], axis=0)
    ids_after = window[conv_taps - 1 :]
    d_conv_in = jnp.zeros_like(d_conv_pre)
    conv_w_rows = []
    for shift_lag in range(conv_taps):
        first_row = conv_taps - 1 - shift_lag
        later_same = (ids_after[shift_lag : shift_lag + row_count] == local_ids).astype(
            jnp.float32
        )[:, None]
        d_conv_in = (
            d_conv_in
            + conv_weight[shift_lag][None, :]
            * ext_grads[shift_lag : shift_lag + row_count]
            * later_same
        )
        conv_w_rows.append(
            jnp.sum(
                d_conv_pre * ext_rows[first_row : first_row + row_count] * same_docs[shift_lag],
                axis=0,
            )
        )
    conv_w_grad = jnp.stack(conv_w_rows, axis=0)
    conv_b_grad = jnp.sum(d_conv_pre, axis=0)
    d_projected = jnp.stack([d_conv_in.astype(jnp.bfloat16), d_gate], axis=1)
    d_hidden = lax.psum_scatter(
        jnp.einsum("tke,dke->td", d_projected, in_back, preferred_element_type=jnp.float32),
        "tp",
        scatter_dimension=0,
        tiled=True,
    )
    d_in_w = jnp.einsum("td,tke->dke", hidden, d_projected, preferred_element_type=jnp.float32)
    in_grad, out_grad = (
        lax.psum_scatter(d_in_w, "seq", scatter_dimension=0, tiled=True),
        lax.psum_scatter(d_out_w, "seq", scatter_dimension=0, tiled=True),
    )
    gain_part = jnp.sum(d_hidden * normed, axis=0)
    scaled = d_hidden * norm_gain[None, :]
    cot_half = lax.dynamic_slice_in_dim(cotangent, tp_index * half_rows, half_rows, 0).astype(
        jnp.float32
    )
    input_grad = cot_half + inv_rms * (
        scaled - normed * jnp.mean(scaled * normed, axis=1, keepdims=True)
    )
    in_square = in_grad * in_grad
    in_row_piece = (DECAY * in_rows + (1.0 - DECAY) * EPS_FACTOR) * tp_first + (
        1.0 - DECAY
    ) * jnp.sum(in_square, axis=(1, 2)) / (2 * channels)
    in_col_piece = (DECAY * in_cols + (1.0 - DECAY) * EPS_FACTOR) * seq_first + (
        1.0 - DECAY
    ) * jnp.sum(in_square, axis=0) / model_dim
    out_square = out_grad * out_grad
    out_row_piece = (DECAY * out_rows + (1.0 - DECAY) * EPS_FACTOR) * tp_first + (
        1.0 - DECAY
    ) * jnp.sum(out_square, axis=1) / channels
    out_col_piece = (DECAY * out_cols + (1.0 - DECAY) * EPS_FACTOR) * seq_first + (
        1.0 - DECAY
    ) * jnp.sum(out_square, axis=0) / model_dim
    vector_grads = jnp.stack([conv_b_grad, step_bias_grad, skip_grad], axis=0)
    (
        conv_full,
        vector_full,
        select_full,
        step_full,
        decay_full,
        gain_grad,
        in_rows_all,
        in_cols_all,
        out_rows_all,
        out_cols_all,
    ) = lax.psum(
        (
            widen_last(conv_w_grad, tp_index, channels),
            widen_last(vector_grads, tp_index, channels),
            widen_last(select_w_grad, tp_index, channels),
            widen_last(step_w_grad, tp_index, channels),
            widen_last(decay_grad, tp_index, channels),
            gain_part,
            widen_last(in_row_piece, seq_index, model_dim),
            widen_last(in_col_piece, tp_index, channels),
            widen_last(out_row_piece, seq_index, model_dim),
            widen_last(out_col_piece, tp_index, channels),
        ),
        ("seq", "tp"),
    )
    conv_local = narrow(conv_full, tp_index, inner_dim)
    vector_local = narrow(vector_full, tp_index, inner_dim)
    select_local = narrow(select_full, tp_index, inner_dim)
    step_local = narrow(step_full, tp_index, inner_dim)
    decay_local = narrow(decay_full, tp_index, inner_dim)
    conv_rows_new, conv_cols_new, conv_update = factor_update(
        conv_full, conv_local, conv_rows, conv_cols
    )
    select_rows_new, select_cols_new, select_update = factor_update(
        select_full, select_local, select_rows, select_cols
    )
    step_rows_new, step_cols_new, stepw_update = factor_update(
        step_full, step_local, step_rows, step_cols
    )
    decay_rows_new, decay_cols_new, decay_update = factor_update(
        decay_full, decay_local, decay_rows, decay_cols
    )
    bias_moment_new, convb_update = moment_update(vector_local[0], bias_moment)
    step_moment_new, stepb_update = moment_update(vector_local[1], step_moment)
    skip_moment_new, skip_update = moment_update(vector_local[2], skip_moment)
    gain_moment_new, gain_update = moment_update(gain_grad, norm_moment)
    in_rows_new = narrow(in_rows_all, seq_index, row_share)
    in_cols_new = narrow(in_cols_all, tp_index, inner_dim)
    in_update = in_grad * lax.rsqrt(
        in_rows_new[:, None, None] * in_cols_new[None] / jnp.mean(in_rows_all)
    )
    out_rows_new = narrow(out_rows_all, seq_index, row_share)
    out_cols_new = narrow(out_cols_all, tp_index, inner_dim)
    out_update = out_grad * lax.rsqrt(
        out_rows_new[:, None] * out_cols_new[None, :] / jnp.mean(out_rows_all)
    )
    clip_totals = lax.psum(
        jnp.stack(
            [
                sum_squares(in_update),
                sum_squares(out_update),
                seq_first * sum_squares(conv_update),
                seq_first * sum_squares(select_update),
                seq_first * sum_squares(stepw_update),
                seq_first * sum_squares(decay_update),
                seq_first * sum_squares(convb_update),
                seq_first * sum_squares(stepb_update),
                seq_first * sum_squares(skip_update),
            ]
        ),
        ("seq", "tp"),
    )
    gain_new = apply_step(norm_gain, gain_update, sum_squares(gain_update), model_dim, RATES[0])
    in_new = apply_step(in_weight, in_update, clip_totals[0], model_dim * 2 * channels, RATES[1])
    out_new = apply_step(out_weight, out_update, clip_totals[1], model_dim * channels, RATES[2])
    convw_new = apply_step(conv_weight, conv_update, clip_totals[2], conv_taps * channels, RATES[3])
    convb_new = apply_step(conv_bias, convb_update, clip_totals[6], channels, RATES[4])
    select_new = apply_step(
        select_weight, select_update, clip_totals[3], select_weight.shape[0] * channels, RATES[5]
    )
    stepw_new = apply_step(
        step_weight, stepw_update, clip_totals[4], step_rank * channels, RATES[6]
    )
    stepb_new = apply_step(step_bias, stepb_update, clip_totals[7], channels, RATES[7])
    decay_new = apply_step(decay_log, decay_update, clip_totals[5], states * channels, RATES[8])
    skip_new = apply_step(skip_gain, skip_update, clip_totals[8], channels, RATES[9])
    low_type = jnp.bfloat16
    return (
        block_out,
        input_grad,
        gain_grad,
        gain_new,
        gain_new.astype(low_type),
        gain_moment_new,
        in_grad,
        in_new,
        in_new.astype(low_type),
        in_rows_new,
        in_cols_new,
        out_grad,
        out_new,
        out_new.astype(low_type),
        out_rows_new,
        out_cols_new,
        conv_local,
        convw_new,
        convw_new.astype(low_type),
        conv_rows_new,
        conv_cols_new,
        vector_local[0],
        convb_new,
        convb_new.astype(low_type),
        bias_moment_new,
        select_local,
        select_new,
        select_new.astype(low_type),
        select_rows_new,
        select_cols_new,
        step_local,
        stepw_new,
        stepw_new.astype(low_type),
        step_rows_new,
        step_cols_new,
        vector_local[1],
        stepb_new,
        stepb_new.astype(low_type),
        step_moment_new,
        decay_local,
        decay_new,
        decay_new.astype(low_type),
        decay_rows_new,
        decay_cols_new,
        vector_local[2],
        skip_new,
        skip_new.astype(low_type),
        skip_moment_new,
    )


def solution(mesh):
    return jax.shard_map(
        on_device,
        mesh=mesh,
        in_specs=(
            P(("seq", "tp"), None),
            P("seq", None),
            P(),
            P(),
            P("seq", None, "tp"),
            P("seq", "tp"),
            P(None, "tp"),
            P("tp"),
            P(None, "tp"),
            P(None, "tp"),
            P("tp"),
            P(None, "tp"),
            P("tp"),
            P(),
            P("seq"),
            P(None, "tp"),
            P("seq"),
            P("tp"),
            P(),
            P("tp"),
            P("tp"),
            P(),
            P("tp"),
            P(),
            P("tp"),
            P("tp"),
            P(),
            P("tp"),
            P("tp"),
        ),
        out_specs=(
            P(("seq", "tp"), None),
            P(("seq", "tp"), None),
            P(),
            P(),
            P(),
            P(),
            P("seq", None, "tp"),
            P("seq", None, "tp"),
            P("seq", None, "tp"),
            P("seq"),
            P(None, "tp"),
            P("seq", "tp"),
            P("seq", "tp"),
            P("seq", "tp"),
            P("seq"),
            P("tp"),
            P(None, "tp"),
            P(None, "tp"),
            P(None, "tp"),
            P(),
            P("tp"),
            P("tp"),
            P("tp"),
            P("tp"),
            P("tp"),
            P(None, "tp"),
            P(None, "tp"),
            P(None, "tp"),
            P(),
            P("tp"),
            P(None, "tp"),
            P(None, "tp"),
            P(None, "tp"),
            P(),
            P("tp"),
            P("tp"),
            P("tp"),
            P("tp"),
            P("tp"),
            P(None, "tp"),
            P(None, "tp"),
            P(None, "tp"),
            P(),
            P("tp"),
            P("tp"),
            P("tp"),
            P("tp"),
            P("tp"),
        ),
        check_vma=False,
    )
```

profile of v0, /device:TPU:0, one launch (start us, length us, event | category | flops | bytes accessed | tf_op | source)
XLA Modules:
  0.0 2385.6 jit_solution(11890816632404038180)
XLA Ops:
  26.1 114.8 %all-gather.9.cloned.1.call-done = bf16[2048,2,2048]{2,0,1:T(8,128)(2,1)} async-done(((bf16[128,2,2048]{2,0,1:T(8,128)(2,1)}), bf16[2048,2,2048]{2,0,1:T(8,128)(2,1)}) %all-gather.9.cloned.1.call-update) | async-done | bytes 16777232 | tf_op jit(solution)/shard_map/all_gather | solution.py:172
  153.3 63.5 %all-gather.11.cloned.1.call-done = bf16[2048,2048]{1,0:T(8,128)(2,1)} async-done(((bf16[128,2048]{1,0:T(8,128)(2,1)}), bf16[2048,2048]{1,0:T(8,128)(2,1)}) %all-gather.11.cloned.1.call-update) | async-done | bytes 8388624 | tf_op jit(solution)/shard_map/all_gather | solution.py:173
  228.1 19.1 all-reduce.7.cloned.1.call-done
  255.8 48.5 %while.179 = (s32[]{:T(128)}, f32[16,2048]{1,0:T(8,128)}, f32[16,2048]{1,0:T(8,128)S(1)}, f32[128,2048]{1,0:T(8,128)S(1)}, f32[128,2048]{1,0:T(8,128)S(1)}, /*index=5*/f32[16,128]{1,0:T(8,128)}) while((s32[]{:T(128)}, f32[16,2048]{1,0:T(8,128)}, f32[16,2048]{1,0:T(8,128)S(1)}, f32[128,2048]{1,0:T(8,128)S(1)}, ...), condition=%wide.region_16.17_spmd.clone, body=%wide.region_14.16_spmd.sunk.clone | while | flops 1046530 | bytes 2147929 | solution.py:273
  305.3 18.9 while.178
  327.1 19.7 all-gather.17.cloned.1.call-done
  349.9 15.4 while.183
  365.4 24.2 %all-gather.15.cloned.1.call-done = f32[256,2048]{1,0:T(8,128)} async-done(((f32[16,2048]{1,0:T(8,128)}), f32[256,2048]{1,0:T(8,128)}) %all-gather.15.cloned.1.call-update) | async-done | bytes 2097168 | tf_op jit(solution)/shard_map/all_gather | solution.py:22
  389.6 16.4 while.182
  406.1 398.4 %while.181 = (s32[]{:T(128)}, f32[16,2048]{1,0:T(8,128)S(1)}, f32[4,32,2048]{2,1,0:T(8,128)S(1)}, f32[4,16,2048]{2,1,0:T(8,128)}, f32[4,32,16]{1,2,0:T(8,128)S(1...) while((s32[]{:T(128)}, f32[16,2048]{1,0:T(8,128)S(1)}, ...), condition=%wide.region_12.13_spmd.clone.clone, body=%wide.region_7.12_spmd.clone.sunk.clone | while | flops 39083104 | bytes 8798394 | solution.py:245
  409.0 94.2 %while.180 = (s32[]{:T(128)}, f32[16,32,2048]{2,1,0:T(8,128)}, f32[16,2048]{1,0:T(8,128)S(1)}, f32[16,32]{1,0:T(8,128)S(1)}, f32[32,32]{1,0:T(8,128)S(1)}, /*ind...) while((s32[]{:T(128)}, f32[16,32,2048]{2,1,0:T(8,128)}, ...), condition=%wide.region_10.10_spmd, body=%wide.region_8.9_spmd.sunk | while | flops 12919810 | bytes 2219041 | solution.py:242
  508.6 94.2 %while.180 = (s32[]{:T(128)}, f32[16,32,2048]{2,1,0:T(8,128)}, f32[16,2048]{1,0:T(8,128)S(1)}, f32[16,32]{1,0:T(8,128)S(1)}, f32[32,32]{1,0:T(8,128)S(1)}, /*ind...) while((s32[]{:T(128)}, f32[16,32,2048]{2,1,0:T(8,128)}, ...), condition=%wide.region_10.10_spmd, body=%wide.region_8.9_spmd.sunk | while | flops 12919810 | bytes 2219041 | solution.py:242
  608.2 94.2 %while.180 = (s32[]{:T(128)}, f32[16,32,2048]{2,1,0:T(8,128)}, f32[16,2048]{1,0:T(8,128)S(1)}, f32[16,32]{1,0:T(8,128)S(1)}, f32[32,32]{1,0:T(8,128)S(1)}, /*ind...) while((s32[]{:T(128)}, f32[16,32,2048]{2,1,0:T(8,128)}, ...), condition=%wide.region_10.10_spmd, body=%wide.region_8.9_spmd.sunk | while | flops 12919810 | bytes 2219041 | solution.py:242
  707.8 94.2 %while.180 = (s32[]{:T(128)}, f32[16,32,2048]{2,1,0:T(8,128)}, f32[16,2048]{1,0:T(8,128)S(1)}, f32[16,32]{1,0:T(8,128)S(1)}, f32[32,32]{1,0:T(8,128)S(1)}, /*ind...) while((s32[]{:T(128)}, f32[16,32,2048]{2,1,0:T(8,128)}, ...), condition=%wide.region_10.10_spmd, body=%wide.region_8.9_spmd.sunk | while | flops 12919810 | bytes 2219041 | solution.py:242
  807.4 602.1 %while.185 = (s32[]{:T(128)}, f32[16,2048]{1,0:T(8,128)S(1)}, f32[16,2048]{1,0:T(8,128)}, f32[4,32,2048]{2,1,0:T(8,128)}, f32[4,32,2048]{2,1,0:T(8,128)}, /*inde...) while((s32[]{:T(128)}, f32[16,2048]{1,0:T(8,128)S(1)}, ...), condition=%wide.region_29.30_spmd.clone.clone.clone, body=%wide.region_19.29_spmd.clone.clone.sunk.clone | while | flops 46087264 | bytes 21587936 | solution.py:316
  814.4 134.8 %while.184 = (s32[]{:T(128)}, f32[16,32,2048]{2,1,0:T(8,128)}, f32[16,32,2048]{2,1,0:T(8,128)}, f32[16,2048]{1,0:T(8,128)}, f32[16,32]{1,0:T(8,128)S(1)}, /*inde...) while((s32[]{:T(128)}, f32[16,32,2048]{2,1,0:T(8,128)}, ...), condition=%wide.region_26.26_spmd.clone, body=%wide.region_20.25_spmd.clone.sunk | while | flops 18875328 | bytes 7791081 | solution.py:308
  964.9 134.8 %while.184 = (s32[]{:T(128)}, f32[16,32,2048]{2,1,0:T(8,128)}, f32[16,32,2048]{2,1,0:T(8,128)}, f32[16,2048]{1,0:T(8,128)}, f32[16,32]{1,0:T(8,128)S(1)}, /*inde...) while((s32[]{:T(128)}, f32[16,32,2048]{2,1,0:T(8,128)}, ...), condition=%wide.region_26.26_spmd.clone, body=%wide.region_20.25_spmd.clone.sunk | while | flops 18875328 | bytes 7791081 | solution.py:308
  1115.4 134.8 %while.184 = (s32[]{:T(128)}, f32[16,32,2048]{2,1,0:T(8,128)}, f32[16,32,2048]{2,1,0:T(8,128)}, f32[16,2048]{1,0:T(8,128)}, f32[16,32]{1,0:T(8,128)S(1)}, /*inde...) while((s32[]{:T(128)}, f32[16,32,2048]{2,1,0:T(8,128)}, ...), condition=%wide.region_26.26_spmd.clone, body=%wide.region_20.25_spmd.clone.sunk | while | flops 18875328 | bytes 7791081 | solution.py:308
  1265.9 134.8 %while.184 = (s32[]{:T(128)}, f32[16,32,2048]{2,1,0:T(8,128)}, f32[16,32,2048]{2,1,0:T(8,128)}, f32[16,2048]{1,0:T(8,128)}, f32[16,32]{1,0:T(8,128)S(1)}, /*inde...) while((s32[]{:T(128)}, f32[16,32,2048]{2,1,0:T(8,128)}, ...), condition=%wide.region_26.26_spmd.clone, body=%wide.region_20.25_spmd.clone.sunk | while | flops 18875328 | bytes 7791081 | solution.py:308
  1490.6 149.4 %all-reduce.11.cloned.1.call-done = (f32[4,4096]{1,0:T(4,128)}, f32[160,4096]{1,0:T(8,128)}, f32[128,4096]{1,0:T(8,128)}, f32[16,4096]{1,0:T(8,128)}) async-done(((f32[4,4096]{1,0:T(4,128)}, f32[160,4096]{1,0:T(8,128)}, f32[128,4096]{1,0:T(8,128)}, f32[16,4096]{1,0:T(8,128)}), (f32[4,4096]{1,0:T(4,128)}, f32[160,4096]{1,0:T(8,128)}, f32[128,4096]{1,0:T(8,128)}, ...) | async-done | bytes 5046288 | tf_op jit(solution)/shard_map/psum | solution.py:419
  1656.3 165.8 %reduce-scatter.11.cloned.1.call-done = f32[128,2048]{0,1:T(8,128)} async-done(((f32[2048,2048]{0,1:T(8,128)}), f32[128,2048]{0,1:T(8,128)}) %reduce-scatter.11.cloned.1.call-update) | async-done | bytes 1048592 | tf_op jit(solution)/shard_map/reduce_scatter | solution.py:383
  1824.5 334.3 %reduce-scatter.9.cloned.1.call-done = f32[128,2,2048]{2,0,1:T(8,128)} async-done(((f32[2048,2,2048]{2,0,1:T(8,128)}), f32[128,2,2048]{2,0,1:T(8,128)}) %reduce-scatter.9.cloned.1.call-update) | async-done | bytes 2097168 | tf_op jit(solution)/shard_map/reduce_scatter | solution.py:382
  2170.6 120.3 %all-reduce.9.cloned.1.call-done = (f32[2048]{0:T(1024)}, f32[2,4096]{1,0:T(2,128)}, f32[2048]{0:T(1024)}, f32[4096]{0:T(1024)}, f32[3,4096]{1,0:T(4,128)}) async-done(((f32[2048]{0:T(1024)}, f32[2,4096]{1,0:T(2,128)}, f32[2048]{0:T(1024)}, f32[4096]{0:T(1024)}, f32[3,4096]{1,0:T(4,128)}), (f32[2048]{0:T(1024)}, f32[2,4096]{1,0:T(2,128)}, f32[2048]{0:T(1024)}, f32[4096]{0:T(1024)}, ...) | async-done | bytes 114704 | tf_op jit(solution)/shard_map/psum | solution.py:419
  2307.4 39.6 %all-reduce = (f32[2048]{0:T(1024)}, f32[9]{0:T(128)S(1)}) all-reduce(f32[2048]{0:T(1024)S(1)} %get-tuple-element.1235, f32[9]{0:T(128)} %stack.87), channel_id=1, replica_groups=mesh['seq'=16,'tp'=2] {'seq','tp'}, use_global_device_ids=true, to_apply=%region_34.35 | all-reduce | flops 2057 | bytes 16456 | tf_op jit(solution)/shard_map/psum | solution.py:419
  (2382 shorter events, 1291.0 us)
Async XLA Ops:
  7.2 133.6 %all-gather.9.cloned.1.call-start = ((), (), s32[]{:S(2)}) async-start(), calls=%async_computation.4 | async-start | bytes 17825792 | tf_op jit(solution)/shard_map/all_gather | solution.py:172
  11.1 205.7 %all-gather.11.cloned.1.call-start = ((), (), s32[]{:S(2)}) async-start(), calls=%async_computation.6 | async-start | bytes 8912896 | tf_op jit(solution)/shard_map/all_gather | solution.py:173
  12.0 235.2 %all-reduce.7.cloned.1.call-start = ((), (), s32[]{:S(2)}) async-start(), calls=%async_computation.5 | async-start | bytes 163840 | tf_op jit(solution)/shard_map/psum | solution.py:197
  12.9 203.9 %copy-start.117 = (f32[128]{0:T(128)}, f32[128]{0:T(128)S(1)}, u32[]{:S(2)}) copy-start(f32[128]{0:T(128)S(1)} %get-tuple-element.1511) | copy-start | bytes 1540
  149.0 3.1 collective-permute-start
  227.9 97.4 %all-gather.13.cloned.1.call-start = ((), (), s32[]{:S(2)}) async-start(), calls=%async_computation.11 | async-start | bytes 2228224 | tf_op jit(solution)/shard_map/all_gather | solution.py:22
  253.8 93.0 %all-gather.17.cloned.1.call-start = ((), (), s32[]{:S(2)}) async-start(), calls=%async_computation.13 | async-start | bytes 2228224 | tf_op jit(solution)/shard_map/all_gather | solution.py:22
  305.2 84.4 %all-gather.15.cloned.1.call-start = ((), (), s32[]{:S(2)}) async-start(), calls=%async_computation.12 | async-start | bytes 2228224 | tf_op jit(solution)/shard_map/all_gather | solution.py:22
  324.8 1162.0 %reduce-scatter.7.cloned.1.call-start = ((), (), s32[]{:S(2)}) async-start(), calls=%async_computation.8 | async-start | bytes 1572864 | tf_op jit(solution)/shard_map/reduce_scatter | solution.py:374
  807.4 603.0 %copy-start.13 = (bf16[128,2048]{1,0:T(8,128)(2,1)S(1)}, bf16[128,2048]{1,0:T(8,128)(2,1)}, u32[]{:S(2)}) copy-start(bf16[128,2048]{1,0:T(8,128)(2,1)} %copy-done.12) | copy-start | bytes 1572868
  807.4 603.0 %copy-start.68 = (f32[2048]{0:T(1024)S(1)}, f32[2048]{0:T(1024)}, u32[]{:S(2)}) copy-start(f32[2048]{0:T(1024)} %param.57) | copy-start | bytes 24580
  1430.7 3.1 collective-permute-start.1
  1447.1 41.1 %reduce-scatter.5.cloned.1.call-start = ((), (), s32[]{:S(2)}) async-start(), calls=%async_computation.7 | async-start | bytes 786432 | tf_op jit(solution)/shard_map/reduce_scatter | solution.py:255
  1454.3 185.7 %all-reduce.11.cloned.1.call-start = ((), (), s32[]{:S(2)}) async-start(), calls=%async_computation.15 | async-start | bytes 10092544 | tf_op jit(solution)/shard_map/psum | solution.py:419
  1459.4 362.7 %reduce-scatter.11.cloned.1.call-start = ((), (), s32[]{:S(2)}) async-start(), calls=%async_computation.10 | async-start | bytes 17825792 | tf_op jit(solution)/shard_map/reduce_scatter | solution.py:383
  1469.5 689.3 %reduce-scatter.9.cloned.1.call-start = ((), (), s32[]{:S(2)}) async-start(), calls=%async_computation.9 | async-start | bytes 35651584 | tf_op jit(solution)/shard_map/reduce_scatter | solution.py:382
  1484.3 806.6 %all-reduce.9.cloned.1.call-start = ((), (), s32[]{:S(2)}) async-start(), calls=%async_computation.14 | async-start | bytes 262144 | tf_op jit(solution)/shard_map/psum | solution.py:419
  1650.9 722.8 %copy-start.40 = (f32[16,2048]{1,0:T(8,128)}, f32[16,2048]{1,0:T(8,128)S(1)}, u32[]{:S(2)}) copy-start(f32[16,2048]{1,0:T(8,128)S(1)} %get-tuple-element.1438) | copy-start | bytes 393220
  1653.0 713.7 %copy-start.58 = (f32[2048]{0:T(1024)}, f32[2048]{0:T(1024)S(1)}, u32[]{:S(2)}) copy-start(f32[2048]{0:T(1024)S(1)} %get-tuple-element.1532) | copy-start | bytes 24580
  1653.1 717.6 %copy-start.59 = (f32[2048]{0:T(1024)}, f32[2048]{0:T(1024)S(1)}, u32[]{:S(2)}) copy-start(f32[2048]{0:T(1024)S(1)} %get-tuple-element.1531) | copy-start | bytes 24580
  1653.1 720.6 %copy-start.61 = (f32[2048]{0:T(1024)}, f32[2048]{0:T(1024)S(1)}, u32[]{:S(2)}) copy-start(f32[2048]{0:T(1024)S(1)} %get-tuple-element.1530) | copy-start | bytes 24580
  1655.1 505.8 %copy-start.120 = (f32[128]{0:T(128)S(1)}, f32[128]{0:T(128)}, u32[]{:S(2)}) copy-start(f32[128]{0:T(128)} %param.59) | copy-start | bytes 1540
  1822.1 344.3 %copy-start.1 = (f32[128,2048]{0,1:T(8,128)S(1)}, f32[128,2048]{0,1:T(8,128)}, u32[]{:S(2)}) copy-start(f32[128,2048]{0,1:T(8,128)} %reduce-scatter.11.cloned.1.call-done) | copy-start | bytes 3145732
  1824.5 337.3 %copy-start.65 = (f32[4096]{0:T(1024)}, f32[4096]{0:T(1024)S(1)}, u32[]{:S(2)}) copy-start(f32[4096]{0:T(1024)S(1)} %add_dynamic-update-slice_fusion.1) | copy-start | bytes 49156
  (120 other events, 3572.5 us)
Sparse Core Ops, SparseCore 0:
  11.2 129.5 all-gather.8
  143.6 73.2 all-gather.10
  228.1 19.1 all-reduce.6
  253.9 41.3 all-gather.12
  305.3 41.4 all-gather.16
  349.4 40.1 all-gather.14
  1447.3 19.7 reduce-scatter.6
  1470.0 14.5 reduce-scatter.4
  1492.5 147.4 all-reduce.10
  1644.5 177.5 reduce-scatter.10
  1826.9 331.8 reduce-scatter.8
  2167.2 123.6 all-reduce.8
where the time goes:
time: 2410 us; the launch traced here: 2390 us
  waiting for transfers between devices  1010 us (42%)
  other arithmetic  825 us (34%)
  local copies, waits for them, and re-layouts  357 us (15%)
  matrix products  82.3 us (3%)
  blocking collectives  58.6 us (2%)
  between operations  32.5 us (1%)
    reduce_sum x128, other arithmetic, per_state(): rows_b = jnp.sum(weights_b * (drive_b * enter_col[:, None])[None], axis=1)  473 us
    reduce_scatter x1, waiting for transfers between devices, on_device(): lax.psum_scatter(d_in_w, 'seq', scatter_dimension=0, tiled=True)  334 us
    psum x2, waiting for transfers between devices, on_device(): lax.psum((widen_last(conv_w_grad, tp_index, channels), widen_last(vector_...  270 us
    reduce_scatter x1, waiting for transfers between devices, on_device(): lax.psum_scatter(d_out_w, 'seq', scatter_dimension=0, tiled=True)  166 us
    dynamic_update_slice x224, local copies, waits for them, and re-layouts, on_device(): local_state = lax.map(state_term, (decay_rate, state_in.T))  149 us
    dynamic_update_slice x128, other arithmetic, block_forward(): lax.map(per_state, (decay_rate, enter_b.T, leave_b.T, state_now))  117 us
    all_gather x1, waiting for transfers between devices, on_device(): lax.all_gather(in_weight.astype(jnp.bfloat16), 'seq', axis=0, tiled=True)  115 us
    all_gather x1, waiting for transfers between devices, on_device(): lax.all_gather(out_weight.astype(jnp.bfloat16), 'seq', axis=0, tiled=True)  63.5 us
  transfers between devices with their start and end apart: 14, of which 11 were waited for; matrix products, arithmetic and copies ran while one was open for 7% of the time, Pallas kernels for 0%

commit v1 on v0

--- a/solution.py
+++ b/solution.py
@@ -1,6 +1,10 @@
+import functools
+
 import jax
 import jax.numpy as jnp
 from jax import lax
+from jax.experimental import pallas as pl
+from jax.experimental.pallas import tpu as pltpu
 from jax.sharding import PartitionSpec as P
 
 EPS_NORM = 1e-05
@@ -8,7 +12,10 @@
 DECAY = 0.5
 CLIP = 0.5
 RATES = (0.45, 0.02, 0.03, 0.1, 0.05, 0.016, 0.09, 1.8, 0.3, 0.45)
-highest = lax.Precision.HIGHEST
+LOG2E = 1.4426950408889634
+RESET = 1e9
+TILE = 512
+VMEM_LIMIT = 48 * 1024 * 1024
 
 
 def passed_along(value, axis, steps):
@@ -17,30 +24,9 @@
     return lax.ppermute(value, axis, [(source, source + steps) for source in range(initial, last)])
 
 
-def prefix(value, axis, join, neutral, backward):
-    count, mine = (lax.axis_size(axis), lax.axis_index(axis))
-    pieces = jax.tree.map(lambda part: lax.all_gather(part, axis), value)
-    if backward:
-        pieces = jax.tree.map(lambda part: part[::-1], pieces)
-        mine = count - 1 - mine
-    subtotal = jax.tree.map(
-        lambda part, zero: jnp.full_like(part, 0) + jnp.asarray(zero, part.dtype), value, neutral
-    )
-
-    def step(position, subtotal):
-        longer = join(subtotal, jax.tree.map(lambda part: part[position], pieces))
-        return jax.tree.map(lambda new, old: jnp.where(position < mine, new, old), longer, subtotal)
-
-    return lax.fori_loop(0, count - 1, step, subtotal)
-
-
 def silu_slope(values):
     sigmoid_v = jax.nn.sigmoid(values)
     return sigmoid_v * (1.0 + values * (1.0 - sigmoid_v))
-
-
-def compose(earlier, later):
-    return (later[0] * earlier[0], later[0] * earlier[1] + later[1])
 
 
 def widen_last(piece_in, index_of, total_len):
@@ -79,19 +65,216 @@
     return weight - step_rate * update / jnp.maximum(1.0, root_mean / CLIP)
 
 
-def block_masks(lower_blk, step_b, keep_b):
-    cum_b = jnp.dot(lower_blk, step_b, precision=highest)
-    resets_b = jnp.dot(lower_blk, 1.0 - keep_b, precision=highest)
-    same_b = (resets_b[:, None] == resets_b[None, :]).astype(jnp.float32) * lower_blk
-    head_b = (resets_b == 0.0).astype(jnp.float32)
-    tail_b = (resets_b == resets_b[-1]).astype(jnp.float32)
-    return (cum_b, same_b, head_b, tail_b)
-
-
-def decay_matrix(rate_row, cum_b, same_b):
-    live = same_b[:, :, None] > 0.0
-    spread = jnp.where(live, cum_b[:, None, :] - cum_b[None, :, :], 0.0)
-    return jnp.where(live, jnp.exp(rate_row[None, None, :] * spread), 0.0)
+def wide(tile, width):
+    return jnp.concatenate([tile] * (width // tile.shape[1]), axis=1)
+
+
+def fold_lanes(value):
+    pieces = [value[:, at : at + 128] for at in range(0, value.shape[1], 128)]
+    while len(pieces) > 1:
+        pieces = [first + second for first, second in zip(pieces[::2], pieces[1::2])]
+    return pieces[0]
+
+
+def state_kernel(backward, step_ref, value_ref, lane_ref, rate_ref, out_ref):
+    rows, width = step_ref.shape
+    states = rate_ref.shape[0]
+    rate = rate_ref[...] * LOG2E
+
+    def block(index, state):
+        base = pl.multiple_of((rows // 8 - 1 - index if backward else index) * 8, 8)
+        for offset in range(8):
+            at = base + (7 - offset if backward else offset)
+            keep = jnp.exp2(rate * step_ref[pl.ds(at, 1), :])
+            term = wide(lane_ref[at], width) * value_ref[pl.ds(at, 1), :]
+            state = keep * (state + term) if backward else keep * state + term
+        return state
+
+    out_ref[0:states, :] = lax.fori_loop(0, rows // 8, block, jnp.zeros((states, width), jnp.float32))
+    total = jnp.sum(step_ref[...], axis=0, keepdims=True)
+    out_ref[states:, :] = jnp.broadcast_to(total, (out_ref.shape[0] - states, width))
+
+
+def piece_state(step, value, lane, rate, backward):
+    rows, width = step.shape
+    states = rate.shape[0]
+    tile = TILE
+    return pl.pallas_call(
+        functools.partial(state_kernel, backward),
+        grid=(width // tile,),
+        in_specs=[
+            pl.BlockSpec((rows, tile), lambda i: (0, i)),
+            pl.BlockSpec((rows, tile), lambda i: (0, i)),
+            pl.BlockSpec((rows, states, 128), lambda i: (0, 0, 0)),
+            pl.BlockSpec((states, tile), lambda i: (0, i)),
+        ],
+        out_specs=pl.BlockSpec((states + 8, tile), lambda i: (0, i)),
+        out_shape=jax.ShapeDtypeStruct((states + 8, width), jnp.float32),
+        compiler_params=pltpu.CompilerParams(vmem_limit_bytes=VMEM_LIMIT),
+    )(step, value, lane, rate)
+
+
+def entering(pieces_ref, rate, first, count, stride):
+    states = rate.shape[0]
+
+    def join(index, state):
+        at = first + index * stride
+        piece = pieces_ref[at]
+        return jnp.exp2(rate * piece[states : states + 1]) * state + piece[:states]
+
+    return lax.fori_loop(0, count, join, jnp.zeros(rate.shape, jnp.float32))
+
+
+def forward_kernel(
+    place_ref, step_ref, drive_ref, enter_ref, leave_ref, rate_ref, pieces_ref, out_ref, start_ref
+):
+    rows, width = step_ref.shape
+    rate = rate_ref[...] * LOG2E
+    start = entering(pieces_ref, rate, 0, place_ref[0], 1)
+    start_ref[...] = start
+
+    def block(index, state):
+        base = pl.multiple_of(index * 8, 8)
+        for offset in range(8):
+            at = base + offset
+            keep = jnp.exp2(rate * step_ref[pl.ds(at, 1), :])
+            state = keep * state + wide(enter_ref[at], width) * drive_ref[pl.ds(at, 1), :]
+            out_ref[pl.ds(at, 1), :] = jnp.sum(
+                wide(leave_ref[at], width) * state, axis=0, keepdims=True
+            )
+        return state
+
+    lax.fori_loop(0, rows // 8, block, start)
+
+
+def scan_forward(place, step, drive, enter, leave, rate, pieces):
+    rows, width = step.shape
+    states = rate.shape[0]
+    tile = TILE
+    return pl.pallas_call(
+        forward_kernel,
+        grid=(width // tile,),
+        in_specs=[
+            pl.BlockSpec(memory_space=pltpu.SMEM),
+            pl.BlockSpec((rows, tile), lambda i: (0, i)),
+            pl.BlockSpec((rows, tile), lambda i: (0, i)),
+            pl.BlockSpec((rows, states, 128), lambda i: (0, 0, 0)),
+            pl.BlockSpec((rows, states, 128), lambda i: (0, 0, 0)),
+            pl.BlockSpec((states, tile), lambda i: (0, i)),
+            pl.BlockSpec((pieces.shape[0], states + 8, tile), lambda i: (0, 0, i)),
+        ],
+        out_specs=[
+            pl.BlockSpec((rows, tile), lambda i: (0, i)),
+            pl.BlockSpec((states, tile), lambda i: (0, i)),
+        ],
+        out_shape=[
+            jax.ShapeDtypeStruct((rows, width), jnp.float32),
+            jax.ShapeDtypeStruct((states, width), jnp.float32),
+        ],
+        compiler_params=pltpu.CompilerParams(vmem_limit_bytes=VMEM_LIMIT),
+    )(place, step, drive, enter, leave, rate, pieces)
+
+
+def backward_kernel(
+    place_ref,
+    step_ref,
+    drive_ref,
+    grad_ref,
+    enter_ref,
+    leave_ref,
+    rate_ref,
+    start_ref,
+    pieces_ref,
+    drive_grad_ref,
+    step_grad_ref,
+    decay_ref,
+    enter_grad_ref,
+    leave_grad_ref,
+    kept_ref,
+    state_ref,
+):
+    rows, width = step_ref.shape
+    rate_own = rate_ref[...]
+    rate = rate_own * LOG2E
+    count = pieces_ref.shape[0]
+
+    @pl.when(pl.program_id(0) == 0)
+    def _():
+        enter_grad_ref[...] = jnp.zeros_like(enter_grad_ref)
+        leave_grad_ref[...] = jnp.zeros_like(leave_grad_ref)
+
+    def again(index, state):
+        base = pl.multiple_of(index * 8, 8)
+        for offset in range(8):
+            at = base + offset
+            keep = jnp.exp2(rate * step_ref[pl.ds(at, 1), :])
+            kept_ref[at] = keep
+            state = keep * state + wide(enter_ref[at], width) * drive_ref[pl.ds(at, 1), :]
+            state_ref[at + 1] = state
+        return state
+
+    start = start_ref[...]
+    state_ref[0] = start
+    lax.fori_loop(0, rows // 8, again, start)
+    follow = entering(pieces_ref, rate, count - 1, count - 1 - place_ref[0], -1)
+
+    def block(index, carry):
+        follow, decay = carry
+        base = pl.multiple_of((rows // 8 - 1 - index) * 8, 8)
+        for offset in range(7, -1, -1):
+            at = base + offset
+            grad = grad_ref[pl.ds(at, 1), :]
+            adjoint = wide(leave_ref[at], width) * grad + follow
+            drive_grad_ref[pl.ds(at, 1), :] = jnp.sum(
+                adjoint * wide(enter_ref[at], width), axis=0, keepdims=True
+            )
+            enter_grad_ref[at] += fold_lanes(adjoint * drive_ref[pl.ds(at, 1), :])
+            leave_grad_ref[at] += fold_lanes(state_ref[at + 1] * grad)
+            follow = kept_ref[at] * adjoint
+            part = follow * state_ref[at]
+            step_grad_ref[pl.ds(at, 1), :] = jnp.sum(part * rate_own, axis=0, keepdims=True)
+            decay = decay + part * step_ref[pl.ds(at, 1), :]
+        return follow, decay
+
+    _, decay = lax.fori_loop(0, rows // 8, block, (follow, jnp.zeros_like(follow)))
+    decay_ref[...] = decay * rate_own
+
+
+def scan_backward(place, step, drive, grad, enter, leave, rate, start, pieces):
+    rows, width = step.shape
+    states = rate.shape[0]
+    tile = TILE
+    by_tile = pl.BlockSpec((rows, tile), lambda i: (0, i))
+    by_state = pl.BlockSpec((states, tile), lambda i: (0, i))
+    whole = pl.BlockSpec((rows, states, 128), lambda i: (0, 0, 0))
+    return pl.pallas_call(
+        backward_kernel,
+        grid=(width // tile,),
+        in_specs=[
+            pl.BlockSpec(memory_space=pltpu.SMEM),
+            by_tile,
+            by_tile,
+            by_tile,
+            whole,
+            whole,
+            by_state,
+            by_state,
+            pl.BlockSpec((pieces.shape[0], states + 8, tile), lambda i: (0, 0, i)),
+        ],
+        out_specs=[by_tile, by_tile, by_state, whole, whole],
+        out_shape=[
+            jax.ShapeDtypeStruct((rows, width), jnp.float32),
+            jax.ShapeDtypeStruct((rows, width), jnp.float32),
+            jax.ShapeDtypeStruct((states, width), jnp.float32),
+            jax.ShapeDtypeStruct((rows, states, 128), jnp.float32),
+            jax.ShapeDtypeStruct((rows, states, 128), jnp.float32),
+        ],
+        scratch_shapes=[
+            pltpu.VMEM((rows, states, tile), jnp.float32),
+            pltpu.VMEM((rows + 1, states, tile), jnp.float32),
+        ],
+        compiler_params=pltpu.CompilerParams(vmem_limit_bytes=VMEM_LIMIT),
+    )(place, step, drive, grad, enter, leave, rate, start, pieces)
 
 
 def on_device(
@@ -138,8 +321,6 @@
     states = decay_log.shape[0]
     step_rank = step_weight.shape[0]
     row_share = in_weight.shape[0]
-    block_len = min(row_count, max(32, row_count // 16))
-    blocks = row_count // block_len
     id_padded = jnp.concatenate(
         [
             jnp.full((conv_taps - 1,), -1, jnp.int32),
@@ -152,15 +333,6 @@
     )
     local_ids = window[conv_taps - 1 : conv_taps - 1 + row_count]
     keep_mask = (local_ids == window[conv_taps - 2 : conv_taps - 2 + row_count]).astype(jnp.float32)
-    lower_tri = (
-        lax.broadcasted_iota(jnp.int32, (row_count, row_count), 0)
-        >= lax.broadcasted_iota(jnp.int32, (row_count, row_count), 1)
-    ).astype(jnp.float32)
-    lower_blk = lower_tri[:block_len, :block_len]
-    resets = jnp.dot(lower_tri, 1.0 - keep_mask, precision=highest)
-    keep_pre = (resets == 0.0).astype(jnp.float32)
-    keep_suf = (resets == resets[-1]).astype(jnp.float32)
-    keep_all = (resets[-1] == 0.0).astype(jnp.float32)
     residual = block_in.astype(jnp.float32)
     mean_sq = jnp.mean(residual * residual, axis=1, keepdims=True)
     inv_rms = lax.rsqrt(mean_sq + EPS_NORM)
@@ -205,49 +377,16 @@
     step_size = jax.nn.softplus(step_pre)
     decay_rate = -jnp.exp(decay_log)
     drive = step_size * conv_value
-    cum_pre = jnp.dot(lower_tri, step_size, precision=highest)
-    total_step = cum_pre[-1]
-    cum_suf = total_step[None, :] - cum_pre
-    masked_drive = drive * keep_suf[:, None]
-
-    def state_term(pair_in):
-        rate_row, column = pair_in
-        return jnp.sum(
-            jnp.exp(rate_row[None, :] * cum_suf) * masked_drive * column[:, None], axis=0
-        )
-
-    local_state = lax.map(state_term, (decay_rate, state_in.T))
-    product = jnp.exp(decay_rate * total_step[None, :]) * keep_all
-    identity = (jnp.ones_like(product), jnp.zeros_like(product))
-    _, incoming = prefix((product, local_state), "seq", compose, identity, False)
-    step_blocks = step_size.reshape(blocks, block_len, inner_dim)
-    drive_blocks = drive.reshape(blocks, block_len, inner_dim)
-    enter_blocks = state_in.reshape(blocks, block_len, states)
-    leave_blocks = state_out.reshape(blocks, block_len, states)
-    keep_blocks = keep_mask.reshape(blocks, block_len)
-
-    def block_forward(state_now, inputs):
-        step_b, drive_b, enter_b, keep_b, leave_b = inputs
-        cum_b, same_b, head_b, _ = block_masks(lower_blk, step_b, keep_b)
-
-        def per_state(args):
-            rate_row, enter_col, leave_col, start_row = args
-            weights_b = decay_matrix(rate_row, cum_b, same_b)
-            rows_b = jnp.sum(weights_b * (drive_b * enter_col[:, None])[None], axis=1)
-            rows_b = (
-                rows_b + jnp.exp(rate_row[None, :] * cum_b) * head_b[:, None] * start_row[None, :]
-            )
-            return (leave_col[:, None] * rows_b, rows_b[-1])
-
-        terms, ends = lax.map(per_state, (decay_rate, enter_b.T, leave_b.T, state_now))
-        return (ends, (jnp.sum(terms, axis=0), state_now))
-
-    _, (scanned, block_starts) = lax.scan(
-        block_forward,
-        incoming,
-        (step_blocks, drive_blocks, enter_blocks, keep_blocks, leave_blocks),
-    )
-    scanned = scanned.reshape(row_count, inner_dim)
+    place = seq_index[None]
+    held_step = jnp.where(keep_mask[:, None] > 0.0, step_size, RESET)
+    enter = jnp.broadcast_to(state_in[:, :, None], (row_count, states, 128))
+    leave = jnp.broadcast_to(state_out[:, :, None], (row_count, states, 128))
+    state_pieces = lax.all_gather(
+        piece_state(held_step, drive, enter, decay_rate, False), "seq"
+    )
+    scanned, start = scan_forward(
+        place, held_step, drive, enter, leave, decay_rate, state_pieces
+    )
     mixed = scanned + skip_gain[None, :] * conv_value
     gate_act = jax.nn.silu(gate_pre)
     gated = (mixed * gate_act).astype(jnp.bfloat16)
@@ -264,78 +403,21 @@
     d_mixed = d_gated * gate_act
     d_gate = (d_gated * mixed * silu_slope(gate_pre)).astype(jnp.bfloat16)
     skip_grad = jnp.sum(d_mixed * conv_value, axis=0)
-    masked_grad = d_mixed * keep_pre[:, None]
-
-    def adjoint_term(pair_in):
-        rate_row, column = pair_in
-        return jnp.sum(jnp.exp(rate_row[None, :] * cum_pre) * masked_grad * column[:, None], axis=0)
-
-    local_adjoint = lax.map(adjoint_term, (decay_rate, state_out.T))
-    _, later_adjoint = prefix((product, local_adjoint), "seq", compose, identity, True)
-
-    def block_backward(carry_in, inputs):
-        following, decay_acc = carry_in
-        step_b, drive_b, enter_b, keep_b, leave_b, grad_b, block_start = inputs
-        cum_b, same_b, head_b, tail_b = block_masks(lower_blk, step_b, keep_b)
-
-        def per_state(args):
-            rate_row, enter_col, leave_col, start_row, follow_row = args
-            weights_b = decay_matrix(rate_row, cum_b, same_b)
-            rows_b = jnp.sum(weights_b * (drive_b * enter_col[:, None])[None], axis=1)
-            rows_b = (
-                rows_b + jnp.exp(rate_row[None, :] * cum_b) * head_b[:, None] * start_row[None, :]
-            )
-            previous = jnp.concatenate([start_row[None], rows_b[:-1]], axis=0)
-            factor_b = jnp.exp(rate_row[None, :] * step_b) * keep_b[:, None]
-            source = grad_b * leave_col[:, None]
-            adjoint = jnp.sum(weights_b * source[:, None, :], axis=0)
-            adjoint = (
-                adjoint
-                + jnp.exp(rate_row[None, :] * (cum_b[-1][None, :] - cum_b))
-                * tail_b[:, None]
-                * follow_row[None, :]
-            )
-            decay_part = adjoint * previous * factor_b
-            return (
-                adjoint * enter_col[:, None],
-                decay_part * rate_row[None, :],
-                jnp.sum(decay_part * step_b, axis=0),
-                jnp.sum(adjoint * drive_b, axis=1),
-                jnp.sum(rows_b * grad_b, axis=1),
-                factor_b[0] * adjoint[0],
-            )
-
-        drive_parts, step_parts, decay_parts, enter_cols, leave_cols, follow_out = lax.map(
-            per_state, (decay_rate, enter_b.T, leave_b.T, block_start, following)
-        )
-        return (
-            (follow_out, decay_acc + decay_parts),
-            (jnp.sum(drive_parts, axis=0), jnp.sum(step_parts, axis=0), enter_cols.T, leave_cols.T),
-        )
-
-    (_, decay_acc), (drive_grad, step_grad, enter_grad, leave_grad) = lax.scan(
-        block_backward,
-        (later_adjoint, jnp.zeros_like(decay_rate)),
-        (
-            step_blocks,
-            drive_blocks,
-            enter_blocks,
-            keep_blocks,
-            leave_blocks,
-            d_mixed.reshape(blocks, block_len, inner_dim),
-            block_starts,
-        ),
-        reverse=True,
-    )
-    drive_grad = drive_grad.reshape(row_count, inner_dim)
-    d_step = drive_grad * conv_value + step_grad.reshape(row_count, inner_dim)
-    decay_grad = decay_acc * decay_rate
+    adjoint_pieces = lax.all_gather(
+        piece_state(held_step, d_mixed, leave, decay_rate, True), "seq"
+    )
+    drive_grad, step_grad, decay_grad, enter_grad, leave_grad = scan_backward(
+        place, held_step, drive, d_mixed, enter, leave, decay_rate, start, adjoint_pieces
+    )
+    enter_grad = jnp.sum(enter_grad, axis=2)
+    leave_grad = jnp.sum(leave_grad, axis=2)
+    d_step = drive_grad * conv_value + step_grad
     d_step_pre = (d_step * jax.nn.sigmoid(step_pre)).astype(jnp.bfloat16)
     step_bias_grad = jnp.sum(d_step_pre.astype(jnp.float32), axis=0)
     step_w_grad = jnp.einsum("tr,te->re", step_in, d_step_pre, preferred_element_type=jnp.float32)
     d_step_in = jnp.einsum("te,re->tr", d_step_pre, step_low, preferred_element_type=jnp.float32)
     select_grads = jnp.concatenate(
-        [d_step_in, enter_grad.reshape(row_count, states), leave_grad.reshape(row_count, states)],
+        [d_step_in, enter_grad, leave_grad],
         axis=1,
     )
     d_select = lax.psum(select_grads, "tp").astype(jnp.bfloat16)

time: 2410 us -> 1350 us (0.56)
  other arithmetic: 825 us -> 51.2 us
  local copies, waits for them, and re-layouts: 357 us -> 41.3 us
  waiting for transfers between devices: 1010 us -> 1050 us
  Pallas kernels: 0 us -> 35 us
    reduce_sum x300 -> x2, other arithmetic: 554 us -> 0.68 us  [the longest x1 0.34 us: on_device(): enter_grad = jnp.sum(enter_grad, axis=2)]
    dynamic_update_slice x372 -> x1, local copies, waits for them, and re-layouts: 165 us -> 0.02 us  [widen_last(): lax.dynamic_update_slice_in_dim(zero_block, piece_in, index_of * piece_in...]
    dynamic_update_slice x128 -> x0, other arithmetic: 117 us -> none  [block_forward(): lax.map(per_state, (decay_rate, enter_b.T, leave_b.T, state_now))]
    dynamic_slice x352 -> x0, local copies, waits for them, and re-layouts: 59.1 us -> none  [the longest x224 57.8 us: on_device(): local_state = lax.map(state_term, (decay_rate, state_in.T))]
    add x68 -> x0, other arithmetic: 49.8 us -> none  [the longest x64 43.3 us: per_state(): rows_b + jnp.exp(rate_row[None, :] * cum_b) * head_b[:, None] * start_row...]
    slice x198 -> x3, local copies, waits for them, and re-layouts: 43 us -> 0.92 us  [the longest x2 0.82 us: on_device(): state_out = select_out[:, step_rank + states:]]
    pallas_call x0 -> x4, Pallas kernels: none -> 35 us  [the longest x1 18.7 us: scan_backward(): pl.pallas_call(backward_kernel, grid=(width // tile,), in_specs=[pl.Block...]
    select_n x30 -> x0, other arithmetic: 31.2 us -> none  [step(): jnp.where(position < mine, new, old)]
  transfers between devices with their start and end apart: 14 -> 13, of which waited for: 11 -> 11; matrix products, arithmetic and copies ran while one was open for 7% -> 5% of each run, Pallas kernels for 0% -> 1%
where the time goes in v1:
time: 1350 us
  waiting for transfers between devices  1050 us (78%)
  matrix products  71.4 us (5%)
  blocking collectives  59.9 us (4%)
  other arithmetic  51.2 us (4%)
  local copies, waits for them, and re-layouts  41.3 us (3%)
  Pallas kernels  35 us (3%)
  between operations  31.4 us (2%)
    reduce_scatter x1, waiting for transfers between devices, on_device(): lax.psum_scatter(d_in_w, 'seq', scatter_dimension=0, tiled=True)  335 us
    psum x2, waiting for transfers between devices, on_device(): lax.psum((widen_last(conv_w_grad, tp_index, channels), widen_last(vector_...  271 us
    reduce_scatter x1, waiting for transfers between devices, on_device(): lax.psum_scatter(d_out_w, 'seq', scatter_dimension=0, tiled=True)  167 us
    all_gather x1, waiting for transfers between devices, on_device(): lax.all_gather(in_weight.astype(jnp.bfloat16), 'seq', axis=0, tiled=True)  118 us
    all_gather x1, waiting for transfers between devices, on_device(): lax.all_gather(out_weight.astype(jnp.bfloat16), 'seq', axis=0, tiled=True)  63.5 us
    psum x1, blocking collectives, on_device(): lax.psum((widen_last(conv_w_grad, tp_index, channels), widen_last(vector_...  39.6 us
    all_gather x1, waiting for transfers between devices, on_device(): lax.all_gather(piece_state(held_step, drive, enter, decay_rate, False), '...  38.4 us
    all_gather x1, waiting for transfers between devices, on_device(): lax.all_gather(piece_state(held_step, d_mixed, leave, decay_rate, True),...  36.6 us
  transfers between devices with their start and end apart: 13, of which 11 were waited for; matrix products, arithmetic and copies ran while one was open for 5% of the time, Pallas kernels for 1%

profile of v1, /device:TPU:0, one launch (start us, length us, event | category | flops | bytes accessed | tf_op | source)
XLA Modules:
  0.0 1345.0 jit_solution(4444252016562752911)
XLA Ops:
  12.6 9.9 all_gather.23
  23.3 117.5 %all-gather.7.cloned.1.call-done = bf16[2048,2,2048]{2,0,1:T(8,128)(2,1)} async-done(((bf16[128,2,2048]{2,0,1:T(8,128)(2,1)}), bf16[2048,2,2048]{2,0,1:T(8,128)(2,1)}) %all-gather.7.cloned.1.call-update) | async-done | bytes 16777232 | tf_op jit(solution)/shard_map/all_gather | solution.py:344
  140.8 8.1 fusion.68
  153.3 63.5 %all-gather.9.cloned.1.call-done = bf16[2048,2048]{1,0:T(8,128)(2,1)} async-done(((bf16[128,2048]{1,0:T(8,128)(2,1)}), bf16[2048,2048]{1,0:T(8,128)(2,1)}) %all-gather.9.cloned.1.call-update) | async-done | bytes 8388624 | tf_op jit(solution)/shard_map/all_gather | solution.py:345
  216.9 9.4 fusion.15
  228.2 19.2 %all-reduce.7.cloned.1.call-done = f32[128,160]{0,1:T(8,128)} async-done(((f32[128,160]{0,1:T(8,128)}), f32[128,160]{0,1:T(8,128)}) %all-reduce.7.cloned.1.call-update) | async-done | bytes 81936 | tf_op jit(solution)/shard_map/psum | solution.py:369
  251.5 4.1 shard_map.652
  257.4 4.2 shard_map.654
  262.6 38.4 %all-gather.11.cloned.1.call-done = f32[384,2048]{1,0:T(8,128)} async-done(((f32[24,2048]{1,0:T(8,128)}), f32[384,2048]{1,0:T(8,128)}) %all-gather.11.cloned.1.call-update) | async-done | bytes 3145744 | tf_op jit(solution)/shard_map/all_gather | solution.py:384
  302.2 7.9 shard_map.653
  311.2 36.6 %all-gather.13.cloned.1.call-done = f32[384,2048]{1,0:T(8,128)} async-done(((f32[24,2048]{1,0:T(8,128)}), f32[384,2048]{1,0:T(8,128)}) %all-gather.13.cloned.1.call-update) | async-done | bytes 3145744 | tf_op jit(solution)/shard_map/all_gather | solution.py:406
  347.7 18.7 %shard_map.655 = (f32[128,2048]{1,0:T(8,128)S(1)}, f32[128,2048]{1,0:T(8,128)S(1)}, f32[16,2048]{1,0:T(8,128)S(1)}, f32[128,16,128]{2,1,0:T(8,128)S(1)}, f32[128,16,128]{2,1,0:T(8,128)S(1)}) custom-call(s32[1]{0:T(128)} %bitcast.place_ref, f32[128,2048]{1,0:T(8,128)S(1)} %get-tuple-element.235.step_ref, f32[128,2048]{1,0:T(8,128)} %copy-done, ...), custom_call_target="tpu_custom_call" | custom-call | tf_op jit(solution)/shard_map/pallas_call | solution.py:250
  370.4 5.5 convert_reduce_fusion
  377.4 10.4 psum.92
  387.9 5.8 multiply_reduce_fusion.12
  397.6 12.7 convolution_bitcast_fusion.1
  410.4 7.1 convolution_convert_fusion
  422.7 9.2 convolution_bitcast_fusion
  433.3 13.4 fusion.23
  453.1 149.7 %all-reduce.11.cloned.1.call-done = (f32[4,4096]{1,0:T(4,128)}, f32[160,4096]{1,0:T(8,128)}, f32[128,4096]{1,0:T(8,128)}, f32[16,4096]{1,0:T(8,128)}) async-done(((f32[4,4096]{1,0:T(4,128)}, f32[160,4096]{1,0:T(8,128)}, f32[128,4096]{1,0:T(8,128)}, f32[16,4096]{1,0:T(8,128)}), (f32[4,4096]{1,0:T(4,128)}, f32[160,4096]{1,0:T(8,128)}, f32[128,4096]{1,0:T(8,128)}, ...) | async-done | bytes 5046288 | tf_op jit(solution)/shard_map/psum | solution.py:501
  618.5 166.6 %reduce-scatter.11.cloned.1.call-done = f32[128,2048]{0,1:T(8,128)} async-done(((f32[2048,2048]{0,1:T(8,128)}), f32[128,2048]{0,1:T(8,128)}) %reduce-scatter.11.cloned.1.call-update) | async-done | bytes 1048592 | tf_op jit(solution)/shard_map/reduce_scatter | solution.py:465
  786.9 334.7 %reduce-scatter.9.cloned.1.call-done = f32[128,2,2048]{2,0,1:T(8,128)} async-done(((f32[2048,2,2048]{2,0,1:T(8,128)}), f32[128,2,2048]{2,0,1:T(8,128)}) %reduce-scatter.9.cloned.1.call-update) | async-done | bytes 2097168 | tf_op jit(solution)/shard_map/reduce_scatter | solution.py:464
  1132.1 121.7 %all-reduce.9.cloned.1.call-done = (f32[2048]{0:T(1024)}, f32[2,4096]{1,0:T(2,128)}, f32[2048]{0:T(1024)}, f32[4096]{0:T(1024)}, f32[3,4096]{1,0:T(4,128)}) async-done(((f32[2048]{0:T(1024)}, f32[2,4096]{1,0:T(2,128)}, f32[2048]{0:T(1024)}, f32[4096]{0:T(1024)}, f32[3,4096]{1,0:T(4,128)}), (f32[2048]{0:T(1024)}, f32[2,4096]{1,0:T(2,128)}, f32[2048]{0:T(1024)}, f32[4096]{0:T(1024)}, ...) | async-done | bytes 114704 | tf_op jit(solution)/shard_map/psum | solution.py:501
  1268.5 39.6 %all-reduce = (f32[2048]{0:T(1024)S(1)}, f32[9]{0:T(128)S(1)}) all-reduce(f32[2048]{0:T(1024)S(1)} %get-tuple-element.167, f32[9]{0:T(128)S(1)} %stack.87), channel_id=1, replica_groups=mesh['seq'=16,'tp'=2] {'seq','tp'}, use_global_device_ids=true, to_apply=%region_9.10 | all-reduce | flops 2057 | bytes 16456 | tf_op jit(solution)/shard_map/psum | solution.py:501
  (380 shorter events, 99.7 us)
Async XLA Ops:
  7.2 133.6 %all-gather.7.cloned.1.call-start = ((), (), s32[]{:S(2)}) async-start(), calls=%async_computation.4 | async-start | bytes 17825792 | tf_op jit(solution)/shard_map/all_gather | solution.py:344
  11.1 205.7 %all-gather.9.cloned.1.call-start = ((), (), s32[]{:S(2)}) async-start(), calls=%async_computation.6 | async-start | bytes 8912896 | tf_op jit(solution)/shard_map/all_gather | solution.py:345
  12.0 235.3 %all-reduce.7.cloned.1.call-start = ((), (), s32[]{:S(2)}) async-start(), calls=%async_computation.5 | async-start | bytes 163840 | tf_op jit(solution)/shard_map/psum | solution.py:369
  149.0 3.1 collective-permute-start
  228.1 72.9 %all-gather.11.cloned.1.call-start = ((), (), s32[]{:S(2)}) async-start(), calls=%async_computation.11 | async-start | bytes 3342336 | tf_op jit(solution)/shard_map/all_gather | solution.py:384
  255.6 92.1 %all-gather.13.cloned.1.call-start = ((), (), s32[]{:S(2)}) async-start(), calls=%async_computation.12 | async-start | bytes 3342336 | tf_op jit(solution)/shard_map/all_gather | solution.py:406
  262.6 186.8 %reduce-scatter.7.cloned.1.call-start = ((), (), s32[]{:S(2)}) async-start(), calls=%async_computation.8 | async-start | bytes 1572864 | tf_op jit(solution)/shard_map/reduce_scatter | solution.py:456
  393.7 3.1 collective-permute-start.1
  410.3 40.5 %reduce-scatter.5.cloned.1.call-start = ((), (), s32[]{:S(2)}) async-start(), calls=%async_computation.7 | async-start | bytes 786432 | tf_op jit(solution)/shard_map/reduce_scatter | solution.py:394
  417.5 185.3 %all-reduce.11.cloned.1.call-start = ((), (), s32[]{:S(2)}) async-start(), calls=%async_computation.14 | async-start | bytes 10092544 | tf_op jit(solution)/shard_map/psum | solution.py:501
  422.7 362.3 %reduce-scatter.11.cloned.1.call-start = ((), (), s32[]{:S(2)}) async-start(), calls=%async_computation.10 | async-start | bytes 17825792 | tf_op jit(solution)/shard_map/reduce_scatter | solution.py:465
  432.0 689.6 %reduce-scatter.9.cloned.1.call-start = ((), (), s32[]{:S(2)}) async-start(), calls=%async_computation.9 | async-start | bytes 35651584 | tf_op jit(solution)/shard_map/reduce_scatter | solution.py:464
  446.8 807.0 %all-reduce.9.cloned.1.call-start = ((), (), s32[]{:S(2)}) async-start(), calls=%async_computation.13 | async-start | bytes 262144 | tf_op jit(solution)/shard_map/psum | solution.py:501
  607.8 718.8 %copy-start.87 = (f32[160]{0:T(256)}, f32[160]{0:T(256)S(1)}, u32[]{:S(2)}) copy-start(f32[160]{0:T(256)S(1)} %get-tuple-element.219) | copy-start | bytes 1924
  611.0 719.4 %copy-start.108 = (f32[128]{0:T(128)}, f32[128]{0:T(128)S(1)}, u32[]{:S(2)}) copy-start(f32[128]{0:T(128)S(1)} %get-tuple-element.215) | copy-start | bytes 1540
  612.4 721.0 %copy-start.109 = (f32[16]{0:T(128)}, f32[16]{0:T(128)S(1)}, u32[]{:S(2)}) copy-start(f32[16]{0:T(128)S(1)} %get-tuple-element.211) | copy-start | bytes 196
  613.2 720.2 %copy-start.41 = (f32[16,2048]{1,0:T(8,128)}, f32[16,2048]{1,0:T(8,128)S(1)}, u32[]{:S(2)}) copy-start(f32[16,2048]{1,0:T(8,128)S(1)} %get-tuple-element.209) | copy-start | bytes 393220
  615.2 508.4 %copy-start.78 = (f32[2048]{0:T(1024)}, f32[2048]{0:T(1024)S(1)}, u32[]{:S(2)}) copy-start(f32[2048]{0:T(1024)S(1)} %get-tuple-element.275) | copy-start | bytes 24580
  615.2 711.3 %copy-start.58 = (f32[2048]{0:T(1024)}, f32[2048]{0:T(1024)S(1)}, u32[]{:S(2)}) copy-start(f32[2048]{0:T(1024)S(1)} %get-tuple-element.274) | copy-start | bytes 24580
  615.3 715.2 %copy-start.59 = (f32[2048]{0:T(1024)}, f32[2048]{0:T(1024)S(1)}, u32[]{:S(2)}) copy-start(f32[2048]{0:T(1024)S(1)} %get-tuple-element.273) | copy-start | bytes 24580
  615.3 718.1 %copy-start.60 = (f32[2048]{0:T(1024)}, f32[2048]{0:T(1024)S(1)}, u32[]{:S(2)}) copy-start(f32[2048]{0:T(1024)S(1)} %get-tuple-element.272) | copy-start | bytes 24580
  617.3 506.4 %copy-start.121 = (f32[128]{0:T(128)S(1)}, f32[128]{0:T(128)}, u32[]{:S(2)}) copy-start(f32[128]{0:T(128)} %param.43) | copy-start | bytes 1540
  617.3 506.6 %copy-start.86 = (f32[2,2048]{1,0:T(2,128)S(1)}, f32[2,2048]{1,0:T(2,128)}, u32[]{:S(2)}) copy-start(f32[2,2048]{1,0:T(2,128)} %param.44) | copy-start | bytes 49156
  785.0 342.8 %copy-start.11 = (f32[128,2048]{0,1:T(8,128)S(1)}, f32[128,2048]{0,1:T(8,128)}, u32[]{:S(2)}) copy-start(f32[128,2048]{0,1:T(8,128)} %reduce-scatter.11.cloned.1.call-done) | copy-start | bytes 3145732
  (114 other events, 5024.3 us)
Sparse Core Ops, SparseCore 0:
  11.2 129.5 all-gather.6
  143.6 73.2 all-gather.8
  228.2 19.1 all-reduce.6
  255.8 45.1 all-gather.10
  303.7 43.9 all-gather.12
  410.4 19.3 reduce-scatter.6
  432.7 14.5 reduce-scatter.4
  455.2 147.5 all-reduce.10
  607.5 177.5 reduce-scatter.10
  789.7 331.8 reduce-scatter.8
  1130.1 123.6 all-reduce.8

commit v2 on v1

--- a/solution.py
+++ b/solution.py
@@ -12,6 +12,7 @@
 DECAY = 0.5
 CLIP = 0.5
 RATES = (0.45, 0.02, 0.03, 0.1, 0.05, 0.016, 0.09, 1.8, 0.3, 0.45)
+MESH = pl.DeviceIdType.MESH
 LOG2E = 1.4426950408889634
 RESET = 1e9
 TILE = 512
@@ -29,26 +30,11 @@
     return sigmoid_v * (1.0 + values * (1.0 - sigmoid_v))
 
 
-def widen_last(piece_in, index_of, total_len):
-    zero_block = jnp.zeros(piece_in.shape[:-1] + (total_len,), jnp.float32)
-    return lax.dynamic_update_slice_in_dim(
-        zero_block, piece_in, index_of * piece_in.shape[-1], piece_in.ndim - 1
-    )
-
-
-def narrow(full_array, index_of, size_of):
-    return lax.dynamic_slice_in_dim(full_array, index_of * size_of, size_of, full_array.ndim - 1)
-
-
-def factor_update(full_grad, local_grad, rows_old, cols_old):
-    rows_new = DECAY * rows_old + (1.0 - DECAY) * (
-        jnp.mean(full_grad * full_grad, axis=1) + EPS_FACTOR
-    )
-    cols_new = DECAY * cols_old + (1.0 - DECAY) * (
-        jnp.mean(local_grad * local_grad, axis=0) + EPS_FACTOR
-    )
+def factor_update(grad, row_sums, rows_old, cols_old, channels):
+    rows_new = DECAY * rows_old + (1.0 - DECAY) * (row_sums / channels + EPS_FACTOR)
+    cols_new = DECAY * cols_old + (1.0 - DECAY) * (jnp.mean(grad * grad, axis=0) + EPS_FACTOR)
     scale_sq = rows_new[:, None] * cols_new[None, :] / jnp.mean(rows_new)
-    return (rows_new, cols_new, local_grad * lax.rsqrt(scale_sq))
+    return (rows_new, cols_new, grad * lax.rsqrt(scale_sq))
 
 
 def moment_update(grad_in, moment_old):
@@ -275,6 +261,357 @@
         ],
         compiler_params=pltpu.CompilerParams(vmem_limit_bytes=VMEM_LIMIT),
     )(place, step, drive, grad, enter, leave, rate, start, pieces)
+
+
+def on_block():
+    return lax.axis_size("seq") == 16 and lax.axis_size("tp") == 2
+
+
+def position():
+    place = lax.axis_index("seq")
+    return lax.div(place, 4), lax.rem(lax.div(place, 2), 2), lax.rem(place, 2)
+
+
+def device(z, x, core):
+    return (z * 4 + x * 2 + core, lax.axis_index("tp"))
+
+
+def other_half():
+    return (lax.axis_index("seq"), 1 - lax.axis_index("tp"))
+
+
+def greet(peers):
+    barrier = pltpu.get_barrier_semaphore()
+    for peer in peers:
+        pl.semaphore_signal(barrier, inc=1, device_id=peer, device_id_type=MESH)
+    pl.semaphore_wait(barrier, len(peers))
+
+
+def remote(source, target, sent, arrived, peer):
+    return pltpu.make_async_remote_copy(
+        src_ref=source,
+        dst_ref=target,
+        send_sem=sent,
+        recv_sem=arrived,
+        device_id=peer,
+        device_id_type=MESH,
+    )
+
+
+def sum_kernel(
+    shared, mine_ref, pair_ref, out_ref, pair_out_ref, work, far, pair_far, sent, arrived
+):
+    z, x, core = position()
+    seq_rows = mine_ref.shape[0]
+    across = [device(lax.rem(z + step, 4), x, core) for step in (1, 2, 3)]
+    peers = [device(z, x, 1 - core), device(z, 1 - x, core)] + across + [other_half()]
+    greet(peers)
+    pair = remote(pair_ref, pair_far, sent.at[0], arrived.at[0], peers[5])
+    pair.start()
+    first = remote(mine_ref, far.at[0], sent.at[1], arrived.at[1], peers[0])
+    first.start()
+    first.wait()
+    work[4] = mine_ref[...] + far[0]
+    second = remote(work.at[4], far.at[1], sent.at[2], arrived.at[2], peers[1])
+    second.start()
+    second.wait()
+    work[z] = work[4] + far[1]
+    copies = [
+        remote(work.at[z], work.at[z], sent.at[3 + at], arrived.at[3 + at], across[at])
+        for at in range(3)
+    ]
+    for copy in copies:
+        copy.start()
+    for copy in copies:
+        copy.wait()
+    out_ref[...] = (work[0] + work[1]) + (work[2] + work[3])
+    last = remote(
+        out_ref.at[seq_rows - shared :],
+        far.at[2, seq_rows - shared :],
+        sent.at[6],
+        arrived.at[6],
+        peers[5],
+    )
+    last.start()
+    pair.wait()
+    pair_out_ref[...] = pair_ref[...] + pair_far[...]
+    last.wait()
+    out_ref[seq_rows - shared :] = (
+        out_ref[seq_rows - shared :] + far[2, seq_rows - shared :]
+    )
+
+
+def sum_over(seq_part, shared_part, tp_part, ident):
+    mine = jnp.concatenate([seq_part, shared_part], axis=0)
+    seq_rows, shared = mine.shape[0], shared_part.shape[0]
+    if not on_block():
+        total = lax.psum(mine, "seq")
+        both = lax.psum(total[seq_rows - shared :], "tp")
+        return total[: seq_rows - shared], both, lax.psum(tp_part, "tp")
+    vmem = pl.BlockSpec(memory_space=pltpu.VMEM)
+    total, pair = pl.pallas_call(
+        functools.partial(sum_kernel, shared),
+        in_specs=[vmem, vmem],
+        out_specs=[vmem, vmem],
+        out_shape=[
+            jax.ShapeDtypeStruct(mine.shape, jnp.float32),
+            jax.ShapeDtypeStruct(tp_part.shape, jnp.float32),
+        ],
+        scratch_shapes=[
+            pltpu.VMEM((5,) + mine.shape, jnp.float32),
+            pltpu.VMEM((3,) + mine.shape, jnp.float32),
+            pltpu.VMEM(tp_part.shape, jnp.float32),
+            pltpu.SemaphoreType.DMA((7,)),
+            pltpu.SemaphoreType.DMA((7,)),
+        ],
+        compiler_params=pltpu.CompilerParams(collective_id=ident, has_side_effects=True),
+    )(mine, tp_part)
+    return total[: seq_rows - shared], total[seq_rows - shared :], pair
+
+
+def reduce_kernel(
+    hidden_ref,
+    grads_ref,
+    extra_ref,
+    out_ref,
+    full_ref,
+    send_core,
+    come_core,
+    send_x,
+    come_x,
+    send_z,
+    come_z,
+    extra_come_core,
+    extra_send_x,
+    extra_come_x,
+    extra_send_z,
+    extra_come_z,
+    sent_core,
+    got_core,
+    sent_x,
+    got_x,
+    sent_z,
+    got_z,
+    extra_sent,
+    extra_got,
+):
+    z, x, core = position()
+    chunks, width = send_core.shape[0], send_core.shape[3]
+    away = [lax.rem(z + step, 4) for step in (1, 2, 3)]
+    core_peer, x_peer = device(z, x, 1 - core), device(z, 1 - x, core)
+    z_peers = [device(at, x, core) for at in away]
+    greet([core_peer, x_peer] + z_peers)
+
+    def product(chunk, block):
+        return jnp.dot(
+            hidden_ref[block],
+            grads_ref[:, chunk * width : (chunk + 1) * width],
+            preferred_element_type=jnp.float32,
+        )
+
+    def to_core(chunk):
+        return remote(
+            send_core.at[chunk], come_core.at[chunk], sent_core.at[chunk], got_core.at[chunk], core_peer
+        )
+
+    def to_x(chunk):
+        return remote(send_x.at[chunk], come_x.at[chunk], sent_x.at[chunk], got_x.at[chunk], x_peer)
+
+    def to_z(chunk, at):
+        return remote(
+            send_z.at[chunk, at],
+            come_z.at[chunk, at],
+            sent_z.at[chunk, at],
+            got_z.at[chunk, at],
+            z_peers[at],
+        )
+
+    def stage_core(chunk):
+        def one(pair, _):
+            send_core[chunk, pair] = product(chunk, pair * 2 + 1 - core).astype(jnp.bfloat16)
+            return 0
+
+        lax.fori_loop(0, 8, one, 0)
+        to_core(chunk).start()
+
+    def after_core(chunk, pair):
+        return product(chunk, pair * 2 + core) + come_core[chunk, pair].astype(jnp.float32)
+
+    def stage_x(chunk):
+        to_core(chunk).wait_recv()
+
+        def one(level, _):
+            send_x[chunk, level] = after_core(chunk, level * 2 + 1 - x).astype(jnp.bfloat16)
+            return 0
+
+        lax.fori_loop(0, 4, one, 0)
+        to_x(chunk).start()
+
+    def stage_z(chunk):
+        to_x(chunk).wait_recv()
+
+        def after_x(level):
+            return after_core(chunk, level * 2 + x) + come_x[chunk, level].astype(jnp.float32)
+
+        def one(at, _):
+            send_z[chunk, at] = after_x(lax.rem(z + 1 + at, 4)).astype(jnp.bfloat16)
+            return 0
+
+        lax.fori_loop(0, 3, one, 0)
+        for at in range(3):
+            to_z(chunk, at).start()
+        out_ref[:, chunk * width : (chunk + 1) * width] = after_x(z)
+
+    def stage_last(chunk):
+        for at in range(3):
+            to_z(chunk, at).wait_recv()
+        total = come_z[chunk, 0].astype(jnp.float32) + come_z[chunk, 1].astype(jnp.float32)
+        total = total + come_z[chunk, 2].astype(jnp.float32)
+        columns = slice(chunk * width, (chunk + 1) * width)
+        out_ref[:, columns] = out_ref[:, columns] + total
+
+    extra_core = remote(
+        extra_ref.at[:, 1 - core], extra_come_core, extra_sent.at[0], extra_got.at[0], core_peer
+    )
+    extra_x = remote(extra_send_x, extra_come_x, extra_sent.at[1], extra_got.at[1], x_peer)
+    extra_z = [
+        remote(
+            extra_send_z.at[at], extra_come_z.at[at], extra_sent.at[2 + at], extra_got.at[2 + at], z_peers[at]
+        )
+        for at in range(3)
+    ]
+    own = full_ref.at[z, x, core]
+    back_z = [
+        remote(own, own, extra_sent.at[5 + at], extra_got.at[5 + at], z_peers[at]) for at in range(3)
+    ]
+    held = full_ref.at[:, x, core]
+    back_x = remote(held, held, extra_sent.at[8], extra_got.at[8], x_peer)
+    halves = full_ref.at[:, :, core]
+    back_core = remote(halves, halves, extra_sent.at[9], extra_got.at[9], core_peer)
+
+    def extra_after_core(pair):
+        return extra_ref[pair, core].astype(jnp.float32) + extra_come_core[pair].astype(jnp.float32)
+
+    def extra_stage_x():
+        extra_core.wait_recv()
+
+        def one(level, _):
+            extra_send_x[level] = extra_after_core(level * 2 + 1 - x).astype(jnp.bfloat16)
+            return 0
+
+        lax.fori_loop(0, 4, one, 0)
+        extra_x.start()
+
+    def extra_after_x(level):
+        return extra_after_core(level * 2 + x) + extra_come_x[level].astype(jnp.float32)
+
+    def extra_stage_z():
+        extra_x.wait_recv()
+
+        def one(at, _):
+            extra_send_z[at] = extra_after_x(lax.rem(z + 1 + at, 4)).astype(jnp.bfloat16)
+            return 0
+
+        lax.fori_loop(0, 3, one, 0)
+        for copy in extra_z:
+            copy.start()
+
+    def extra_stage_last():
+        for copy in extra_z:
+            copy.wait_recv()
+        total = extra_after_x(z)
+        for at in range(3):
+            total = total + extra_come_z[at].astype(jnp.float32)
+        full_ref[z, x, core] = total.astype(full_ref.dtype)
+        for copy in back_z:
+            copy.start()
+
+    def extra_back_x():
+        for copy in back_z:
+            copy.wait_recv()
+        back_x.start()
+
+    def extra_back_core():
+        back_x.wait_recv()
+        back_core.start()
+
+    extra_core.start()
+    extra_steps = {1: extra_stage_x, 3: extra_stage_z, 5: extra_stage_last, 7: extra_back_x, 9: extra_back_core}
+    for step in range(max(chunks + 5, 10)):
+        if step < chunks:
+            stage_core(step)
+        if 0 <= step - 1 < chunks:
+            stage_x(step - 1)
+        if 0 <= step - 3 < chunks:
+            stage_z(step - 3)
+        if 0 <= step - 5 < chunks:
+            stage_last(step - 5)
+        if step in extra_steps:
+            extra_steps[step]()
+    back_core.wait_recv()
+    for chunk in range(chunks):
+        to_core(chunk).wait_send()
+        to_x(chunk).wait_send()
+        for at in range(3):
+            to_z(chunk, at).wait_send()
+    for copy in [extra_core, extra_x] + extra_z + back_z + [back_x, back_core]:
+        copy.wait_send()
+
+
+def reduce_grads(hidden, grads, extra, ident):
+    rows, model = hidden.shape
+    columns = grads.shape[1]
+    extra_columns = extra.shape[1]
+    if not on_block():
+        product = jnp.einsum("td,tn->dn", hidden, grads, preferred_element_type=jnp.float32)
+        return (
+            lax.psum_scatter(product, "seq", scatter_dimension=0, tiled=True),
+            lax.psum(extra, "seq"),
+        )
+    share, extra_share = model // 16, extra.shape[0] // 16
+    width = 512
+    chunks = columns // width
+    low = jnp.bfloat16
+    vmem = pl.BlockSpec(memory_space=pltpu.VMEM)
+    dma = pltpu.SemaphoreType.DMA
+    out, full = pl.pallas_call(
+        reduce_kernel,
+        in_specs=[vmem, vmem, vmem],
+        out_specs=[vmem, vmem],
+        out_shape=[
+            jax.ShapeDtypeStruct((share, columns), jnp.float32),
+            jax.ShapeDtypeStruct((4, 2, 2, extra_share, extra_columns), low),
+        ],
+        scratch_shapes=[
+            pltpu.VMEM((chunks, 8, share, width), low),
+            pltpu.VMEM((chunks, 8, share, width), low),
+            pltpu.VMEM((chunks, 4, share, width), low),
+            pltpu.VMEM((chunks, 4, share, width), low),
+            pltpu.VMEM((chunks, 3, share, width), low),
+            pltpu.VMEM((chunks, 3, share, width), low),
+            pltpu.VMEM((8, extra_share, extra_columns), low),
+            pltpu.VMEM((4, extra_share, extra_columns), low),
+            pltpu.VMEM((4, extra_share, extra_columns), low),
+            pltpu.VMEM((3, extra_share, extra_columns), low),
+            pltpu.VMEM((3, extra_share, extra_columns), low),
+            dma((chunks,)),
+            dma((chunks,)),
+            dma((chunks,)),
+            dma((chunks,)),
+            dma((chunks, 3)),
+            dma((chunks, 3)),
+            dma((10,)),
+            dma((10,)),
+        ],
+        compiler_params=pltpu.CompilerParams(
+            collective_id=ident, has_side_effects=True, vmem_limit_bytes=VMEM_LIMIT
+        ),
+    )(
+        hidden.T.reshape(16, share, rows),
+        grads,
+        extra.astype(low).reshape(8, 2, extra_share, extra_columns),
+    )
+    return out, full.reshape(extra.shape).astype(jnp.float32)
 
 
 def on_device(
@@ -452,18 +789,30 @@
         )
     conv_w_grad = jnp.stack(conv_w_rows, axis=0)
     conv_b_grad = jnp.sum(d_conv_pre, axis=0)
-    d_projected = jnp.stack([d_conv_in.astype(jnp.bfloat16), d_gate], axis=1)
+    d_projected = jnp.concatenate([d_conv_in.astype(jnp.bfloat16), d_gate], axis=1)
     d_hidden = lax.psum_scatter(
-        jnp.einsum("tke,dke->td", d_projected, in_back, preferred_element_type=jnp.float32),
+        jnp.einsum(
+            "tn,dn->td",
+            d_projected,
+            in_back.reshape(model_dim, 2 * inner_dim),
+            preferred_element_type=jnp.float32,
+        ),
         "tp",
         scatter_dimension=0,
         tiled=True,
     )
-    d_in_w = jnp.einsum("td,tke->dke", hidden, d_projected, preferred_element_type=jnp.float32)
-    in_grad, out_grad = (
-        lax.psum_scatter(d_in_w, "seq", scatter_dimension=0, tiled=True),
-        lax.psum_scatter(d_out_w, "seq", scatter_dimension=0, tiled=True),
-    )
+    vector_grads = jnp.stack([conv_b_grad, step_bias_grad, skip_grad], axis=0)
+    small_grads = jnp.concatenate(
+        [step_w_grad, select_w_grad, decay_grad, conv_w_grad, vector_grads], axis=0
+    )
+    small_count = small_grads.shape[0]
+    small_grads = jnp.pad(small_grads, ((0, -small_count % 128), (0, 0)))
+    in_grad, small_full = reduce_grads(hidden, d_projected, small_grads.T, 0)
+    in_grad = in_grad.reshape(in_weight.shape)
+    small_full = small_full.T
+    out_grad = lax.psum_scatter(
+        d_out_w.astype(jnp.bfloat16), "seq", scatter_dimension=0, tiled=True
+    ).astype(jnp.float32)
     gain_part = jnp.sum(d_hidden * normed, axis=0)
     scaled = d_hidden * norm_gain[None, :]
     cot_half = lax.dynamic_slice_in_dim(cotangent, tp_index * half_rows, half_rows, 0).astype(
@@ -472,94 +821,85 @@
     input_grad = cot_half + inv_rms * (
         scaled - normed * jnp.mean(scaled * normed, axis=1, keepdims=True)
     )
+    edges = [step_rank, select_weight.shape[0], states, conv_taps, 3]
+    edges = [sum(edges[:at]) for at in range(len(edges) + 1)]
+    step_local, select_local, decay_local, conv_local, vector_local = [
+        small_full[low:high] for low, high in zip(edges, edges[1:])
+    ]
     in_square = in_grad * in_grad
-    in_row_piece = (DECAY * in_rows + (1.0 - DECAY) * EPS_FACTOR) * tp_first + (
+    out_square = out_grad * out_grad
+    in_row_part = jnp.sum(in_square, axis=(1, 2))
+    out_row_part = jnp.sum(out_square, axis=1)
+    small_row_part = jnp.sum(small_full * small_full, axis=1)
+    in_total = jnp.sum(DECAY * in_rows + (1.0 - DECAY) * EPS_FACTOR) * tp_first + (
         1.0 - DECAY
-    ) * jnp.sum(in_square, axis=(1, 2)) / (2 * channels)
-    in_col_piece = (DECAY * in_cols + (1.0 - DECAY) * EPS_FACTOR) * seq_first + (
+    ) * jnp.sum(in_row_part) / (2 * channels)
+    out_total = jnp.sum(DECAY * out_rows + (1.0 - DECAY) * EPS_FACTOR) * tp_first + (
         1.0 - DECAY
-    ) * jnp.sum(in_square, axis=0) / model_dim
-    out_square = out_grad * out_grad
-    out_row_piece = (DECAY * out_rows + (1.0 - DECAY) * EPS_FACTOR) * tp_first + (
-        1.0 - DECAY
-    ) * jnp.sum(out_square, axis=1) / channels
-    out_col_piece = (DECAY * out_cols + (1.0 - DECAY) * EPS_FACTOR) * seq_first + (
-        1.0 - DECAY
-    ) * jnp.sum(out_square, axis=0) / model_dim
-    vector_grads = jnp.stack([conv_b_grad, step_bias_grad, skip_grad], axis=0)
-    (
-        conv_full,
-        vector_full,
-        select_full,
-        step_full,
-        decay_full,
-        gain_grad,
-        in_rows_all,
-        in_cols_all,
-        out_rows_all,
-        out_cols_all,
-    ) = lax.psum(
-        (
-            widen_last(conv_w_grad, tp_index, channels),
-            widen_last(vector_grads, tp_index, channels),
-            widen_last(select_w_grad, tp_index, channels),
-            widen_last(step_w_grad, tp_index, channels),
-            widen_last(decay_grad, tp_index, channels),
-            gain_part,
-            widen_last(in_row_piece, seq_index, model_dim),
-            widen_last(in_col_piece, tp_index, channels),
-            widen_last(out_row_piece, seq_index, model_dim),
-            widen_last(out_col_piece, tp_index, channels),
-        ),
-        ("seq", "tp"),
-    )
-    conv_local = narrow(conv_full, tp_index, inner_dim)
-    vector_local = narrow(vector_full, tp_index, inner_dim)
-    select_local = narrow(select_full, tp_index, inner_dim)
-    step_local = narrow(step_full, tp_index, inner_dim)
-    decay_local = narrow(decay_full, tp_index, inner_dim)
+    ) * jnp.sum(out_row_part) / channels
+    seq_part = jnp.concatenate(
+        [jnp.sum(in_square, axis=0).reshape(-1, 128), jnp.sum(out_square, axis=0).reshape(-1, 128)]
+    )
+    shared_part = jnp.concatenate(
+        [
+            gain_part.reshape(-1, 128),
+            jnp.broadcast_to(in_total, (8, 128)),
+            jnp.broadcast_to(out_total, (8, 128)),
+        ]
+    )
+    row_parts = jnp.concatenate([in_row_part, out_row_part, small_row_part])
+    row_parts = jnp.pad(row_parts, (0, -row_parts.shape[0] % 1024)).reshape(-1, 128)
+    col_sums, shared_sums, row_sums = sum_over(seq_part, shared_part, row_parts, 1)
+    col_sums = col_sums.reshape(-1)
+    in_col_sums = col_sums[: 2 * inner_dim].reshape(2, inner_dim)
+    out_col_sums = col_sums[2 * inner_dim :]
+    gain_grad = shared_sums[: model_dim // 128].reshape(-1)
+    in_mean = shared_sums[model_dim // 128, 0] / model_dim
+    out_mean = shared_sums[model_dim // 128 + 8, 0] / model_dim
+    row_sums = row_sums.reshape(-1)
+    in_row_sums = row_sums[:row_share]
+    out_row_sums = row_sums[row_share : 2 * row_share]
+    small_row_sums = row_sums[2 * row_share :]
+    in_rows_new = DECAY * in_rows + (1.0 - DECAY) * (in_row_sums / (2 * channels) + EPS_FACTOR)
+    in_cols_new = DECAY * in_cols + (1.0 - DECAY) * (in_col_sums / model_dim + EPS_FACTOR)
+    out_rows_new = DECAY * out_rows + (1.0 - DECAY) * (out_row_sums / channels + EPS_FACTOR)
+    out_cols_new = DECAY * out_cols + (1.0 - DECAY) * (out_col_sums / model_dim + EPS_FACTOR)
+    step_rows_new, step_cols_new, stepw_update = factor_update(
+        step_local, small_row_sums[edges[0] : edges[1]], step_rows, step_cols, channels
+    )
+    select_rows_new, select_cols_new, select_update = factor_update(
+        select_local, small_row_sums[edges[1] : edges[2]], select_rows, select_cols, channels
+    )
+    decay_rows_new, decay_cols_new, decay_update = factor_update(
+        decay_local, small_row_sums[edges[2] : edges[3]], decay_rows, decay_cols, channels
+    )
     conv_rows_new, conv_cols_new, conv_update = factor_update(
-        conv_full, conv_local, conv_rows, conv_cols
-    )
-    select_rows_new, select_cols_new, select_update = factor_update(
-        select_full, select_local, select_rows, select_cols
-    )
-    step_rows_new, step_cols_new, stepw_update = factor_update(
-        step_full, step_local, step_rows, step_cols
-    )
-    decay_rows_new, decay_cols_new, decay_update = factor_update(
-        decay_full, decay_local, decay_rows, decay_cols
+        conv_local, small_row_sums[edges[3] : edges[4]], conv_rows, conv_cols, channels
     )
     bias_moment_new, convb_update = moment_update(vector_local[0], bias_moment)
     step_moment_new, stepb_update = moment_update(vector_local[1], step_moment)
     skip_moment_new, skip_update = moment_update(vector_local[2], skip_moment)
     gain_moment_new, gain_update = moment_update(gain_grad, norm_moment)
-    in_rows_new = narrow(in_rows_all, seq_index, row_share)
-    in_cols_new = narrow(in_cols_all, tp_index, inner_dim)
-    in_update = in_grad * lax.rsqrt(
-        in_rows_new[:, None, None] * in_cols_new[None] / jnp.mean(in_rows_all)
-    )
-    out_rows_new = narrow(out_rows_all, seq_index, row_share)
-    out_cols_new = narrow(out_cols_all, tp_index, inner_dim)
-    out_update = out_grad * lax.rsqrt(
-        out_rows_new[:, None] * out_cols_new[None, :] / jnp.mean(out_rows_all)
-    )
-    clip_totals = lax.psum(
-        jnp.stack(
-            [
-                sum_squares(in_update),
-                sum_squares(out_update),
-                seq_first * sum_squares(conv_update),
-                seq_first * sum_squares(select_update),
-                seq_first * sum_squares(stepw_update),
-                seq_first * sum_squares(decay_update),
-                seq_first * sum_squares(convb_update),
-                seq_first * sum_squares(stepb_update),
-                seq_first * sum_squares(skip_update),
-            ]
-        ),
-        ("seq", "tp"),
-    )
+    in_update = in_grad * lax.rsqrt(in_rows_new[:, None, None] * in_cols_new[None] / in_mean)
+    out_update = out_grad * lax.rsqrt(out_rows_new[:, None] * out_cols_new[None, :] / out_mean)
+    squares = jnp.stack(
+        [
+            sum_squares(in_update),
+            sum_squares(out_update),
+            seq_first * sum_squares(conv_update),
+            seq_first * sum_squares(select_update),
+            seq_first * sum_squares(stepw_update),
+            seq_first * sum_squares(decay_update),
+            seq_first * sum_squares(convb_update),
+            seq_first * sum_squares(stepb_update),
+            seq_first * sum_squares(skip_update),
+        ]
+    )
+    nothing = jnp.zeros((8, 128), jnp.float32)
+    _, clip_totals, _ = sum_over(
+        nothing, jnp.broadcast_to(jnp.pad(squares, (0, 7))[:, None], (16, 128)), nothing, 2
+    )
+    clip_totals = clip_totals[:, 0]
     gain_new = apply_step(norm_gain, gain_update, sum_squares(gain_update), model_dim, RATES[0])
     in_new = apply_step(in_weight, in_update, clip_totals[0], model_dim * 2 * channels, RATES[1])
     out_new = apply_step(out_weight, out_update, clip_totals[1], model_dim * channels, RATES[2])

time: 1350 us -> 752 us (0.56)
  waiting for transfers between devices: 1050 us -> 254 us
  Pallas kernels: 35 us -> 244 us
  blocking collectives: 59.9 us -> 19.1 us
  local copies, waits for them, and re-layouts: 41.3 us -> 80.8 us
  matrix products: 71.4 us -> 45.4 us
    reduce_scatter x3 -> x1, waiting for transfers between devices: 501 us -> 0.01 us  [on_device(): lax.psum_scatter(jnp.einsum('tn,dn->td', d_projected, in_back.reshape(mod...]
    psum x2 -> x0, waiting for transfers between devices: 271 us -> none  [on_device(): lax.psum((widen_last(conv_w_grad, tp_index, channels), widen_last(vector_...]
    pallas_call x0 -> x3, Pallas kernels: none -> 209 us  [the longest x1 179 us: reduce_grads(): pl.pallas_call(reduce_kernel, in_specs=[vmem, vmem, vmem], out_specs=[vme...]
    psum x1 -> x0, blocking collectives: 39.6 us -> none  [on_device(): lax.psum((widen_last(conv_w_grad, tp_index, channels), widen_last(vector_...]
    dot_general x2 -> x1, matrix products: 26.1 us -> 3.4 us  [on_device(): jnp.einsum('tn,dn->td', d_projected, in_back.reshape(model_dim, 2 * inner...]
    all_gather x0 -> x1, local copies, waits for them, and re-layouts: none -> 22.6 us  [on_device(): lax.all_gather(in_weight.astype(jnp.bfloat16), 'seq', axis=0, tiled=True)]
    all_gather x1, waiting for transfers between devices: 38.4 us -> 15.8 us  [on_device(): lax.all_gather(piece_state(held_step, drive, enter, decay_rate, False), '...]
    unnamed x258 -> x224, local copies, waits for them, and re-layouts: 30.4 us -> 34.6 us
  transfers between devices with their start and end apart: 13 -> 10, of which waited for: 11 -> 6; matrix products, arithmetic and copies ran while one was open for 5% -> 13% of each run, Pallas kernels for 1% -> 26%
where the time goes in v2:
time: 752 us; the launch traced here: 742 us
  waiting for transfers between devices  254 us (34%)
  Pallas kernels  244 us (32%)
  local copies, waits for them, and re-layouts  80.8 us (11%)
  other arithmetic  60.1 us (8%)
  matrix products  45.4 us (6%)
  between operations  34.2 us (5%)
  blocking collectives  19.1 us (3%)
    pallas_call x1, Pallas kernels, reduce_grads(): pl.pallas_call(reduce_kernel, in_specs=[vmem, vmem, vmem], out_specs=[vme...  179 us
    all_gather x1, waiting for transfers between devices, on_device(): lax.all_gather(in_weight.astype(jnp.bfloat16), 'seq', axis=0, tiled=True)  118 us
    all_gather x1, waiting for transfers between devices, on_device(): lax.all_gather(out_weight.astype(jnp.bfloat16), 'seq', axis=0, tiled=True)  63.5 us
    all_gather x1, waiting for transfers between devices, on_device(): lax.all_gather(piece_state(held_step, d_mixed, leave, decay_rate, True),...  36.6 us
    unnamed x224, local copies, waits for them, and re-layouts  34.6 us
    pallas_call x2, Pallas kernels, sum_over(): pl.pallas_call(functools.partial(sum_kernel, shared), in_specs=[vmem, vme...  29.9 us
    all_gather x1, local copies, waits for them, and re-layouts, on_device(): lax.all_gather(in_weight.astype(jnp.bfloat16), 'seq', axis=0, tiled=True)  22.6 us
    psum x1, waiting for transfers between devices, on_device(): lax.psum(jnp.einsum('te,ke->tk', conv_out, select_low, preferred_element_...  19.2 us
  transfers between devices with their start and end apart: 10, of which 6 were waited for; matrix products, arithmetic and copies ran while one was open for 13% of the time, Pallas kernels for 26%

profile of v2, /device:TPU:0, one launch (start us, length us, event | category | flops | bytes accessed | tf_op | source)
XLA Modules:
  0.0 741.7 jit_solution(5751064070545717310)
XLA Ops:
  12.6 9.9 %all_gather.23 = bf16[128,2048]{1,0:T(8,128)(2,1)S(1)} all-gather(bf16[64,2048]{1,0:T(8,128)(2,1)S(1)} %fusion.23), channel_id=1, replica_groups=mesh['seq'=16,'tp'=2] {'tp'}, dimensions={0}, use_global_device_ids=true | all-gather | bytes 786432 | tf_op jit(solution)/shard_map/all_gather | solution.py:677
  23.3 117.5 %all-gather.7.cloned.1.call-done = bf16[2048,2,2048]{2,0,1:T(8,128)(2,1)} async-done(((bf16[128,2,2048]{2,0,1:T(8,128)(2,1)}), bf16[2048,2,2048]{2,0,1:T(8,128)(2,1)}) %all-gather.7.cloned.1.call-update) | async-done | bytes 16777232 | tf_op jit(solution)/shard_map/all_gather | solution.py:681
  140.8 8.1 %fusion.69 = (bf16[128,2,2048]{2,0,1:T(8,128)(2,1)S(1)}, f32[128,2,2048]{2,0,1:T(8,128)S(1)}) fusion(bf16[2048,2,2048]{2,0,1:T(8,128)(2,1)} %all-gather.7.cloned.1.call-done, bf16[128,2048]{1,0:T(8,128)(2,1)S(1)} %all_gather.23), kind=kOutput, calls=%fused_computation.185 | convolution fusion | flops 2148007936 | bytes 20447232 | tf_op jit(solution)/shard_map/td,dke->tke/dot_general | solution.py:684
  153.3 63.5 %all-gather.9.cloned.1.call-done = bf16[2048,2048]{1,0:T(8,128)(2,1)} async-done(((bf16[128,2048]{1,0:T(8,128)(2,1)}), bf16[2048,2048]{1,0:T(8,128)(2,1)}) %all-gather.9.cloned.1.call-update) | async-done | bytes 8388624 | tf_op jit(solution)/shard_map/all_gather | solution.py:682
  216.9 9.3 %fusion.15 = (bf16[2048]{0:T(1024)(128)(2,1)}, f32[128,2048]{1,0:T(8,128)}, bf16[128,2048]{1,0:T(8,128)(2,1)S(1)}, f32[128,2048]{1,0:T(8,128)}, f32[128,2048]{1,0:T(8,128)}) fusion(f32[128,2,2048]{2,0,1:T(8,128)S(1)} %get-tuple-element.319, f32[128]{0:T(128)S(1)} %get-tuple-element.314, f32[131,2048]{1,0:T(8,128)} %maximum_convert_fusion, ...), kind=kOutput, calls=%fused_computation.43 | convolution fusion | flops 1080031232 | bytes 17872384 | tf_op jit(solution)/shard_map/td,de->te/dot_general | solution.py:738
  227.4 19.2 %all-reduce.6.cloned.1.call-done = f32[128,160]{0,1:T(8,128)} async-done(((f32[128,160]{0,1:T(8,128)}), f32[128,160]{0,1:T(8,128)}) %all-reduce.6.cloned.1.call-update) | async-done | bytes 81936 | tf_op jit(solution)/shard_map/psum | solution.py:706
  250.8 4.1 shard_map.652
  256.7 4.2 shard_map.654
  261.9 22.6 %copy.103 = bf16[2048,2,2048]{0,2,1:T(8,128)(2,1)} copy(bf16[2048,2,2048]{2,0,1:T(8,128)(2,1)} %all-gather.7.cloned.1.call-done) | data formatting | bytes 33554432 | tf_op jit(solution)/shard_map/all_gather | solution.py:681
  284.5 15.8 %all-gather.11.cloned.1.call-done = f32[384,2048]{1,0:T(8,128)} async-done(((f32[24,2048]{1,0:T(8,128)}), f32[384,2048]{1,0:T(8,128)}) %all-gather.11.cloned.1.call-update) | async-done | bytes 3145744 | tf_op jit(solution)/shard_map/all_gather | solution.py:721
  301.6 7.9 %shard_map.653 = (f32[128,2048]{1,0:T(8,128)S(1)}, f32[16,2048]{1,0:T(8,128)S(1)}) custom-call(s32[1]{0:T(128)} %bitcast.place_ref, f32[128,2048]{1,0:T(8,128)S(1)} %get-tuple-element.288.step_ref, f32[128,2048]{1,0:T(8,128)S(1)} %get-tuple-element.287.value_ref.drive_ref, f32[128,16,128]{2,1,0:T(8,128)S(1)} %broadcast_in_dim.27.lane_ref.enter_ref, ...), custom_call_target="tpu_custom_call" | custom-call | tf_op jit(solution)/shard_map/pallas_call | solution.py:140
  310.5 36.6 %all-gather.13.cloned.1.call-done = f32[384,2048]{1,0:T(8,128)} async-done(((f32[24,2048]{1,0:T(8,128)}), f32[384,2048]{1,0:T(8,128)}) %all-gather.13.cloned.1.call-update) | async-done | bytes 3145744 | tf_op jit(solution)/shard_map/all_gather | solution.py:743
  347.1 18.7 %shard_map.655 = (f32[128,2048]{1,0:T(8,128)S(1)}, f32[128,2048]{1,0:T(8,128)S(1)}, f32[16,2048]{1,0:T(8,128)S(1)}, f32[128,16,128]{2,1,0:T(8,128)S(1)}, f32[128,16,128]{2,1,0:T(8,128)S(1)}) custom-call(s32[1]{0:T(128)} %bitcast.place_ref, f32[128,2048]{1,0:T(8,128)S(1)} %get-tuple-element.288.step_ref, f32[128,2048]{1,0:T(8,128)} %copy-done, ...), custom_call_target="tpu_custom_call" | custom-call | tf_op jit(solution)/shard_map/pallas_call | solution.py:236
  373.7 9.2 %psum.15 = bf16[128,160]{0,1:T(8,128)(2,1)S(1)} all-reduce(f32[128,160]{0,1:T(8,128)S(1)} %pad_maximum_fusion.2), channel_id=1, replica_groups=mesh['seq'=16,'tp'=2] {'tp'}, use_global_device_ids=true, to_apply=%region_5.6 | all-reduce | flops 20480 | bytes 122880 | tf_op jit(solution)/shard_map/psum | solution.py:760
  383.0 5.2 multiply_reduce_fusion.10
  396.8 7.1 convolution_convert_fusion.1
  404.2 5.6 convert_bitcast_fusion
  409.8 12.3 %copy.111 = bf16[2048,2048]{1,0:T(8,128)(2,1)} copy(bf16[2048,2048]{0,1:T(8,128)(2,1)} %convert_bitcast_fusion) | data formatting | bytes 16777216
  430.1 4.8 concatenate.35
  438.2 179.2 %shard_map.656 = (f32[128,4096]{1,0:T(8,128)}, bf16[4,2,2,128,384]{4,3,2,1,0:T(8,128)(2,1)S(1)}) custom-call(bf16[16,128,128]{2,1,0:T(8,128)(2,1)S(1)} %bitcast.107, bf16[128,4096]{1,0:T(8,128)(2,1)S(1)} %pad_maximum_fusion.1.grads_ref, bf16[8,2,128,384]{3,2,1,0:T(8,128)(2,1)S(1)} %bitcast.106), custom_call_target="tpu_custom_call" | custom-call | tf_op jit(solution)/shard_map/pallas_call | solution.py:577
  621.8 4.2 reshape.298
  649.5 16.2 %shard_map.657 = (f32[80,128]{1,0:T(8,128)}, f32[8,128]{1,0:T(8,128)}) custom-call(f32[80,128]{1,0:T(8,128)} %constant_dynamic-update-slice_fusion.mine_ref, f32[8,128]{1,0:T(8,128)} %fusion.42.pair_ref), custom_call_target="tpu_custom_call" | custom-call | tf_op jit(solution)/shard_map/pallas_call | solution.py:352
  692.5 13.7 %shard_map.658 = (f32[24,128]{1,0:T(8,128)}, f32[8,128]{1,0:T(8,128)}) custom-call(f32[24,128]{1,0:T(8,128)} %concatenate.39.mine_ref, f32[8,128]{1,0:T(8,128)} %broadcast_in_dim.31.pair_ref), custom_call_target="tpu_custom_call" | custom-call | tf_op jit(solution)/shard_map/pallas_call | solution.py:352
  725.9 5.4 fusion.54
  (343 shorter events, 107.0 us)
Async XLA Ops:
  7.2 133.6 %all-gather.7.cloned.1.call-start = ((), (), s32[]{:S(2)}) async-start(), calls=%async_computation.3 | async-start | bytes 17825792 | tf_op jit(solution)/shard_map/all_gather | solution.py:681
  11.1 205.7 %all-gather.9.cloned.1.call-start = ((), (), s32[]{:S(2)}) async-start(), calls=%async_computation.5 | async-start | bytes 8912896 | tf_op jit(solution)/shard_map/all_gather | solution.py:682
  12.0 234.5 %all-reduce.6.cloned.1.call-start = ((), (), s32[]{:S(2)}) async-start(), calls=%async_computation.4 | async-start | bytes 163840 | tf_op jit(solution)/shard_map/psum | solution.py:706
  22.5 126.4 %copy-start.19 = (bf16[128,2048]{1,0:T(8,128)(2,1)}, bf16[128,2048]{1,0:T(8,128)(2,1)S(1)}, u32[]{:S(2)}) copy-start(bf16[128,2048]{1,0:T(8,128)(2,1)S(1)} %all_gather.23) | copy-start | bytes 1572868
  23.2 193.6 %copy-start.93 = (f32[128]{0:T(128)}, f32[128]{0:T(128)S(1)}, u32[]{:S(2)}) copy-start(f32[128]{0:T(128)S(1)} %get-tuple-element.314) | copy-start | bytes 1540
  23.2 193.6 %copy-start.95 = (f32[128]{0:T(128)}, f32[128]{0:T(128)S(1)}, u32[]{:S(2)}) copy-start(f32[128]{0:T(128)S(1)} %get-tuple-element.315) | copy-start | bytes 1540
  23.2 193.6 %copy-start.97 = (f32[128]{0:T(128)}, f32[128]{0:T(128)S(1)}, u32[]{:S(2)}) copy-start(f32[128]{0:T(128)S(1)} %get-tuple-element.317) | copy-start | bytes 1540
  23.3 193.6 %copy-start.54 = (f32[1,2048]{1,0:T(1,128)}, f32[1,2048]{1,0:T(1,128)S(1)}, u32[]{:S(2)}) copy-start(f32[1,2048]{1,0:T(1,128)S(1)} %get-tuple-element.297) | copy-start | bytes 24580
  23.3 193.5 %copy-start.56 = (f32[1,2048]{1,0:T(1,128)}, f32[1,2048]{1,0:T(1,128)S(1)}, u32[]{:S(2)}) copy-start(f32[1,2048]{1,0:T(1,128)S(1)} %get-tuple-element.298) | copy-start | bytes 24580
  23.3 193.5 %copy-start.58 = (f32[1,2048]{1,0:T(1,128)}, f32[1,2048]{1,0:T(1,128)S(1)}, u32[]{:S(2)}) copy-start(f32[1,2048]{1,0:T(1,128)S(1)} %get-tuple-element.299) | copy-start | bytes 24580
  149.0 77.2 %copy-start.14 = (f32[128,2,2048]{2,0,1:T(8,128)}, f32[128,2,2048]{2,0,1:T(8,128)S(1)}, u32[]{:S(2)}) copy-start(f32[128,2,2048]{2,0,1:T(8,128)S(1)} %get-tuple-element.319) | copy-start | bytes 6291460
  149.0 67.9 %copy-start.29 = (bf16[128,2048]{1,0:T(8,128)(2,1)S(1)}, bf16[128,2048]{1,0:T(8,128)(2,1)}, u32[]{:S(2)}) copy-start(bf16[128,2048]{1,0:T(8,128)(2,1)} %param.30) | copy-start | bytes 1572868
  149.0 67.9 %copy-start.78 = (f32[2048]{0:T(1024)S(1)}, f32[2048]{0:T(1024)}, u32[]{:S(2)}) copy-start(f32[2048]{0:T(1024)} %param.36) | copy-start | bytes 24580
  149.0 3.1 collective-permute-start
  227.3 73.1 %all-gather.11.cloned.1.call-start = ((), (), s32[]{:S(2)}) async-start(), calls=%async_computation.8 | async-start | bytes 3342336 | tf_op jit(solution)/shard_map/all_gather | solution.py:721
  255.0 92.1 %all-gather.13.cloned.1.call-start = ((), (), s32[]{:S(2)}) async-start(), calls=%async_computation.9 | async-start | bytes 3342336 | tf_op jit(solution)/shard_map/all_gather | solution.py:743
  261.9 377.8 %reduce-scatter.8.cloned.1.call-start = ((), (), s32[]{:S(2)}) async-start(), calls=%async_computation.7 | async-start | bytes 1572864 | tf_op jit(solution)/shard_map/reduce_scatter | solution.py:793
  388.2 4.2 collective-permute-start.1
  396.7 244.4 %reduce-scatter.6.cloned.1.call-start = ((), (), s32[]{:S(2)}) async-start(), calls=%async_computation.6 | async-start | bytes 786432 | tf_op jit(solution)/shard_map/reduce_scatter | solution.py:731
  403.9 239.7 %reduce-scatter.10.cloned.1.call-start = ((), (), s32[]{:S(2)}) async-start(), calls=%async_computation.10 | async-start | bytes 8912896
  626.1 98.1 %copy-start.31 = (f32[16,2048]{1,0:T(8,128)}, f32[16,2048]{1,0:T(8,128)S(1)}, u32[]{:S(2)}) copy-start(f32[16,2048]{1,0:T(8,128)S(1)} %get-tuple-element.254) | copy-start | bytes 393220
  638.8 82.5 %copy-start.41 = (f32[2048]{0:T(1024)}, f32[2048]{0:T(1024)S(1)}, u32[]{:S(2)}) copy-start(f32[2048]{0:T(1024)S(1)} %get-tuple-element.326) | copy-start | bytes 24580
  670.2 63.6 %copy-start.64 = (f32[2048]{0:T(1024)}, f32[2048]{0:T(1024)S(1)}, u32[]{:S(2)}) copy-start(f32[2048]{0:T(1024)S(1)} %get-tuple-element.274) | copy-start | bytes 24580
  670.2 63.6 %copy-start.65 = (f32[2048]{0:T(1024)}, f32[2048]{0:T(1024)S(1)}, u32[]{:S(2)}) copy-start(f32[2048]{0:T(1024)S(1)} %get-tuple-element.275) | copy-start | bytes 24580
  (92 other events, 1225.4 us)
Sparse Core Ops, SparseCore 0:
  11.2 129.5 all-gather.6
  143.6 73.2 all-gather.8
  227.4 19.1 all-reduce.5
  255.1 45.1 all-gather.10
  303.0 43.9 all-gather.12
  396.8 18.5 reduce-scatter.7
  418.3 14.5 reduce-scatter.5
  437.0 167.5 reduce-scatter.9

commit v3 on v1

--- a/solution.py
+++ b/solution.py
@@ -1,4 +1,6 @@
 import functools
+from types import SimpleNamespace
+from typing import NamedTuple
 
 import jax
 import jax.numpy as jnp
@@ -12,10 +14,16 @@
 DECAY = 0.5
 CLIP = 0.5
 RATES = (0.45, 0.02, 0.03, 0.1, 0.05, 0.016, 0.09, 1.8, 0.3, 0.45)
+MESH = pl.DeviceIdType.MESH
 LOG2E = 1.4426950408889634
 RESET = 1e9
 TILE = 512
+X_FIRST = (4, 8)
+SHARE_WIDTH = 256
+GATE_EARLY = 1024
+RENEW_TILES = 4
 VMEM_LIMIT = 48 * 1024 * 1024
+FINISH_LIMIT = 63 * 1024 * 1024
 
 
 def passed_along(value, axis, steps):
@@ -29,26 +37,11 @@
     return sigmoid_v * (1.0 + values * (1.0 - sigmoid_v))
 
 
-def widen_last(piece_in, index_of, total_len):
-    zero_block = jnp.zeros(piece_in.shape[:-1] + (total_len,), jnp.float32)
-    return lax.dynamic_update_slice_in_dim(
-        zero_block, piece_in, index_of * piece_in.shape[-1], piece_in.ndim - 1
-    )
-
-
-def narrow(full_array, index_of, size_of):
-    return lax.dynamic_slice_in_dim(full_array, index_of * size_of, size_of, full_array.ndim - 1)
-
-
-def factor_update(full_grad, local_grad, rows_old, cols_old):
-    rows_new = DECAY * rows_old + (1.0 - DECAY) * (
-        jnp.mean(full_grad * full_grad, axis=1) + EPS_FACTOR
-    )
-    cols_new = DECAY * cols_old + (1.0 - DECAY) * (
-        jnp.mean(local_grad * local_grad, axis=0) + EPS_FACTOR
-    )
+def factor_update(grad, row_sums, rows_old, cols_old, channels):
+    rows_new = DECAY * rows_old + (1.0 - DECAY) * (row_sums / channels + EPS_FACTOR)
+    cols_new = DECAY * cols_old + (1.0 - DECAY) * (jnp.mean(grad * grad, axis=0) + EPS_FACTOR)
     scale_sq = rows_new[:, None] * cols_new[None, :] / jnp.mean(rows_new)
-    return (rows_new, cols_new, local_grad * lax.rsqrt(scale_sq))
+    return (rows_new, cols_new, grad * lax.rsqrt(scale_sq))
 
 
 def moment_update(grad_in, moment_old):
@@ -114,24 +107,11 @@
     )(step, value, lane, rate)
 
 
-def entering(pieces_ref, rate, first, count, stride):
-    states = rate.shape[0]
-
-    def join(index, state):
-        at = first + index * stride
-        piece = pieces_ref[at]
-        return jnp.exp2(rate * piece[states : states + 1]) * state + piece[:states]
-
-    return lax.fori_loop(0, count, join, jnp.zeros(rate.shape, jnp.float32))
-
-
 def forward_kernel(
-    place_ref, step_ref, drive_ref, enter_ref, leave_ref, rate_ref, pieces_ref, out_ref, start_ref
+    step_ref, drive_ref, enter_ref, leave_ref, rate_ref, start_ref, out_ref
 ):
     rows, width = step_ref.shape
     rate = rate_ref[...] * LOG2E
-    start = entering(pieces_ref, rate, 0, place_ref[0], 1)
-    start_ref[...] = start
 
     def block(index, state):
         base = pl.multiple_of(index * 8, 8)
@@ -144,39 +124,27 @@
             )
         return state
 
-    lax.fori_loop(0, rows // 8, block, start)
-
-
-def scan_forward(place, step, drive, enter, leave, rate, pieces):
+    lax.fori_loop(0, rows // 8, block, start_ref[...])
+
+
+def scan_forward(step, drive, enter, leave, rate, start):
     rows, width = step.shape
     states = rate.shape[0]
     tile = TILE
+    by_tile = pl.BlockSpec((rows, tile), lambda i: (0, i))
+    by_state = pl.BlockSpec((states, tile), lambda i: (0, i))
+    whole = pl.BlockSpec((rows, states, 128), lambda i: (0, 0, 0))
     return pl.pallas_call(
         forward_kernel,
         grid=(width // tile,),
-        in_specs=[
-            pl.BlockSpec(memory_space=pltpu.SMEM),
-            pl.BlockSpec((rows, tile), lambda i: (0, i)),
-            pl.BlockSpec((rows, tile), lambda i: (0, i)),
-            pl.BlockSpec((rows, states, 128), lambda i: (0, 0, 0)),
-            pl.BlockSpec((rows, states, 128), lambda i: (0, 0, 0)),
-            pl.BlockSpec((states, tile), lambda i: (0, i)),
-            pl.BlockSpec((pieces.shape[0], states + 8, tile), lambda i: (0, 0, i)),
-        ],
-        out_specs=[
-            pl.BlockSpec((rows, tile), lambda i: (0, i)),
-            pl.BlockSpec((states, tile), lambda i: (0, i)),
-        ],
-        out_shape=[
-            jax.ShapeDtypeStruct((rows, width), jnp.float32),
-            jax.ShapeDtypeStruct((states, width), jnp.float32),
-        ],
+        in_specs=[by_tile, by_tile, whole, whole, by_state, by_state],
+        out_specs=by_tile,
+        out_shape=jax.ShapeDtypeStruct((rows, width), jnp.float32),
         compiler_params=pltpu.CompilerParams(vmem_limit_bytes=VMEM_LIMIT),
-    )(place, step, drive, enter, leave, rate, pieces)
+    )(step, drive, enter, leave, rate, start)
 
 
 def backward_kernel(
-    place_ref,
     step_ref,
     drive_ref,
     grad_ref,
@@ -184,7 +152,7 @@
     leave_ref,
     rate_ref,
     start_ref,
-    pieces_ref,
+    follow_ref,
     drive_grad_ref,
     step_grad_ref,
     decay_ref,
@@ -196,7 +164,6 @@
     rows, width = step_ref.shape
     rate_own = rate_ref[...]
     rate = rate_own * LOG2E
-    count = pieces_ref.shape[0]
 
     @pl.when(pl.program_id(0) == 0)
     def _():
@@ -216,7 +183,7 @@
     start = start_ref[...]
     state_ref[0] = start
     lax.fori_loop(0, rows // 8, again, start)
-    follow = entering(pieces_ref, rate, count - 1, count - 1 - place_ref[0], -1)
+    follow = follow_ref[...]
 
     def block(index, carry):
         follow, decay = carry
@@ -240,7 +207,7 @@
     decay_ref[...] = decay * rate_own
 
 
-def scan_backward(place, step, drive, grad, enter, leave, rate, start, pieces):
+def scan_backward(step, drive, grad, enter, leave, rate, start, follow):
     rows, width = step.shape
     states = rate.shape[0]
     tile = TILE
@@ -250,17 +217,7 @@
     return pl.pallas_call(
         backward_kernel,
         grid=(width // tile,),
-        in_specs=[
-            pl.BlockSpec(memory_space=pltpu.SMEM),
-            by_tile,
-            by_tile,
-            by_tile,
-            whole,
-            whole,
-            by_state,
-            by_state,
-            pl.BlockSpec((pieces.shape[0], states + 8, tile), lambda i: (0, 0, i)),
-        ],
+        in_specs=[by_tile, by_tile, by_tile, whole, whole, by_state, by_state, by_state],
         out_specs=[by_tile, by_tile, by_state, whole, whole],
         out_shape=[
             jax.ShapeDtypeStruct((rows, width), jnp.float32),
@@ -274,7 +231,1849 @@
             pltpu.VMEM((rows + 1, states, tile), jnp.float32),
         ],
         compiler_params=pltpu.CompilerParams(vmem_limit_bytes=VMEM_LIMIT),
-    )(place, step, drive, grad, enter, leave, rate, start, pieces)
+    )(step, drive, grad, enter, leave, rate, start, follow)
+
+
+def on_block():
+    return lax.axis_size("seq") == 16 and lax.axis_size("tp") == 2
+
+
+def position():
+    place = lax.axis_index("seq")
+    return lax.div(place, 4), lax.rem(lax.div(place, 2), 2), lax.rem(place, 2)
+
+
+def device(z, x, core):
+    return (z * 4 + x * 2 + core, lax.axis_index("tp"))
+
+
+def other_half():
+    return (lax.axis_index("seq"), 1 - lax.axis_index("tp"))
+
+
+def greet(peers):
+    barrier = pltpu.get_barrier_semaphore()
+    for peer in peers:
+        pl.semaphore_signal(barrier, inc=1, device_id=peer, device_id_type=MESH)
+    pl.semaphore_wait(barrier, len(peers))
+
+
+def remote(source, target, sent, arrived, peer):
+    return pltpu.make_async_remote_copy(
+        src_ref=source,
+        dst_ref=target,
+        send_sem=sent,
+        recv_sem=arrived,
+        device_id=peer,
+        device_id_type=MESH,
+    )
+
+
+def sum_over(seq_part, shared_part, tp_part):
+    return lax.psum(seq_part, "seq"), lax.psum(shared_part, ("seq", "tp")), lax.psum(tp_part, "tp")
+
+
+def project(half, weight, ident):
+    hidden = lax.all_gather(half, "tp", axis=0, tiled=True)
+    full = lax.all_gather(weight, "seq", axis=0, tiled=True)
+    return jnp.dot(hidden, full, preferred_element_type=jnp.float32), hidden, full[None]
+
+
+def pair_kernel(mine_ref, out_ref, far, sent, arrived):
+    greet([other_half()])
+    copy = remote(mine_ref, far, sent, arrived, other_half())
+    copy.start()
+    copy.wait()
+    out_ref[...] = mine_ref[...] + far[...]
+
+
+def pair_sum(value, ident):
+    if not on_block():
+        return lax.psum(value, "tp")
+    vmem = pl.BlockSpec(memory_space=pltpu.VMEM)
+    return pl.pallas_call(
+        pair_kernel,
+        in_specs=[vmem],
+        out_specs=vmem,
+        out_shape=jax.ShapeDtypeStruct(value.shape, value.dtype),
+        scratch_shapes=[
+            pltpu.VMEM(value.shape, value.dtype),
+            pltpu.SemaphoreType.DMA,
+            pltpu.SemaphoreType.DMA,
+        ],
+        compiler_params=pltpu.CompilerParams(collective_id=ident, has_side_effects=True),
+    )(value)
+
+
+def chain_kernel(backward, piece_ref, rate_ref, swap_ref, out_ref, swapped_ref, come, back, sems, swap_sems):
+    place = lax.axis_index("seq")
+    states = rate_ref.shape[0]
+    peers = [(lax.rem(place + step, 16), lax.axis_index("tp")) for step in range(1, 16)]
+    greet(peers + [other_half()])
+    swap = remote(swap_ref, swapped_ref, swap_sems.at[0], swap_sems.at[1], other_half())
+    swap.start()
+
+    def lanes(at):
+        return pl.ds(pl.multiple_of(at * 128, 128), 128)
+
+    def out(at):
+        return remote(
+            piece_ref.at[:, lanes(peers[at][0])],
+            come.at[place],
+            sems.at[0, at],
+            sems.at[1, at],
+            peers[at],
+        )
+
+    def home(at):
+        return remote(
+            back.at[peers[at][0]],
+            out_ref.at[:, lanes(place)],
+            sems.at[2, at],
+            sems.at[3, at],
+            peers[at],
+        )
+
+    for at in range(15):
+        out(at).start()
+    come[place] = piece_ref[:, lanes(place)]
+    rate = rate_ref[:, lanes(place)] * LOG2E
+    for at in range(15):
+        out(at).wait_recv()
+
+    def join(index, state):
+        at = 15 - index if backward else index
+        back[at] = state
+        piece = come[at]
+        return jnp.exp2(rate * piece[states : states + 1]) * state + piece[:states]
+
+    lax.fori_loop(0, 16, join, jnp.zeros((states, 128), jnp.float32))
+    for at in range(15):
+        home(at).start()
+    out_ref[:, lanes(place)] = back[place]
+    for at in range(15):
+        home(at).wait_recv()
+    for at in range(15):
+        out(at).wait_send()
+        home(at).wait_send()
+    swap.wait()
+
+
+def chain(piece, rate, swap, backward, ident):
+    states, width = rate.shape
+    if not on_block():
+        count, place = lax.axis_size("seq"), lax.axis_index("seq")
+        pieces = lax.all_gather(piece, "seq")
+
+        def join(index, state):
+            at = count - 1 - index if backward else index
+            longer = (
+                jnp.exp2(rate * LOG2E * pieces[at, states : states + 1]) * state + pieces[at, :states]
+            )
+            return jnp.where(at > place if backward else at < place, longer, state)
+
+        state = lax.fori_loop(0, count, join, jnp.zeros((states, width), jnp.float32))
+        order = [(0, 1), (1, 0)]
+        return state, lax.ppermute(swap, "tp", order)
+    vmem = pl.BlockSpec(memory_space=pltpu.VMEM)
+    return pl.pallas_call(
+        functools.partial(chain_kernel, backward),
+        in_specs=[vmem, vmem, vmem],
+        out_specs=[vmem, vmem],
+        out_shape=[
+            jax.ShapeDtypeStruct((states, width), jnp.float32),
+            jax.ShapeDtypeStruct(swap.shape, swap.dtype),
+        ],
+        scratch_shapes=[
+            pltpu.VMEM((16, states + 8, 128), jnp.float32),
+            pltpu.VMEM((16, states, 128), jnp.float32),
+            pltpu.SemaphoreType.DMA((4, 15)),
+            pltpu.SemaphoreType.DMA((2,)),
+        ],
+        compiler_params=pltpu.CompilerParams(collective_id=ident, has_side_effects=True),
+    )(piece, rate, swap)
+
+
+def wait_all(copies):
+    for copy in copies:
+        copy.wait_recv()
+
+
+def gathered(refs, *groups):
+    named, at = {}, 0
+    for group in groups:
+        named.update(zip(group._fields, refs[at:]))
+        at += len(group._fields)
+    return SimpleNamespace(**named), list(refs[at:])
+
+
+def shared(source, group):
+    return {name: value for name, value in source._asdict().items() if name in group._fields}
+
+
+class Reducer:
+    def __init__(self, jobs, refs):
+        self.jobs, self.at = jobs, 0
+        self.send, self.come = refs[:3], refs[3:6]
+        self.sent, self.got, self.total = refs[6:9], refs[9:12], refs[12]
+        self.z, self.x, self.core = position()
+        self.chunks, self.width = self.come[2].shape[0], self.come[2].shape[3]
+        self.peers = [
+            [device(self.z, self.x, 1 - self.core)],
+            [device(self.z, 1 - self.x, self.core)],
+            [device(lax.rem(self.z + step, 4), self.x, self.core) for step in (1, 2, 3)],
+        ]
+
+    def copies(self, level, chunk):
+        slot = chunk % self.send[level].shape[0]
+        if level < 2:
+            return [
+                remote(
+                    self.send[level].at[slot],
+                    self.come[level].at[chunk],
+                    self.sent[level].at[chunk],
+                    self.got[level].at[chunk],
+                    self.peers[level][0],
+                )
+            ]
+        return [
+            remote(
+                self.send[2].at[slot, 0, lax.rem(self.z + 1 + at, 4)],
+                self.come[2].at[chunk, at],
+                self.sent[2].at[chunk, at],
+                self.got[2].at[chunk, at],
+                self.peers[2][at],
+            )
+            for at in range(3)
+        ]
+
+    def free(self, level, chunk):
+        older = chunk - self.send[level].shape[0]
+        if older >= 0:
+            for copy in self.copies(level, older):
+                copy.wait_send()
+
+    def product(self, chunk, first, count):
+        left, right, start = self.jobs[chunk][:3]
+        _, rows, depth = left.shape
+        block = left[pl.ds(first, count)].reshape(count * rows, depth)
+        value = jnp.dot(
+            block, right[:, start : start + self.width], preferred_element_type=jnp.float32
+        )
+        return value.reshape(count, rows, self.width)
+
+    def put(self, chunk, value, more):
+        out, start = self.jobs[chunk][3:]
+        here = slice(start, start + self.width)
+        out[:, here] = out[:, here] + value if more else value
+
+    def after_core(self, chunk, x):
+        come = self.come[0][chunk, x].astype(jnp.float32)
+        return self.product(chunk, self.core * 8 + x * 4, 4) + come
+
+    def fill(self, level, chunk, values):
+        self.free(level, chunk)
+        slot = chunk % self.send[level].shape[0]
+        for at, value in enumerate(values):
+            self.send[level][slot, at] = value().astype(jnp.bfloat16)
+        for copy in self.copies(level, chunk):
+            copy.start()
+
+    def stage(self, level, chunk):
+        if not 0 <= chunk < self.chunks:
+            return
+        if level > 0:
+            wait_all(self.copies(level - 1, chunk))
+        if level == 0:
+            away = (1 - self.core) * 8
+            self.fill(
+                0, chunk, [lambda at=at: self.product(chunk, away + at * 4, 4) for at in range(2)]
+            )
+        elif level == 1:
+            self.fill(1, chunk, [lambda: self.after_core(chunk, 1 - self.x)])
+        elif level == 2:
+            come = self.come[1][chunk, 0].astype(jnp.float32)
+            self.total[...] = self.after_core(chunk, self.x) + come
+            self.fill(2, chunk, [lambda: self.total[...]])
+            self.put(chunk, self.total[self.z], False)
+        else:
+            come = [self.come[2][chunk, at].astype(jnp.float32) for at in range(3)]
+            self.put(chunk, (come[0] + come[1]) + come[2], True)
+
+    def step(self, step):
+        for level, lag in enumerate((0, 1, 3, 5)):
+            self.stage(level, step - lag)
+
+    def advance(self, count=1):
+        for _ in range(count):
+            if self.at < self.chunks + 5:
+                self.step(self.at)
+                self.at += 1
+
+    def drain(self):
+        for level in range(3):
+            for chunk in range(max(0, self.chunks - self.send[level].shape[0]), self.chunks):
+                for copy in self.copies(level, chunk):
+                    copy.wait_send()
+
+
+def reducer_scratch(columns, share, width):
+    chunks = columns // width
+    low, dma = jnp.bfloat16, pltpu.SemaphoreType.DMA
+    return [
+        pltpu.VMEM((4, 2, 4, share, width), low),
+        pltpu.VMEM((4, 1, 4, share, width), low),
+        pltpu.VMEM((4, 1, 4, share, width), low),
+        pltpu.VMEM((chunks, 2, 4, share, width), low),
+        pltpu.VMEM((chunks, 1, 4, share, width), low),
+        pltpu.VMEM((chunks, 3, share, width), low),
+        dma((chunks,)),
+        dma((chunks,)),
+        dma((chunks, 3)),
+        dma((chunks,)),
+        dma((chunks,)),
+        dma((chunks, 3)),
+        pltpu.VMEM((4, share, width), jnp.float32),
+    ]
+
+
+def rows_to_lanes(partial):
+    return jnp.sum(partial.T, axis=0, keepdims=True)
+
+
+def lanes_to_rows(row):
+    return jnp.broadcast_to(row, (128, 128)).T
+
+
+class FinishIn(NamedTuple):
+    hidden_t: object
+    d_value: object
+    d_gate: object
+    gate_grad: object
+    extra: object
+    weights: object
+    block: object
+    cot: object
+    lanes: object
+    out_grad: object
+    norm_gain: object
+    norm_moment: object
+    in_cols: object
+    out_cols: object
+    step_cols: object
+    select_cols: object
+    decay_cols: object
+    conv_cols: object
+    bias_moment: object
+    step_moment: object
+    skip_moment: object
+    conv_bias: object
+    step_bias: object
+    skip_gain: object
+
+
+class FinishOut(NamedTuple):
+    in_grad: object
+    input_grad: object
+    small: object
+    scales: object
+    lanes_new: object
+    vectors_new: object
+
+
+class FinishWork(NamedTuple):
+    come_core: object
+    send_x: object
+    come_x: object
+    send_z: object
+    come_z: object
+    full: object
+    mine: object
+    acc: object
+    far: object
+    pair: object
+    pair_far: object
+    totals: object
+    totals_acc: object
+    totals_far: object
+    come_half: object
+    d_hidden: object
+    held: object
+    held_sems: object
+    extra_sent: object
+    extra_got: object
+    sums_sent: object
+    sums_got: object
+    half_sems: object
+
+
+def finish_kernel(channels, model, *refs):
+    r, rest = gathered(refs, FinishIn, FinishOut, FinishWork)
+    z, x, core = position()
+    place, tp = lax.axis_index("seq"), lax.axis_index("tp")
+    core_peer, x_peer = device(z, x, 1 - core), device(z, 1 - x, core)
+    z_peers = [device(lax.rem(z + step, 4), x, core) for step in (1, 2, 3)]
+    others = [
+        (lax.rem(z + step, 4) * 4 + x * 2 + core, 1 - lax.axis_index("tp")) for step in range(4)
+    ]
+    greet([core_peer, x_peer, device(z, 1 - x, 1 - core)] + z_peers + others)
+    low = jnp.bfloat16
+    half_rows = r.block.shape[0]
+    own_half = pl.ds(pl.multiple_of(tp * half_rows, half_rows), half_rows)
+    far_half = pl.ds(pl.multiple_of((1 - tp) * half_rows, half_rows), half_rows)
+    d_hidden = r.d_hidden
+    swap = remote(
+        d_hidden.at[far_half], r.come_half, r.half_sems.at[0], r.half_sems.at[1], other_half()
+    )
+    sides = [r.d_value, r.d_gate]
+    inner = r.out_grad.shape[1]
+    early = r.gate_grad.shape[1]
+    r.in_grad[:, inner : inner + early] = r.gate_grad[...]
+    main = Reducer(
+        [(r.hidden_t, r.d_value, at, r.in_grad, at) for at in range(0, inner, SHARE_WIDTH)]
+        + [(r.hidden_t, r.d_gate, at, r.in_grad, inner + at) for at in range(early, inner, SHARE_WIDTH)],
+        rest,
+    )
+
+    kept_chunks, _, kept_width = r.weights.shape
+
+    def fetch(chunk):
+        return pltpu.make_async_copy(
+            r.weights.at[chunk], r.held.at[chunk % 2], r.held_sems.at[chunk]
+        )
+
+    def hidden_stage(chunk):
+        fetch(chunk).wait()
+        per_side = kept_chunks // 2
+        at = chunk % per_side
+        part = lax.dot_general(
+            sides[chunk // per_side][:, at * kept_width : (at + 1) * kept_width],
+            r.held[chunk % 2],
+            (((1,), (1,)), ((), ())),
+            preferred_element_type=jnp.float32,
+        )
+        d_hidden[...] = part if chunk == 0 else d_hidden[...] + part
+        if chunk + 2 < kept_chunks:
+            fetch(chunk + 2).start()
+        if chunk == kept_chunks - 1:
+            swap.start()
+
+    fetch(0).start()
+    fetch(1).start()
+
+    sent, got = r.extra_sent, r.extra_got
+    extra, full = r.extra, r.full
+    extra_core = remote(extra.at[:, 1 - core], r.come_core, sent.at[0], got.at[0], core_peer)
+    extra_x = remote(r.send_x, r.come_x, sent.at[1], got.at[1], x_peer)
+    extra_z = [
+        remote(r.send_z.at[at], r.come_z.at[at], sent.at[2 + at], got.at[2 + at], z_peers[at])
+        for at in range(3)
+    ]
+    own, held, halves = full.at[z, x, core], full.at[:, x, core], full.at[:, :, core]
+    back_z = [remote(own, own, sent.at[5 + at], got.at[5 + at], z_peers[at]) for at in range(3)]
+    back_x = remote(held, held, sent.at[8], got.at[8], x_peer)
+    back_core = remote(halves, halves, sent.at[9], got.at[9], core_peer)
+
+    def extra_after_core(pair):
+        return extra[pair, core].astype(jnp.float32) + r.come_core[pair].astype(jnp.float32)
+
+    def extra_after_x(level):
+        return extra_after_core(level * 2 + x) + r.come_x[level].astype(jnp.float32)
+
+    def extra_stage_x():
+        extra_core.wait_recv()
+
+        def one(level, _):
+            r.send_x[level] = extra_after_core(level * 2 + 1 - x).astype(low)
+            return 0
+
+        lax.fori_loop(0, 4, one, 0)
+        extra_x.start()
+
+    def extra_stage_z():
+        extra_x.wait_recv()
+
+        def one(at, _):
+            r.send_z[at] = extra_after_x(lax.rem(z + 1 + at, 4)).astype(low)
+            return 0
+
+        lax.fori_loop(0, 3, one, 0)
+        for copy in extra_z:
+            copy.start()
+
+    def extra_stage_last():
+        wait_all(extra_z)
+        total = extra_after_x(z)
+        for at in range(3):
+            total = total + r.come_z[at].astype(jnp.float32)
+        full[z, x, core] = total.astype(low)
+        for copy in back_z:
+            copy.start()
+
+    def extra_back_x():
+        wait_all(back_z)
+        back_x.start()
+
+    def extra_back_core():
+        back_x.wait_recv()
+        back_core.start()
+
+    mine = r.mine
+    vectors_new = r.vectors_new
+
+    def line(ref):
+        return ref[...].reshape(1, -1)
+
+    in_tiles, out_tiles = r.in_grad.shape[1] // 128, r.out_grad.shape[1] // 128
+    seq_rows = in_tiles + out_tiles
+    gain_tiles = model // 128
+
+    def put(base, row):
+        for at in range(row.shape[1] // 128):
+            mine[base + at : base + at + 1, :] = row[:, at * 128 : (at + 1) * 128]
+
+    def take(ref, base, tiles):
+        return jnp.concatenate([ref[base + at : base + at + 1, :] for at in range(tiles)], axis=1)
+
+    def residual_stage():
+        swap.wait()
+        total = d_hidden[own_half, :] + r.come_half[...]
+        residual = r.block[...].astype(jnp.float32)
+        inv_rms = lax.rsqrt(jnp.mean(residual * residual, axis=1, keepdims=True) + EPS_NORM)
+        normed = residual * inv_rms
+        put(seq_rows, jnp.sum(total * normed, axis=0, keepdims=True))
+        scaled = total * line(r.norm_gain)
+        mean = jnp.mean(scaled * normed, axis=1, keepdims=True)
+        r.input_grad[...] = r.cot[own_half, :].astype(jnp.float32) + inv_rms * (scaled - normed * mean)
+
+    span = 512
+    wide_span = span // 128
+    small = r.small
+    groups = {"step": (0, 128), "select": (128, 288), "decay": (288, 304), "conv": (304, 308)}
+    pair = r.pair
+
+    def put_rows(at, partial):
+        pair[at : at + 1, :] = rows_to_lanes(partial)
+
+    def fold_square(value):
+        return fold_lanes(value * value)
+
+    def small_stage():
+        back_core.wait_recv()
+        for block in range(16):
+            small[:, block * 128 : (block + 1) * 128] = full[
+                block // 4, block // 2 % 2, block % 2
+            ].astype(jnp.float32)
+        for at in range(3):
+            rows = min(128, small.shape[0] - at * 128)
+
+            def one(index, partial):
+                columns = pl.ds(pl.multiple_of(index * span, span), span)
+                return partial + fold_square(small[at * 128 : at * 128 + rows, columns])
+
+            partial = lax.fori_loop(
+                0, small.shape[1] // span, one, jnp.zeros((rows, 128), jnp.float32)
+            )
+            if rows < 128:
+                partial = jnp.concatenate(
+                    [partial, jnp.zeros((128 - rows, 128), jnp.float32)], axis=0
+                )
+            put_rows(at, partial)
+
+    def column_sums(ref, base):
+        def one(index, partial):
+            columns = pl.ds(pl.multiple_of(index * span, span), span)
+            value = ref[:, columns]
+            sums = jnp.sum(value * value, axis=0, keepdims=True)
+            for at in range(wide_span):
+                mine[pl.ds(base + index * wide_span + at, 1), :] = sums[:, at * 128 : (at + 1) * 128]
+            return partial + fold_square(value)
+
+        return lax.fori_loop(
+            0, ref.shape[1] // span, one, jnp.zeros((ref.shape[0], 128), jnp.float32)
+        )
+
+    def out_stage():
+        put_rows(4, column_sums(r.out_grad, in_tiles))
+
+    pair[...] = jnp.zeros(pair.shape, jnp.float32)
+    extra_core.start()
+    extra_steps = {1: extra_stage_x, 3: extra_stage_z, 5: extra_stage_last, 7: extra_back_x, 9: extra_back_core}
+    extra_steps.update({14: residual_stage, 12: out_stage, 11: small_stage})
+    for step in range(max(main.chunks + 5, 16)):
+        main.advance()
+        if step < kept_chunks:
+            hidden_stage(step)
+        if step in extra_steps:
+            extra_steps[step]()
+    put_rows(3, column_sums(r.in_grad, 0))
+
+    lanes = r.lanes
+    row_at = lax.broadcasted_iota(jnp.int32, lanes.shape, 0)
+    lane_at = lax.broadcasted_iota(jnp.int32, lanes.shape, 1)
+    counts = jnp.where(row_at == 3, 2.0 * channels, 1.0 * channels)
+    held_lanes = DECAY * lanes[...] + (1.0 - DECAY) * EPS_FACTOR
+    part = jnp.where(tp == 0, held_lanes, 0.0) + (1.0 - DECAY) * pair[...] / counts
+
+    def total(value):
+        return jnp.sum(jnp.sum(value, axis=1, keepdims=True), axis=0, keepdims=True)
+
+    base = seq_rows + gain_tiles
+    for at in range(2):
+        mean = total(jnp.where(row_at == 3 + at, part, 0.0)) / model
+        mine[base + 8 * at : base + 8 * at + 8, :] = jnp.broadcast_to(mean, (8, 128))
+
+    sums_sent, sums_got = r.sums_sent, r.sums_got
+
+    def hop(at, source, target, peer):
+        return remote(source, target, sums_sent.at[at], sums_got.at[at], peer)
+
+    plane = x * 2 + core
+    mates = [core_peer, x_peer, device(z, 1 - x, 1 - core)]
+    across = [(lax.rem(z + step, 4) * 4 + plane, 1 - tp) for step in range(4)]
+
+    def sum_hops(first, value, acc, far, shared):
+        acc[plane] = value[...]
+        copies = [hop(first + at, acc.at[plane], acc.at[plane], mates[at]) for at in range(3)]
+        for copy in copies:
+            copy.start()
+        for copy in copies:
+            copy.wait()
+        acc[4 + z] = (acc[0] + acc[1]) + (acc[2] + acc[3])
+        part = acc.at[4 + z]
+        copies = [hop(first + 3 + at, part, part, z_peers[at]) for at in range(3)]
+        copies += [
+            hop(first + 6 + at, part.at[shared:], far.at[z], across[at]) for at in range(4)
+        ]
+        for copy in copies:
+            copy.start()
+        for copy in copies:
+            copy.wait()
+        value[...] = (acc[4] + acc[5]) + (acc[6] + acc[7])
+        value[shared:] = value[shared:] + ((far[0] + far[1]) + (far[2] + far[3]))
+
+    pair_copy = hop(20, pair, r.pair_far, other_half())
+    pair_copy.start()
+    sum_hops(0, mine, r.acc, r.far, seq_rows)
+    pair_copy.wait()
+
+    lanes_new = held_lanes + (1.0 - DECAY) * (pair[...] + r.pair_far[...]) / counts
+    r.lanes_new[...] = lanes_new
+    flat = row_at * 128 + lane_at
+    means = jnp.where(row_at == 3, mine[base : base + 8, :], mine[base + 8 : base + 16, :])
+    for low_edge, high_edge in groups.values():
+        member = (flat >= low_edge) & (flat < high_edge)
+        mean = total(jnp.where(member, lanes_new, 0.0)) / (high_edge - low_edge)
+        means = jnp.where(member, mean, means)
+    scale = lax.rsqrt(lanes_new / means)
+    scales = [lanes_to_rows(scale[at : at + 1, :]) for at in range(5)]
+    small_scale = jnp.concatenate(scales[:3], axis=0)
+    in_scale, out_scale = scales[3], scales[4]
+
+    def cols_new(old, sums, count):
+        return DECAY * old + (1.0 - DECAY) * (sums / count + EPS_FACTOR)
+
+    in_cols = cols_new(
+        jnp.concatenate([r.in_cols[0:1, :], r.in_cols[1:2, :]], axis=1), take(mine, 0, in_tiles), model
+    )
+    half = in_cols.shape[1] // 2
+    out_cols = cols_new(line(r.out_cols), take(mine, in_tiles, out_tiles), model)
+    vectors_new[3:4, :] = in_cols[:, :half]
+    vectors_new[4:5, :] = in_cols[:, half:]
+    vectors_new[5:6, :] = out_cols
+
+    def squares(ref, row_scale, first_row):
+        def one(index, partial):
+            columns = pl.ds(pl.multiple_of(index * span, span), span)
+            col = vectors_new[pl.ds(first_row + lax.div(index, half // span), 1), pl.ds(
+                pl.multiple_of(lax.rem(index, half // span) * span, span), span
+            )]
+            return partial + fold_square(ref[:, columns] * wide(row_scale, span) * lax.rsqrt(col))
+
+        return total(
+            lax.fori_loop(0, ref.shape[1] // span, one, jnp.zeros((ref.shape[0], 128), jnp.float32))
+        )
+
+    sums = [squares(r.in_grad, in_scale, 3), squares(r.out_grad, out_scale, 5)]
+    group_cols = {
+        "step": (line(r.step_cols), 8),
+        "select": (line(r.select_cols), 7),
+        "decay": (line(r.decay_cols), 9),
+        "conv": (line(r.conv_cols), 6),
+    }
+    for name, (low_edge, high_edge) in groups.items():
+        old_cols, new_row = group_cols[name]
+        partial = jnp.zeros((high_edge - low_edge, 128), jnp.float32)
+        for at in range(0, small.shape[1], span):
+            columns = slice(at, at + span)
+            value = small[low_edge:high_edge, columns]
+            col = cols_new(
+                old_cols[:, columns],
+                jnp.sum(value * value, axis=0, keepdims=True),
+                high_edge - low_edge,
+            )
+            vectors_new[new_row : new_row + 1, columns] = col
+            row_scale = small_scale[low_edge:high_edge]
+            partial = partial + fold_square(value * wide(row_scale, span) * lax.rsqrt(col))
+        sums.append(total(partial))
+    updates = []
+    for at in range(3):
+        value = small[308 + at : 309 + at, :]
+        old = line((r.bias_moment, r.step_moment, r.skip_moment)[at])
+        moment = DECAY * old + (1.0 - DECAY) * (value * value + EPS_FACTOR)
+        vectors_new[24 + at : 25 + at, :] = moment
+        vectors_new[18 + at : 19 + at, :] = value
+        update = value * lax.rsqrt(moment)
+        updates.append(update)
+        sums.append(jnp.sum(update * update, axis=1, keepdims=True))
+    totals = r.totals
+    for at in range(9):
+        totals[at : at + 1, :] = jnp.broadcast_to(sums[at], (1, 128))
+    totals[9:16, :] = jnp.zeros((7, 128), jnp.float32)
+    sum_hops(10, totals, r.totals_acc, r.totals_far, 0)
+
+    def rate(at, count, step_rate, copies):
+        root = jnp.sqrt(totals[at : at + 1, :] / (copies * count))
+        return step_rate / jnp.maximum(1.0, root / CLIP)
+
+    in_rate = rate(0, 2.0 * channels * model, RATES[1], 1)
+    out_rate = rate(1, 1.0 * channels * model, RATES[2], 1)
+
+    scales_out = r.scales
+    scales_out[3] = in_scale * in_rate
+    scales_out[4] = out_scale * out_rate
+    small_rates = {"step": RATES[6], "select": RATES[5], "decay": RATES[8], "conv": RATES[3]}
+    at_total = {"step": 2, "select": 3, "decay": 4, "conv": 5}
+    row_number = lax.broadcasted_iota(jnp.int32, small_scale.shape, 0)
+    for name, (low_edge, high_edge) in groups.items():
+        step_rate = rate(
+            at_total[name], 1.0 * (high_edge - low_edge) * channels, small_rates[name], 16
+        )
+        member = (row_number >= low_edge) & (row_number < high_edge)
+        small_scale = jnp.where(member, small_scale * step_rate, small_scale)
+    for at in range(3):
+        scales_out[at] = small_scale[at * 128 : (at + 1) * 128, :]
+    for at, step_rate in enumerate((RATES[4], RATES[7], RATES[9])):
+        step_rate = rate(6 + at, 1.0 * channels, step_rate, 16)
+        vectors_new[21 + at : 22 + at, :] = (
+            line((r.conv_bias, r.step_bias, r.skip_gain)[at]) - wide(step_rate, half) * updates[at]
+        )
+    gain_grad = take(mine, seq_rows, gain_tiles)
+    moment = DECAY * line(r.norm_moment) + (1.0 - DECAY) * (gain_grad * gain_grad + EPS_FACTOR)
+    update = gain_grad * lax.rsqrt(moment)
+    root = jnp.sqrt(jnp.mean(update * update, axis=1, keepdims=True))
+    vectors_new[0:1, :] = gain_grad
+    vectors_new[1:2, :] = line(r.norm_gain) - RATES[0] / jnp.maximum(1.0, root / CLIP) * update
+    vectors_new[2:3, :] = moment
+    vectors_new[10:18, :] = jnp.zeros((8, half), jnp.float32)
+    vectors_new[27:32, :] = jnp.zeros((5, half), jnp.float32)
+
+    main.drain()
+    for copy in [extra_core, extra_x] + extra_z + back_z + [back_x, back_core]:
+        copy.wait_send()
+
+
+def finish(ident, channels, given):
+    half_rows, model = given.block.shape
+    share, inner = given.out_grad.shape
+    columns = 2 * inner
+    f32, low = jnp.float32, jnp.bfloat16
+    small_rows = given.extra.shape[2]
+    vmem = pl.BlockSpec(memory_space=pltpu.VMEM)
+    dma = pltpu.SemaphoreType.DMA
+    shape = jax.ShapeDtypeStruct
+    seq_rows = columns // 128 + inner // 128 + model // 128 + 16
+    kept_chunks, _, kept_width = given.weights.shape
+    block = (small_rows, 128)
+    outs = pl.pallas_call(
+        functools.partial(finish_kernel, channels, model),
+        in_specs=[
+            pl.BlockSpec(memory_space=pltpu.HBM) if value is given.weights else vmem for value in given
+        ],
+        out_specs=[vmem] * len(FinishOut._fields),
+        out_shape=[
+            shape((share, columns), f32),
+            shape((half_rows, model), f32),
+            shape((small_rows, inner), f32),
+            shape((5, 128, 128), f32),
+            shape((8, 128), f32),
+            shape((32, inner), f32),
+        ],
+        scratch_shapes=[
+            pltpu.VMEM((8,) + block, low),
+            pltpu.VMEM((4,) + block, low),
+            pltpu.VMEM((4,) + block, low),
+            pltpu.VMEM((3,) + block, low),
+            pltpu.VMEM((3,) + block, low),
+            pltpu.VMEM((4, 2, 2) + block, low),
+            pltpu.VMEM((seq_rows, 128), f32),
+            pltpu.VMEM((8, seq_rows, 128), f32),
+            pltpu.VMEM((4, model // 128 + 16, 128), f32),
+            pltpu.VMEM((8, 128), f32),
+            pltpu.VMEM((8, 128), f32),
+            pltpu.VMEM((16, 128), f32),
+            pltpu.VMEM((8, 16, 128), f32),
+            pltpu.VMEM((4, 16, 128), f32),
+            pltpu.VMEM((half_rows, model), f32),
+            pltpu.VMEM((2 * half_rows, model), f32),
+            pltpu.VMEM((2, model, kept_width), low),
+            dma((kept_chunks,)),
+            dma((10,)),
+            dma((10,)),
+            dma((21,)),
+            dma((21,)),
+            dma((2,)),
+        ]
+        + reducer_scratch(columns - given.gate_grad.shape[1], share, SHARE_WIDTH),
+        compiler_params=pltpu.CompilerParams(
+            collective_id=ident, has_side_effects=True, vmem_limit_bytes=FINISH_LIMIT
+        ),
+    )(*given)
+    return FinishOut(*outs)
+
+
+class RenewIn(NamedTuple):
+    value_grad: object
+    gate_grad: object
+    out_grad: object
+    input_grad: object
+    block_out: object
+    small: object
+    scales: object
+    lanes_new: object
+    vectors_new: object
+    in_weight: object
+    out_weight: object
+    step_weight: object
+    select_weight: object
+    decay_log: object
+    conv_weight: object
+
+
+def renew_kernel(*refs):
+    r, out = gathered(refs, RenewIn)
+    cols, small, scales = r.vectors_new, r.small, r.scales
+    span = small.shape[1]
+
+    def write(*values):
+        for value in values:
+            ref = out.pop(0)
+            ref[...] = value.astype(ref.dtype).reshape(ref.shape)
+
+    def line(at):
+        return cols[at : at + 1, :]
+
+    def rows(low_edge, high_edge):
+        flat = [r.lanes_new[at : at + 1, :] for at in range(5)]
+        return jnp.concatenate(flat, axis=1)[:, low_edge:high_edge]
+
+    def matrix(grad, weight, scale, col):
+        new = weight - grad * wide(scale, span) * lax.rsqrt(line(col))
+        write(grad, new, new)
+
+    write(r.block_out[...], r.input_grad[...], line(0), line(1), line(1), line(2))
+    in_refs = [out.pop(0) for _ in range(3)]
+    for part, grad_ref in enumerate((r.value_grad, r.gate_grad)):
+        grad = grad_ref[...]
+        new = r.in_weight[:, part, :] - grad * wide(scales[3], span) * lax.rsqrt(line(3 + part))
+        for ref, value in zip(in_refs, (grad, new, new)):
+            ref[:, part, :] = value.astype(ref.dtype)
+    write(rows(384, 512), cols[3:5, :])
+    matrix(r.out_grad[...], r.out_weight[...], scales[4], 5)
+    write(rows(512, 640), line(5))
+    small_scale = jnp.concatenate([scales[0], scales[1], scales[2]], axis=0)
+    matrix(small[304:308, :], r.conv_weight[...], small_scale[304:308], 6)
+    write(rows(304, 308), line(6))
+    write(line(18), line(21), line(21), line(24))
+    matrix(small[128:288, :], r.select_weight[...], small_scale[128:288], 7)
+    write(rows(128, 288), line(7))
+    matrix(small[0:128, :], r.step_weight[...], small_scale[0:128], 8)
+    write(rows(0, 128), line(8), line(19), line(22), line(22), line(25))
+    matrix(small[288:304, :], r.decay_log[...], small_scale[288:304], 9)
+    write(rows(288, 304), line(9))
+    write(line(20), line(23), line(23), line(26))
+
+
+def renew(given):
+    f32, low = jnp.float32, jnp.bfloat16
+    inner = given.out_grad.shape[1]
+    shape = jax.ShapeDtypeStruct
+
+    def three(ref):
+        return [shape(ref.shape, f32), shape(ref.shape, f32), shape(ref.shape, low)]
+
+    def vector(count):
+        return shape((count,), f32)
+
+    def trio(count):
+        return [vector(count), vector(count), shape((count,), low)]
+
+    model = given.block_out.shape[1]
+    share = given.out_grad.shape[0]
+    outs = (
+        [shape(given.block_out.shape, f32), shape(given.input_grad.shape, f32)]
+        + trio(model)
+        + [vector(model)]
+        + three(given.in_weight)
+        + [vector(share), shape((2, inner), f32)]
+        + three(given.out_weight)
+        + [vector(share), vector(inner)]
+        + three(given.conv_weight)
+        + [vector(given.conv_weight.shape[0]), vector(inner)]
+        + trio(inner)
+        + [vector(inner)]
+        + three(given.select_weight)
+        + [vector(given.select_weight.shape[0]), vector(inner)]
+        + three(given.step_weight)
+        + [vector(given.step_weight.shape[0]), vector(inner)]
+        + trio(inner)
+        + [vector(inner)]
+        + three(given.decay_log)
+        + [vector(given.decay_log.shape[0]), vector(inner)]
+        + trio(inner)
+        + [vector(inner)]
+    )
+    span = inner // RENEW_TILES
+
+    def by_tile(ref, first=0):
+        *front, last = ref.shape
+        if not front and last != inner:
+            return pl.BlockSpec((last,), lambda i: (0,))
+        zeros = (0,) * len(front)
+        return pl.BlockSpec((*front, span), lambda i: zeros + (first + i,))
+
+    def whole(ref):
+        zeros = (0,) * len(ref.shape)
+        return pl.BlockSpec(ref.shape, lambda i: zeros)
+
+    specs = RenewIn(*[by_tile(ref) for ref in given])
+    specs = specs._replace(
+        gate_grad=by_tile(given.gate_grad, RENEW_TILES),
+        scales=whole(given.scales),
+        lanes_new=whole(given.lanes_new),
+    )
+    return tuple(
+        pl.pallas_call(
+            renew_kernel,
+            grid=(RENEW_TILES,),
+            in_specs=list(specs),
+            out_specs=[by_tile(ref) for ref in outs],
+            out_shape=outs,
+            compiler_params=pltpu.CompilerParams(vmem_limit_bytes=FINISH_LIMIT),
+        )(*given)
+    )
+
+
+class ForwardIn(NamedTuple):
+    in_weight: object
+    out_weight: object
+    block: object
+    cot: object
+    norm_gain: object
+    conv_weight: object
+    conv_bias: object
+    step_bias: object
+    skip_gain: object
+    masks: object
+    select_weight: object
+    step_weight: object
+    decay_log: object
+
+
+class ForwardOut(NamedTuple):
+    hidden_t: object
+    cot_t: object
+    piece: object
+    conv_in: object
+    rim: object
+    conv_pre: object
+    conv_out: object
+    select_out: object
+    step_pre: object
+    step_size: object
+    held: object
+    drive: object
+    enter: object
+    leave: object
+    start: object
+    gated: object
+    d_mixed: object
+    d_gate: object
+    branch: object
+    skip_grad: object
+    weights: object
+
+
+class ForwardWork(NamedTuple):
+    hidden: object
+    full: object
+    ext: object
+    gate: object
+    scanned: object
+    state_piece: object
+    come: object
+    back: object
+    select_far: object
+    z_sent: object
+    z_got: object
+    x_sent: object
+    x_got: object
+    core_sems: object
+    kept: object
+    rim_sems: object
+    chain_sems: object
+    pair_sems: object
+
+
+def forward_block_kernel(*refs):
+    r, _ = gathered(refs, ForwardIn, ForwardOut, ForwardWork)
+    z, x, core = position()
+    place, tp = lax.axis_index("seq"), lax.axis_index("tp")
+    full, hidden = r.full, r.hidden
+
+    def line(ref):
+        return ref[...].reshape(1, -1)
+
+    chunks, width = full.shape[0], full.shape[5]
+    third = chunks // 3
+    low = jnp.bfloat16
+    z_peers = [device(lax.rem(z + step, 4), x, core) for step in (1, 2, 3)]
+    x_peer, core_peer = device(z, 1 - x, core), device(z, x, 1 - core)
+    seq_peers = [(lax.rem(place + step, 16), tp) for step in range(1, 16)]
+    greet(seq_peers + [other_half()])
+
+    def slot(chunk, level):
+        if chunk in X_FIRST:
+            return full.at[chunk, level, :, core]
+        return full.at[chunk, level, x, core]
+
+    def up(chunk, hop):
+        ref = slot(chunk, z - hop)
+        peer = device(z + 1, x, core)
+        return remote(ref, ref, r.z_sent.at[chunk, hop], r.z_got.at[chunk, hop], peer)
+
+    def down(chunk, hop):
+        ref = slot(chunk, z + hop)
+        peer = device(z - 1, x, core)
+        return remote(ref, ref, r.z_sent.at[chunk, 3 + hop], r.z_got.at[chunk, 3 + hop], peer)
+
+    def from_below(chunk, hop):
+        ref = slot(chunk, z - hop)
+        peer = device(z - 1, x, core)
+        return remote(ref, ref, r.z_sent.at[chunk, hop - 1], r.z_got.at[chunk, hop - 1], peer)
+
+    def from_above(chunk, hop):
+        ref = slot(chunk, z + hop)
+        peer = device(z + 1, x, core)
+        return remote(ref, ref, r.z_sent.at[chunk, 2 + hop], r.z_got.at[chunk, 2 + hop], peer)
+
+    def along_x(chunk, level):
+        ref = full.at[chunk, level, x, core]
+        return remote(ref, ref, r.x_sent.at[chunk, level], r.x_got.at[chunk, level], x_peer)
+
+    def along_core(chunk):
+        ref = full.at[chunk, :, :, core]
+        return remote(ref, ref, r.core_sems.at[0, chunk], r.core_sems.at[1, chunk], core_peer)
+
+    def keep(chunk):
+        return pltpu.make_async_copy(full.at[chunk], r.weights.at[chunk], r.kept.at[chunk])
+
+    def columns(at):
+        return slice(at * width, (at + 1) * width)
+
+    def when(condition, action):
+        pl.when(condition)(action)
+
+    def z_start(chunk):
+        when(z < 3, lambda: up(chunk, 0).start())
+        when(z > 0, lambda: down(chunk, 0).start())
+
+    def z_hop(chunk, hop):
+        def below():
+            from_below(chunk, hop).wait_recv()
+            if hop < 3:
+                when(z < 3, lambda: up(chunk, hop).start())
+            if chunk not in X_FIRST:
+                along_x(chunk, z - hop).start()
+
+        def above():
+            from_above(chunk, hop).wait_recv()
+            if hop < 3:
+                when(z > 0, lambda: down(chunk, hop).start())
+            if chunk not in X_FIRST:
+                along_x(chunk, z + hop).start()
+
+        when(z >= hop, below)
+        when(z + hop < 4, above)
+
+    def own_columns(chunk):
+        if chunk < 2 * third:
+            return r.in_weight[:, chunk // third, columns(chunk % third)]
+        return r.out_weight[:, columns(chunk - 2 * third)]
+
+    def ready(step):
+        return 0 <= step < chunks
+
+    def pump(step):
+        for first in [step + 1] if step else range(2):
+            if ready(first):
+                full[first, z, x, core] = own_columns(first).astype(low)
+                along_x(first, z).start()
+                if first not in X_FIRST:
+                    z_start(first)
+        for hop in range(4):
+            chunk = step - 1 - hop
+            if not ready(chunk):
+                continue
+            late = 1 if chunk in X_FIRST else 0
+            if late and hop == 0:
+                along_x(chunk, z).wait_recv()
+                z_start(chunk)
+            elif hop + 1 - late < 4 and hop + 1 - late > 0:
+                z_hop(chunk, hop + 1 - late)
+            if hop == 3:
+                if late == 0:
+                    wait_all([along_x(chunk, level) for level in range(4)])
+                along_core(chunk).start()
+        if ready(step - 5):
+            along_core(step - 5).wait_recv()
+            if step - 5 < 2 * third:
+                keep(step - 5).start()
+
+    def weights(chunk):
+        return full[chunk].reshape(hidden.shape[1], width)
+
+    def dot(left, right):
+        return jnp.dot(left, right, preferred_element_type=jnp.float32)
+
+    def dot_last(left, right):
+        return lax.dot_general(
+            left, right, (((1,), (1,)), ((), ())), preferred_element_type=jnp.float32
+        )
+
+    half_rows = r.block.shape[0]
+    mine = pl.ds(pl.multiple_of(tp * half_rows, half_rows), half_rows)
+    residual = r.block[...].astype(jnp.float32)
+    inv_rms = lax.rsqrt(jnp.mean(residual * residual, axis=1, keepdims=True) + EPS_NORM)
+    hidden[mine] = (residual * inv_rms * line(r.norm_gain)).astype(low)
+    pair_sems = r.pair_sems
+    swap = remote(hidden.at[mine], hidden.at[mine], pair_sems.at[0], pair_sems.at[1], other_half())
+    swap.start()
+
+    rows = hidden.shape[0]
+    conv_in, conv_pre, conv_out, rim, ext = (
+        r.conv_in,
+        r.conv_pre,
+        r.conv_out,
+        r.rim,
+        r.ext,
+    )
+
+    def rim_copy(tile):
+        return remote(
+            conv_in.at[rows - 16 :, columns(tile)],
+            rim.at[:, columns(tile)],
+            r.rim_sems.at[0, tile],
+            r.rim_sems.at[1, tile],
+            seq_peers[0],
+        )
+
+    def value_tile(tile):
+        conv_in[:, columns(tile)] = dot(hidden[...], weights(tile)).astype(low)
+        rim_copy(tile).start()
+
+    masks = r.masks
+    select_out = r.select_out
+
+    def conv_tile(tile):
+        rim_copy(tile).wait_recv()
+        ext[0:8, :] = rim[8:16, columns(tile)].astype(jnp.float32)
+        ext[8:, :] = conv_in[:, columns(tile)].astype(jnp.float32)
+        conv_weight = r.conv_weight
+        total = line(r.conv_bias)[:, columns(tile)] + conv_weight[0:1, columns(tile)] * ext[8:, :]
+        for lag in range(1, 4):
+            total = total + conv_weight[lag : lag + 1, columns(tile)] * (
+                ext[8 - lag : 8 - lag + rows, :] * wide(masks[lag - 1], width)
+            )
+        conv_pre[:, columns(tile)] = total
+        out = (total * jax.nn.sigmoid(total)).astype(low)
+        conv_out[:, columns(tile)] = out
+        select_low = r.select_weight[:, columns(tile)].astype(low)
+        spare = jnp.zeros((select_out.shape[1] - select_low.shape[0], width), low)
+        part = dot_last(out, jnp.concatenate([select_low, spare], axis=0))
+        select_out[...] = part if tile == 0 else select_out[...] + part
+
+    select_swap = remote(
+        select_out, r.select_far, pair_sems.at[2], pair_sems.at[3], other_half()
+    )
+    enter, leave = r.enter, r.leave
+    states = r.decay_log.shape[0]
+    step_rank = r.step_weight.shape[0]
+    held, drive = r.held, r.drive
+
+    def select_stage():
+        select_swap.wait()
+        select_out[...] = select_out[...] + r.select_far[...]
+        turned = select_out[:, step_rank : step_rank + 128].T
+        for at in range(rows):
+            enter[at] = jnp.broadcast_to(turned[:states, at : at + 1], (states, 128))
+            leave[at] = jnp.broadcast_to(turned[states : 2 * states, at : at + 1], (states, 128))
+
+    def step_tile(tile):
+        here = columns(tile)
+        step_low = r.step_weight[:, here].astype(low)
+        pre = dot(select_out[:, :step_rank].astype(low), step_low) + line(r.step_bias)[:, here]
+        size = jnp.maximum(pre, 0.0) + jnp.log1p(jnp.exp(-jnp.abs(pre)))
+        r.step_pre[:, here] = pre
+        r.step_size[:, here] = size
+        held[:, here] = jnp.where(wide(masks[0], width) > 0.0, size, RESET)
+        drive[:, here] = size * conv_out[:, here].astype(jnp.float32)
+
+    piece = r.state_piece
+
+    def rate_of(here):
+        return -jnp.exp(r.decay_log[:, here]) * LOG2E
+
+    def state_tile(tile):
+        here = columns(tile)
+        rate = rate_of(here)
+
+        def block(index, state):
+            base = pl.multiple_of(index * 8, 8)
+            for offset in range(8):
+                at = base + offset
+                kept = jnp.exp2(rate * held[pl.ds(at, 1), here])
+                state = kept * state + wide(enter[at], width) * drive[pl.ds(at, 1), here]
+            return state
+
+        piece[0:states, here] = lax.fori_loop(
+            0, rows // 8, block, jnp.zeros((states, width), jnp.float32)
+        )
+        total = jnp.sum(held[:, here], axis=0, keepdims=True)
+        piece[states:, here] = jnp.broadcast_to(total, (8, width))
+
+    chain_out, chain_home, chain_middle, chain_end = chain_parts(
+        False, piece, lambda: rate_of(own_lanes(place)), r.start, r.come, r.back, r.chain_sems
+    )
+    scanned, start = r.scanned, r.start
+
+    def scan_tile(tile):
+        here = columns(tile)
+        rate = rate_of(here)
+
+        def block(index, state):
+            base = pl.multiple_of(index * 8, 8)
+            for offset in range(8):
+                at = base + offset
+                kept = jnp.exp2(rate * held[pl.ds(at, 1), here])
+                state = kept * state + wide(enter[at], width) * drive[pl.ds(at, 1), here]
+                scanned[pl.ds(at, 1), here] = jnp.sum(
+                    wide(leave[at], width) * state, axis=0, keepdims=True
+                )
+            return state
+
+        lax.fori_loop(0, rows // 8, block, start[:, here])
+
+    gate = r.gate
+
+    def gate_tile(tile):
+        gate[:, columns(tile)] = dot(hidden[...], weights(third + tile))
+
+    def out_tile(tile):
+        here = columns(tile)
+        out_weight = weights(2 * third + tile)
+        value = conv_out[:, here].astype(jnp.float32)
+        mixed = scanned[:, here] + line(r.skip_gain)[:, here] * value
+        pre = gate[:, here]
+        sigmoid = jax.nn.sigmoid(pre)
+        act = pre * sigmoid
+        gated = (mixed * act).astype(low)
+        r.gated[:, here] = gated
+        d_gated = dot(r.cot[...], out_weight)
+        d_mixed = d_gated * act
+        r.d_mixed[:, here] = d_mixed
+        slope = sigmoid * (1.0 + pre * (1.0 - sigmoid))
+        r.d_gate[:, here] = (d_gated * mixed * slope).astype(low)
+        r.skip_grad[:, here] = jnp.sum(d_mixed * value, axis=0, keepdims=True)
+        part = dot_last(gated, out_weight)
+        r.branch[...] = part if tile == 0 else r.branch[...] + part
+
+    def adjoint_tile(tile):
+        here = columns(tile)
+        rate = rate_of(here)
+
+        def block(index, state):
+            base = pl.multiple_of((rows // 8 - 1 - index) * 8, 8)
+            for offset in range(7, -1, -1):
+                at = base + offset
+                kept = jnp.exp2(rate * held[pl.ds(at, 1), here])
+                state = kept * (state + wide(leave[at], width) * r.d_mixed[pl.ds(at, 1), here])
+            return state
+
+        r.piece[0:states, here] = lax.fori_loop(
+            0, rows // 8, block, jnp.zeros((states, width), jnp.float32)
+        )
+        total = jnp.sum(held[:, here], axis=0, keepdims=True)
+        r.piece[states:, here] = jnp.broadcast_to(total, (8, width))
+
+    def turn(source, target):
+        for at in range(target.shape[0]):
+            value = source[:, at * 128 : (at + 1) * 128].astype(jnp.float32)
+            target[at % 2 * 8 + at // 2 % 2 * 4 + at // 4] = value.T.astype(low)
+
+    for step in range(third + 5):
+        pump(step)
+        if step == 0:
+            turn(r.cot, r.cot_t)
+        if step == 2:
+            swap.wait()
+            turn(hidden, r.hidden_t)
+        if step >= 5:
+            value_tile(step - 5)
+        if step >= 6:
+            conv_tile(step - 6)
+    conv_tile(third - 1)
+    select_swap.start()
+    pump(third + 5)
+    gate_tile(0)
+    select_stage()
+    for tile in range(third):
+        step_tile(tile)
+    pump(third + 6)
+    gate_tile(1)
+    for tile in range(third):
+        state_tile(tile)
+    chain_out()
+    chain_middle()
+    pump(third + 7)
+    gate_tile(2)
+    chain_home()
+    for tile in range(third):
+        scan_tile(tile)
+    pump(third + 8)
+    gate_tile(3)
+    for tile in range(third):
+        pump(2 * third + 5 + tile)
+        out_tile(tile)
+        adjoint_tile(tile)
+    chain_end()
+    for chunk in range(chunks):
+        for hop in range(3):
+            when((z < 3) & (z >= hop), up(chunk, hop).wait_send)
+            when((z > 0) & (z + hop < 4), down(chunk, hop).wait_send)
+        for level in range(4):
+            if chunk not in X_FIRST:
+                along_x(chunk, level).wait_send()
+        if chunk in X_FIRST:
+            along_x(chunk, z).wait_send()
+        along_core(chunk).wait_send()
+        if chunk < 2 * third:
+            keep(chunk).wait()
+    for tile in range(third):
+        rim_copy(tile).wait_send()
+
+
+def own_lanes(at):
+    return pl.ds(pl.multiple_of(at * 128, 128), 128)
+
+
+def chain_parts(backward, piece, rate_own, out, come, back, sems):
+    place = lax.axis_index("seq")
+    peers = [(lax.rem(place + step, 16), lax.axis_index("tp")) for step in range(1, 16)]
+    states = out.shape[0]
+
+    def away(at):
+        return remote(
+            piece.at[:, own_lanes(peers[at][0])],
+            come.at[place],
+            sems.at[0, at],
+            sems.at[1, at],
+            peers[at],
+        )
+
+    def home(at):
+        return remote(
+            back.at[peers[at][0]],
+            out.at[:, own_lanes(place)],
+            sems.at[2, at],
+            sems.at[3, at],
+            peers[at],
+        )
+
+    def begin():
+        for at in range(15):
+            away(at).start()
+        come[place] = piece[:, own_lanes(place)]
+
+    def middle():
+        rate = rate_own()
+        for at in range(15):
+            away(at).wait_recv()
+
+        def join(index, state):
+            at = 15 - index if backward else index
+            back[at] = state
+            part = come[at]
+            return jnp.exp2(rate * part[states : states + 1]) * state + part[:states]
+
+        lax.fori_loop(0, 16, join, jnp.zeros((states, 128), jnp.float32))
+        for at in range(15):
+            home(at).start()
+        out[:, own_lanes(place)] = back[place]
+
+    def arrive():
+        for at in range(15):
+            home(at).wait_recv()
+
+    def end():
+        for at in range(15):
+            away(at).wait_send()
+            home(at).wait_send()
+
+    return begin, arrive, middle, end
+
+
+def forward_block(ident, given):
+    half_rows, model = given.block.shape
+    rows = 2 * half_rows
+    share, inner = given.out_weight.shape
+    total = 3 * inner
+    states = given.decay_log.shape[0]
+    f32, low = jnp.float32, jnp.bfloat16
+    vmem = pl.BlockSpec(memory_space=pltpu.VMEM)
+    dma = pltpu.SemaphoreType.DMA
+    width = 512
+    chunks = total // width
+    select_rows = 256
+
+    def like(columns, dtype):
+        return jax.ShapeDtypeStruct((rows, columns), dtype)
+
+    lanes = jax.ShapeDtypeStruct((rows, states, 128), f32)
+    outs = pl.pallas_call(
+        forward_block_kernel,
+        in_specs=[vmem] * len(ForwardIn._fields),
+        out_specs=[vmem] * (len(ForwardOut._fields) - 1) + [pl.BlockSpec(memory_space=pltpu.HBM)],
+        out_shape=[
+            jax.ShapeDtypeStruct((16, share, rows), low),
+            jax.ShapeDtypeStruct((16, share, rows), low),
+            jax.ShapeDtypeStruct((states + 8, inner), f32),
+            like(inner, low),
+            jax.ShapeDtypeStruct((16, inner), low),
+            like(inner, f32),
+            like(inner, low),
+            like(select_rows, f32),
+            like(inner, f32),
+            like(inner, f32),
+            like(inner, f32),
+            like(inner, f32),
+            lanes,
+            lanes,
+            jax.ShapeDtypeStruct((states, inner), f32),
+            like(inner, low),
+            like(inner, f32),
+            like(inner, low),
+            like(model, f32),
+            jax.ShapeDtypeStruct((1, inner), f32),
+            jax.ShapeDtypeStruct((chunks * 2 // 3, 4, 2, 2, share, width), low),
+        ],
+        scratch_shapes=[
+            pltpu.VMEM((rows, model), low),
+            pltpu.VMEM((chunks, 4, 2, 2, share, width), low),
+            pltpu.VMEM((rows + 8, width), f32),
+            pltpu.VMEM((rows, inner), f32),
+            pltpu.VMEM((rows, inner), f32),
+            pltpu.VMEM((states + 8, inner), f32),
+            pltpu.VMEM((16, states + 8, 128), f32),
+            pltpu.VMEM((16, states, 128), f32),
+            pltpu.VMEM((rows, select_rows), f32),
+            dma((chunks, 6)),
+            dma((chunks, 6)),
+            dma((chunks, 4)),
+            dma((chunks, 4)),
+            dma((2, chunks)),
+            dma((chunks,)),
+            dma((2, chunks // 3)),
+            dma((4, 15)),
+            dma((4,)),
+        ],
+        compiler_params=pltpu.CompilerParams(
+            collective_id=ident, has_side_effects=True, vmem_limit_bytes=FINISH_LIMIT
+        ),
+    )(*given)
+    out = ForwardOut(*outs)
+    return out._replace(weights=out.weights.reshape(-1, model, width))
+
+
+class BackwardIn(NamedTuple):
+    hidden_t: object
+    cot_t: object
+    gated: object
+    d_gate: object
+    piece: object
+    d_mixed: object
+    held: object
+    drive: object
+    enter: object
+    leave: object
+    start: object
+    conv_out: object
+    step_pre: object
+    step_size: object
+    conv_pre: object
+    conv_in: object
+    rim: object
+    select_out: object
+    branch: object
+    block: object
+    skip_grad: object
+    masks: object
+    masks_after: object
+    conv_weight: object
+    skip_gain: object
+    select_weight: object
+    step_weight: object
+    decay_log: object
+
+
+class BackwardOut(NamedTuple):
+    out_grad: object
+    gate_grad: object
+    block_out: object
+    d_value: object
+    extra: object
+
+
+class BackwardWork(NamedTuple):
+    come: object
+    back: object
+    follow: object
+    kept: object
+    state: object
+    drive_grad: object
+    d_step_pre: object
+    decay_grad: object
+    enter_grad: object
+    leave_grad: object
+    select_grad: object
+    select_far: object
+    conv_grad: object
+    rim_next: object
+    ext: object
+    branch_send: object
+    branch_far: object
+    chain_sems: object
+    pair_sems: object
+    rim_sems: object
+
+
+def backward_block_kernel(*refs):
+    r, rest = gathered(refs, BackwardIn, BackwardOut, BackwardWork)
+    z, x, core = position()
+    place, tp = lax.axis_index("seq"), lax.axis_index("tp")
+    low = jnp.bfloat16
+    seq_peers = [(lax.rem(place + step, 16), tp) for step in range(1, 16)]
+    greet(seq_peers + [other_half()])
+    rows, inner = r.held.shape
+    main = Reducer(
+        [(r.cot_t, r.gated, at, r.out_grad, at) for at in range(0, inner, SHARE_WIDTH)]
+        + [
+            (r.hidden_t, r.d_gate, at, r.gate_grad, at)
+            for at in range(0, r.gate_grad.shape[1], SHARE_WIDTH)
+        ],
+        rest,
+    )
+    states = r.decay_log.shape[0]
+    width = 512
+    tiles = inner // width
+    pair_sems = r.pair_sems
+
+    def columns(at):
+        return slice(at * width, (at + 1) * width)
+
+    def dot(left, right):
+        return jnp.dot(left, right, preferred_element_type=jnp.float32)
+
+    def dot_last(left, right):
+        return lax.dot_general(
+            left, right, (((1,), (1,)), ((), ())), preferred_element_type=jnp.float32
+        )
+
+    def line(ref):
+        return ref[...].reshape(1, -1)
+
+    half_rows = r.block.shape[0]
+    own_half = pl.ds(pl.multiple_of(tp * half_rows, half_rows), half_rows)
+    far_half = pl.ds(pl.multiple_of((1 - tp) * half_rows, half_rows), half_rows)
+    r.branch_send[...] = r.branch[far_half, :].astype(low)
+    branch_swap = remote(
+        r.branch_send, r.branch_far, pair_sems.at[0], pair_sems.at[1], other_half()
+    )
+    branch_swap.start()
+
+    held, drive, grad = r.held, r.drive, r.d_mixed
+    enter, leave, piece = r.enter, r.leave, r.piece
+
+    def rate_of(here):
+        return -jnp.exp(r.decay_log[:, here])
+
+    chain_out, chain_home, chain_middle, chain_end = chain_parts(
+        True,
+        piece,
+        lambda: rate_of(own_lanes(place)) * LOG2E,
+        r.follow,
+        r.come,
+        r.back,
+        r.chain_sems,
+    )
+    kept_all, state_all = r.kept, r.state
+    drive_grad, d_step_pre = r.drive_grad, r.d_step_pre
+    enter_grad, leave_grad = r.enter_grad, r.leave_grad
+
+    def again_tile(tile):
+        here = columns(tile)
+        rate = rate_of(here) * LOG2E
+
+        def block(index, state):
+            base = pl.multiple_of(index * 8, 8)
+            for offset in range(8):
+                at = base + offset
+                kept = jnp.exp2(rate * held[pl.ds(at, 1), here])
+                kept_all[at] = kept
+                state = kept * state + wide(enter[at], width) * drive[pl.ds(at, 1), here]
+                state_all[at + 1] = state
+            return state
+
+        start = r.start[:, here]
+        state_all[0] = start
+        lax.fori_loop(0, rows // 8, block, start)
+
+    def reverse_tile(tile):
+        here = columns(tile)
+        rate = rate_of(here)
+
+        def block(index, carry):
+            follow, decay = carry
+            base = pl.multiple_of((rows // 8 - 1 - index) * 8, 8)
+            for offset in range(7, -1, -1):
+                at = base + offset
+                now = grad[pl.ds(at, 1), here]
+                adjoint = wide(leave[at], width) * now + follow
+                drive_grad[pl.ds(at, 1), here] = jnp.sum(
+                    adjoint * wide(enter[at], width), axis=0, keepdims=True
+                )
+                enters = fold_lanes(adjoint * drive[pl.ds(at, 1), here])
+                leaves = fold_lanes(state_all[at + 1] * now)
+                if tile == 0:
+                    enter_grad[at], leave_grad[at] = enters, leaves
+                else:
+                    enter_grad[at] += enters
+                    leave_grad[at] += leaves
+                follow = kept_all[at] * adjoint
+                part = follow * state_all[at]
+                r.ext[pl.ds(at, 1), :] = jnp.sum(part * rate, axis=0, keepdims=True)
+                decay = decay + part * held[pl.ds(at, 1), here]
+            return follow, decay
+
+        follow = r.follow[:, here]
+        _, decay = lax.fori_loop(0, rows // 8, block, (follow, jnp.zeros_like(follow)))
+        r.decay_grad[:, here] = decay * rate
+        d_step = (
+            drive_grad[:, here] * r.conv_out[:, here].astype(jnp.float32) + r.ext[0:rows, :]
+        )
+        d_step_pre[:, here] = (d_step * jax.nn.sigmoid(r.step_pre[:, here])).astype(low)
+
+    step_rank = r.step_weight.shape[0]
+    select_grad = r.select_grad
+    extra = r.extra
+
+    def turned(value):
+        return value.astype(jnp.float32).T.astype(low)
+
+    def store_extra(first, tile, value):
+        for at in range(width // 128):
+            owner = tile * (width // 128) + at
+            extra[owner // 2, owner % 2, first : first + value.shape[0], :] = value[
+                :, at * 128 : (at + 1) * 128
+            ].astype(low)
+
+    def select_start():
+        step_in = turned(r.select_out[:, :step_rank])
+        total = jnp.zeros((rows, step_rank), jnp.float32)
+        for tile in range(tiles):
+            here = columns(tile)
+            total = total + dot_last(d_step_pre[:, here], r.step_weight[:, here].astype(low))
+            store_extra(0, tile, dot(step_in, d_step_pre[:, here]))
+        select_grad[:, :step_rank] = total
+        row_at = lax.broadcasted_iota(jnp.int32, (8, states, 128), 1)
+        lane_at = lax.broadcasted_iota(jnp.int32, (8, states, 128), 2)
+
+        def block(index, _):
+            base = pl.multiple_of(index * 8, 8)
+            here = pl.ds(base, 8)
+            enters = jnp.sum(enter_grad[here], axis=2, keepdims=True)
+            leaves = jnp.sum(leave_grad[here], axis=2, keepdims=True)
+            spread = jnp.where(lane_at == row_at, enters, 0.0)
+            spread = jnp.where(lane_at == row_at + states, leaves, spread)
+            select_grad[here, step_rank:] = jnp.sum(spread, axis=1)
+            return 0
+
+        lax.fori_loop(0, rows // 8, block, 0)
+        select_swap.start()
+
+    select_swap = remote(
+        select_grad, r.select_far, pair_sems.at[2], pair_sems.at[3], other_half()
+    )
+    conv_grad, rim_next, ext = r.conv_grad, r.rim_next, r.ext
+
+    def rim_copy(tile):
+        return remote(
+            conv_grad.at[0:8, columns(tile)],
+            rim_next.at[:, columns(tile)],
+            r.rim_sems.at[0, tile],
+            r.rim_sems.at[1, tile],
+            seq_peers[14],
+        )
+
+    select_count = r.select_weight.shape[0]
+
+    def select_end():
+        select_swap.wait()
+        total = (select_grad[...] + r.select_far[...]).astype(low)
+        select_low = total[:, :256]
+        first, second = turned(select_low[:, :128]), turned(select_low[:, 128:])
+        for tile in range(tiles):
+            here = columns(tile)
+            conv_out = r.conv_out[:, here]
+            store_extra(step_rank, tile, dot(first, conv_out))
+            store_extra(step_rank + 128, tile, dot(second[: select_count - 128], conv_out))
+            weight = r.select_weight[:, here].astype(low)
+            spare = jnp.zeros((256 - select_count, width), low)
+            d_conv = (
+                drive_grad[:, here] * r.step_size[:, here]
+                + grad[:, here] * line(r.skip_gain)[:, here]
+                + dot(select_low, jnp.concatenate([weight, spare], axis=0))
+            )
+            pre = r.conv_pre[:, here]
+            sigmoid = jax.nn.sigmoid(pre)
+            conv_grad[:, here] = d_conv * (sigmoid * (1.0 + pre * (1.0 - sigmoid)))
+            rim_copy(tile).start()
+            if tile % 2:
+                main.advance()
+
+    masks, masks_after = r.masks, r.masks_after
+
+    def conv_tile(tile):
+        here = columns(tile)
+        value = conv_grad[:, here]
+        weight = r.conv_weight
+        lines = []
+        ext[0:8, :] = r.rim[8:16, here].astype(jnp.float32)
+        ext[8:, :] = r.conv_in[:, here].astype(jnp.float32)
+        for lag in range(4):
+            shifted = ext[8 - lag : 8 - lag + rows, :]
+            if lag > 0:
+                shifted = shifted * wide(masks[lag - 1], width)
+            lines.append(jnp.sum(value * shifted, axis=0, keepdims=True))
+        lines.append(jnp.sum(value, axis=0, keepdims=True))
+        lines.append(
+            jnp.sum(d_step_pre[:, here].astype(jnp.float32), axis=0, keepdims=True)
+        )
+        lines.append(r.skip_grad[:, here])
+        lines.append(jnp.zeros((9, width), jnp.float32))
+        first = step_rank + select_count
+        store_extra(first, tile, r.decay_grad[:, here])
+        store_extra(first + states, tile, jnp.concatenate(lines, axis=0))
+        rim_copy(tile).wait_recv()
+        ext[0:rows, :] = value
+        ext[rows:, :] = rim_next[:, here]
+        total = weight[0:1, here] * value
+        for lag in range(1, 4):
+            total = total + weight[lag : lag + 1, here] * (
+                ext[lag : lag + rows, :] * wide(masks_after[lag - 1], width)
+            )
+        r.d_value[:, here] = total.astype(low)
+
+    chain_out()
+    main.advance(2)
+    chain_middle()
+    again_tile(0)
+    main.advance(1)
+    chain_home()
+    for tile in range(tiles):
+        if tile > 0:
+            again_tile(tile)
+            main.advance()
+        reverse_tile(tile)
+        main.advance()
+    select_start()
+    main.advance()
+    branch_swap.wait()
+    r.block_out[...] = (
+        r.block[...].astype(jnp.float32)
+        + r.branch[own_half, :]
+        + r.branch_far[...].astype(jnp.float32)
+    )
+    select_end()
+    main.advance()
+    for tile in range(tiles):
+        conv_tile(tile)
+        main.advance()
+    main.advance(main.chunks + 5)
+    chain_end()
+    main.drain()
+    for tile in range(tiles):
+        rim_copy(tile).wait_send()
+
+
+def backward_block(ident, given):
+    rows, inner = given.held.shape
+    half_rows, model = given.block.shape
+    states = given.decay_log.shape[0]
+    small_rows = given.step_weight.shape[0] + given.select_weight.shape[0] + states + 16
+    f32, low = jnp.float32, jnp.bfloat16
+    vmem = pl.BlockSpec(memory_space=pltpu.VMEM)
+    dma = pltpu.SemaphoreType.DMA
+    share = model // 16
+    outs = pl.pallas_call(
+        backward_block_kernel,
+        in_specs=[vmem] * len(BackwardIn._fields),
+        out_specs=[vmem] * len(BackwardOut._fields),
+        out_shape=[
+            jax.ShapeDtypeStruct((share, inner), f32),
+            jax.ShapeDtypeStruct((share, GATE_EARLY), f32),
+            jax.ShapeDtypeStruct((half_rows, model), f32),
+            jax.ShapeDtypeStruct((rows, inner), low),
+            jax.ShapeDtypeStruct((8, 2, small_rows, 128), low),
+        ],
+        scratch_shapes=[
+            pltpu.VMEM((16, states + 8, 128), f32),
+            pltpu.VMEM((16, states, 128), f32),
+            pltpu.VMEM((states, inner), f32),
+            pltpu.VMEM((rows, states, 512), f32),
+            pltpu.VMEM((rows + 1, states, 512), f32),
+            pltpu.VMEM((rows, inner), f32),
+            pltpu.VMEM((rows, inner), low),
+            pltpu.VMEM((states, inner), f32),
+            pltpu.VMEM((rows, states, 128), f32),
+            pltpu.VMEM((rows, states, 128), f32),
+            pltpu.VMEM((rows, 256), f32),
+            pltpu.VMEM((rows, 256), f32),
+            pltpu.VMEM((rows, inner), f32),
+            pltpu.VMEM((8, inner), f32),
+            pltpu.VMEM((rows + 8, 512), f32),
+            pltpu.VMEM((half_rows, model), low),
+            pltpu.VMEM((half_rows, model), low),
+            dma((4, 15)),
+            dma((4,)),
+            dma((2, inner // 512)),
+        ]
+        + reducer_scratch(inner + GATE_EARLY, share, SHARE_WIDTH),
+        compiler_params=pltpu.CompilerParams(
+            collective_id=ident, has_side_effects=True, vmem_limit_bytes=FINISH_LIMIT
+        ),
+    )(*given)
+    return BackwardOut(*outs)
 
 
 def on_device(
@@ -337,16 +2136,16 @@
     mean_sq = jnp.mean(residual * residual, axis=1, keepdims=True)
     inv_rms = lax.rsqrt(mean_sq + EPS_NORM)
     normed = residual * inv_rms
-    hidden = lax.all_gather(
-        (normed * norm_gain[None, :]).astype(jnp.bfloat16), "tp", axis=0, tiled=True
-    )
-    in_full, out_full = (
-        lax.all_gather(in_weight.astype(jnp.bfloat16), "seq", axis=0, tiled=True),
-        lax.all_gather(out_weight.astype(jnp.bfloat16), "seq", axis=0, tiled=True),
-    )
-    projected = jnp.einsum("td,dke->tke", hidden, in_full, preferred_element_type=jnp.float32)
-    conv_in = projected[:, 0].astype(jnp.bfloat16)
-    gate_pre = projected[:, 1]
+    low_type = jnp.bfloat16
+    projected, hidden, in_full = project(
+        (normed * norm_gain[None, :]).astype(low_type),
+        in_weight.astype(low_type).reshape(row_share, 2 * inner_dim),
+        0,
+    )
+    out_low, projected = lax.optimization_barrier((out_weight.astype(low_type), projected))
+    out_full = lax.all_gather(out_low, "seq", axis=0, tiled=True)
+    conv_in = projected[:, :inner_dim].astype(jnp.bfloat16)
+    gate_pre = projected[:, inner_dim:]
     rim_rows = passed_along(conv_in[row_count - (conv_taps - 1) :], "seq", 1)
     ext_rows = jnp.concatenate([rim_rows, conv_in], axis=0).astype(jnp.float32)
     same_docs = []
@@ -366,8 +2165,8 @@
     conv_out = jax.nn.silu(conv_pre).astype(jnp.bfloat16)
     conv_value = conv_out.astype(jnp.float32)
     select_low = select_weight.astype(jnp.bfloat16)
-    select_out = lax.psum(
-        jnp.einsum("te,ke->tk", conv_out, select_low, preferred_element_type=jnp.float32), "tp"
+    select_out = pair_sum(
+        jnp.einsum("te,ke->tk", conv_out, select_low, preferred_element_type=jnp.float32), 1
     )
     step_in = select_out[:, :step_rank].astype(jnp.bfloat16)
     state_in = select_out[:, step_rank : step_rank + states]
@@ -377,37 +2176,41 @@
     step_size = jax.nn.softplus(step_pre)
     decay_rate = -jnp.exp(decay_log)
     drive = step_size * conv_value
-    place = seq_index[None]
     held_step = jnp.where(keep_mask[:, None] > 0.0, step_size, RESET)
     enter = jnp.broadcast_to(state_in[:, :, None], (row_count, states, 128))
     leave = jnp.broadcast_to(state_out[:, :, None], (row_count, states, 128))
-    state_pieces = lax.all_gather(
-        piece_state(held_step, drive, enter, decay_rate, False), "seq"
-    )
-    scanned, start = scan_forward(
-        place, held_step, drive, enter, leave, decay_rate, state_pieces
-    )
+    nothing = jnp.zeros((8, 128), jnp.float32)
+    start, _ = chain(
+        piece_state(held_step, drive, enter, decay_rate, False), decay_rate, nothing, False, 2
+    )
+    scanned = scan_forward(held_step, drive, enter, leave, decay_rate, start)
     mixed = scanned + skip_gain[None, :] * conv_value
     gate_act = jax.nn.silu(gate_pre)
     gated = (mixed * gate_act).astype(jnp.bfloat16)
     branch = jnp.einsum("te,de->td", gated, out_full, preferred_element_type=jnp.float32)
-    block_out = residual + lax.psum_scatter(
-        branch.astype(jnp.bfloat16), "tp", scatter_dimension=0, tiled=True
-    ).astype(jnp.float32)
-    in_back, out_back = (
-        lax.all_gather(in_weight.astype(jnp.bfloat16), "seq", axis=0, tiled=True),
-        lax.all_gather(out_weight.astype(jnp.bfloat16), "seq", axis=0, tiled=True),
-    )
-    d_gated = jnp.einsum("td,de->te", cotangent, out_back, preferred_element_type=jnp.float32)
+    own_rows, far_rows = tp_index * half_rows, (1 - tp_index) * half_rows
+    d_gated = jnp.einsum("td,de->te", cotangent, out_full, preferred_element_type=jnp.float32)
     d_out_w = jnp.einsum("td,te->de", cotangent, gated, preferred_element_type=jnp.float32)
+    out_half = lax.psum_scatter(
+        d_out_w.astype(low_type), "seq", scatter_dimension=0, tiled=True
+    )
     d_mixed = d_gated * gate_act
     d_gate = (d_gated * mixed * silu_slope(gate_pre)).astype(jnp.bfloat16)
     skip_grad = jnp.sum(d_mixed * conv_value, axis=0)
-    adjoint_pieces = lax.all_gather(
-        piece_state(held_step, d_mixed, leave, decay_rate, True), "seq"
+    follow, branch_far = chain(
+        piece_state(held_step, d_mixed, leave, decay_rate, True),
+        decay_rate,
+        lax.dynamic_slice_in_dim(branch, far_rows, half_rows, 0).astype(low_type),
+        True,
+        3,
+    )
+    block_out = (
+        residual
+        + lax.dynamic_slice_in_dim(branch, own_rows, half_rows, 0)
+        + branch_far.astype(jnp.float32)
     )
     drive_grad, step_grad, decay_grad, enter_grad, leave_grad = scan_backward(
-        place, held_step, drive, d_mixed, enter, leave, decay_rate, start, adjoint_pieces
+        held_step, drive, d_mixed, enter, leave, decay_rate, start, follow
     )
     enter_grad = jnp.sum(enter_grad, axis=2)
     leave_grad = jnp.sum(leave_grad, axis=2)
@@ -420,7 +2223,7 @@
         [d_step_in, enter_grad, leave_grad],
         axis=1,
     )
-    d_select = lax.psum(select_grads, "tp").astype(jnp.bfloat16)
+    d_select = pair_sum(select_grads, 4).astype(jnp.bfloat16)
     select_w_grad = jnp.einsum("tk,te->ke", d_select, conv_out, preferred_element_type=jnp.float32)
     d_conv = (
         drive_grad * step_size
@@ -452,114 +2255,113 @@
         )
     conv_w_grad = jnp.stack(conv_w_rows, axis=0)
     conv_b_grad = jnp.sum(d_conv_pre, axis=0)
-    d_projected = jnp.stack([d_conv_in.astype(jnp.bfloat16), d_gate], axis=1)
-    d_hidden = lax.psum_scatter(
-        jnp.einsum("tke,dke->td", d_projected, in_back, preferred_element_type=jnp.float32),
-        "tp",
+    d_projected = jnp.concatenate([d_conv_in.astype(jnp.bfloat16), d_gate], axis=1)
+    d_hidden = jnp.einsum(
+        "tkn,kdn->td",
+        d_projected.reshape(row_count, in_full.shape[0], -1),
+        in_full,
+        preferred_element_type=jnp.float32,
+    )
+    vector_grads = jnp.stack([conv_b_grad, step_bias_grad, skip_grad], axis=0)
+    small_grads = jnp.concatenate(
+        [step_w_grad, select_w_grad, decay_grad, conv_w_grad, vector_grads], axis=0
+    )
+    out_grad = out_half.astype(jnp.float32)
+    in_grad = lax.psum_scatter(
+        jnp.einsum("td,tn->dn", hidden, d_projected, preferred_element_type=jnp.float32),
+        "seq",
         scatter_dimension=0,
         tiled=True,
     )
-    d_in_w = jnp.einsum("td,tke->dke", hidden, d_projected, preferred_element_type=jnp.float32)
-    in_grad, out_grad = (
-        lax.psum_scatter(d_in_w, "seq", scatter_dimension=0, tiled=True),
-        lax.psum_scatter(d_out_w, "seq", scatter_dimension=0, tiled=True),
-    )
+    small_full = lax.psum(small_grads, "seq")
+    d_hidden = lax.psum_scatter(d_hidden, "tp", scatter_dimension=0, tiled=True)
+    in_grad = in_grad.reshape(in_weight.shape)
     gain_part = jnp.sum(d_hidden * normed, axis=0)
     scaled = d_hidden * norm_gain[None, :]
-    cot_half = lax.dynamic_slice_in_dim(cotangent, tp_index * half_rows, half_rows, 0).astype(
+    cot_half = lax.dynamic_slice_in_dim(cotangent, own_rows, half_rows, 0).astype(
         jnp.float32
     )
     input_grad = cot_half + inv_rms * (
         scaled - normed * jnp.mean(scaled * normed, axis=1, keepdims=True)
     )
+    edges = [step_rank, select_weight.shape[0], states, conv_taps, 3]
+    edges = [sum(edges[:at]) for at in range(len(edges) + 1)]
+    step_local, select_local, decay_local, conv_local, vector_local = [
+        small_full[low:high] for low, high in zip(edges, edges[1:])
+    ]
     in_square = in_grad * in_grad
-    in_row_piece = (DECAY * in_rows + (1.0 - DECAY) * EPS_FACTOR) * tp_first + (
+    out_square = out_grad * out_grad
+    in_row_part = jnp.sum(in_square, axis=(1, 2))
+    out_row_part = jnp.sum(out_square, axis=1)
+    small_row_part = jnp.sum(small_full * small_full, axis=1)
+    in_total = jnp.sum(DECAY * in_rows + (1.0 - DECAY) * EPS_FACTOR) * tp_first + (
         1.0 - DECAY
-    ) * jnp.sum(in_square, axis=(1, 2)) / (2 * channels)
-    in_col_piece = (DECAY * in_cols + (1.0 - DECAY) * EPS_FACTOR) * seq_first + (
+    ) * jnp.sum(in_row_part) / (2 * channels)
+    out_total = jnp.sum(DECAY * out_rows + (1.0 - DECAY) * EPS_FACTOR) * tp_first + (
         1.0 - DECAY
-    ) * jnp.sum(in_square, axis=0) / model_dim
-    out_square = out_grad * out_grad
-    out_row_piece = (DECAY * out_rows + (1.0 - DECAY) * EPS_FACTOR) * tp_first + (
-        1.0 - DECAY
-    ) * jnp.sum(out_square, axis=1) / channels
-    out_col_piece = (DECAY * out_cols + (1.0 - DECAY) * EPS_FACTOR) * seq_first + (
-        1.0 - DECAY
-    ) * jnp.sum(out_square, axis=0) / model_dim
-    vector_grads = jnp.stack([conv_b_grad, step_bias_grad, skip_grad], axis=0)
-    (
-        conv_full,
-        vector_full,
-        select_full,
-        step_full,
-        decay_full,
-        gain_grad,
-        in_rows_all,
-        in_cols_all,
-        out_rows_all,
-        out_cols_all,
-    ) = lax.psum(
-        (
-            widen_last(conv_w_grad, tp_index, channels),
-            widen_last(vector_grads, tp_index, channels),
-            widen_last(select_w_grad, tp_index, channels),
-            widen_last(step_w_grad, tp_index, channels),
-            widen_last(decay_grad, tp_index, channels),
-            gain_part,
-            widen_last(in_row_piece, seq_index, model_dim),
-            widen_last(in_col_piece, tp_index, channels),
-            widen_last(out_row_piece, seq_index, model_dim),
-            widen_last(out_col_piece, tp_index, channels),
-        ),
-        ("seq", "tp"),
-    )
-    conv_local = narrow(conv_full, tp_index, inner_dim)
-    vector_local = narrow(vector_full, tp_index, inner_dim)
-    select_local = narrow(select_full, tp_index, inner_dim)
-    step_local = narrow(step_full, tp_index, inner_dim)
-    decay_local = narrow(decay_full, tp_index, inner_dim)
+    ) * jnp.sum(out_row_part) / channels
+    seq_part = jnp.concatenate(
+        [jnp.sum(in_square, axis=0).reshape(-1, 128), jnp.sum(out_square, axis=0).reshape(-1, 128)]
+    )
+    shared_part = jnp.concatenate(
+        [
+            gain_part.reshape(-1, 128),
+            jnp.broadcast_to(in_total, (8, 128)),
+            jnp.broadcast_to(out_total, (8, 128)),
+        ]
+    )
+    row_parts = jnp.concatenate([in_row_part, out_row_part, small_row_part])
+    row_parts = jnp.pad(row_parts, (0, -row_parts.shape[0] % 1024)).reshape(-1, 128)
+    col_sums, shared_sums, row_sums = sum_over(seq_part, shared_part, row_parts)
+    col_sums = col_sums.reshape(-1)
+    in_col_sums = col_sums[: 2 * inner_dim].reshape(2, inner_dim)
+    out_col_sums = col_sums[2 * inner_dim :]
+    gain_grad = shared_sums[: model_dim // 128].reshape(-1)
+    in_mean = shared_sums[model_dim // 128, 0] / model_dim
+    out_mean = shared_sums[model_dim // 128 + 8, 0] / model_dim
+    row_sums = row_sums.reshape(-1)
+    in_row_sums = row_sums[:row_share]
+    out_row_sums = row_sums[row_share : 2 * row_share]
+    small_row_sums = row_sums[2 * row_share :]
+    in_rows_new = DECAY * in_rows + (1.0 - DECAY) * (in_row_sums / (2 * channels) + EPS_FACTOR)
+    in_cols_new = DECAY * in_cols + (1.0 - DECAY) * (in_col_sums / model_dim + EPS_FACTOR)
+    out_rows_new = DECAY * out_rows + (1.0 - DECAY) * (out_row_sums / channels + EPS_FACTOR)
+    out_cols_new = DECAY * out_cols + (1.0 - DECAY) * (out_col_sums / model_dim + EPS_FACTOR)
+    step_rows_new, step_cols_new, stepw_update = factor_update(
+        step_local, small_row_sums[edges[0] : edges[1]], step_rows, step_cols, channels
+    )
+    select_rows_new, select_cols_new, select_update = factor_update(
+        select_local, small_row_sums[edges[1] : edges[2]], select_rows, select_cols, channels
+    )
+    decay_rows_new, decay_cols_new, decay_update = factor_update(
+        decay_local, small_row_sums[edges[2] : edges[3]], decay_rows, decay_cols, channels
+    )
     conv_rows_new, conv_cols_new, conv_update = factor_update(
-        conv_full, conv_local, conv_rows, conv_cols
-    )
-    select_rows_new, select_cols_new, select_update = factor_update(
-        select_full, select_local, select_rows, select_cols
-    )
-    step_rows_new, step_cols_new, stepw_update = factor_update(
-        step_full, step_local, step_rows, step_cols
-    )
-    decay_rows_new, decay_cols_new, decay_update = factor_update(
-        decay_full, decay_local, decay_rows, decay_cols
+        conv_local, small_row_sums[edges[3] : edges[4]], conv_rows, conv_cols, channels
     )
     bias_moment_new, convb_update = moment_update(vector_local[0], bias_moment)
     step_moment_new, stepb_update = moment_update(vector_local[1], step_moment)
     skip_moment_new, skip_update = moment_update(vector_local[2], skip_moment)
     gain_moment_new, gain_update = moment_update(gain_grad, norm_moment)
-    in_rows_new = narrow(in_rows_all, seq_index, row_share)
-    in_cols_new = narrow(in_cols_all, tp_index, inner_dim)
-    in_update = in_grad * lax.rsqrt(
-        in_rows_new[:, None, None] * in_cols_new[None] / jnp.mean(in_rows_all)
-    )
-    out_rows_new = narrow(out_rows_all, seq_index, row_share)
-    out_cols_new = narrow(out_cols_all, tp_index, inner_dim)
-    out_update = out_grad * lax.rsqrt(
-        out_rows_new[:, None] * out_cols_new[None, :] / jnp.mean(out_rows_all)
-    )
-    clip_totals = lax.psum(
-        jnp.stack(
-            [
-                sum_squares(in_update),
-                sum_squares(out_update),
-                seq_first * sum_squares(conv_update),
-                seq_first * sum_squares(select_update),
-                seq_first * sum_squares(stepw_update),
-                seq_first * sum_squares(decay_update),
-                seq_first * sum_squares(convb_update),
-                seq_first * sum_squares(stepb_update),
-                seq_first * sum_squares(skip_update),
-            ]
-        ),
-        ("seq", "tp"),
-    )
+    in_update = in_grad * lax.rsqrt(in_rows_new[:, None, None] * in_cols_new[None] / in_mean)
+    out_update = out_grad * lax.rsqrt(out_rows_new[:, None] * out_cols_new[None, :] / out_mean)
+    squares = jnp.stack(
+        [
+            sum_squares(in_update),
+            sum_squares(out_update),
+            seq_first * sum_squares(conv_update),
+            seq_first * sum_squares(select_update),
+            seq_first * sum_squares(stepw_update),
+            seq_first * sum_squares(decay_update),
+            seq_first * sum_squares(convb_update),
+            seq_first * sum_squares(stepb_update),
+            seq_first * sum_squares(skip_update),
+        ]
+    )
+    _, clip_totals, _ = sum_over(
+        nothing, jnp.broadcast_to(jnp.pad(squares, (0, 7))[:, None], (16, 128)), nothing
+    )
+    clip_totals = clip_totals[:, 0]
     gain_new = apply_step(norm_gain, gain_update, sum_squares(gain_update), model_dim, RATES[0])
     in_new = apply_step(in_weight, in_update, clip_totals[0], model_dim * 2 * channels, RATES[1])
     out_new = apply_step(out_weight, out_update, clip_totals[1], model_dim * channels, RATES[2])
@@ -574,7 +2376,6 @@
     stepb_new = apply_step(step_bias, stepb_update, clip_totals[7], channels, RATES[7])
     decay_new = apply_step(decay_log, decay_update, clip_totals[5], states * channels, RATES[8])
     skip_new = apply_step(skip_gain, skip_update, clip_totals[8], channels, RATES[9])
-    low_type = jnp.bfloat16
     return (
         block_out,
         input_grad,
@@ -627,9 +2428,157 @@
     )
 
 
+def on_block_device(
+    block_in,
+    cotangent,
+    segment_ids,
+    norm_gain,
+    in_weight,
+    out_weight,
+    conv_weight,
+    conv_bias,
+    select_weight,
+    step_weight,
+    step_bias,
+    decay_log,
+    skip_gain,
+    norm_moment,
+    in_rows,
+    in_cols,
+    out_rows,
+    out_cols,
+    conv_rows,
+    conv_cols,
+    bias_moment,
+    select_rows,
+    select_cols,
+    step_rows,
+    step_cols,
+    step_moment,
+    decay_rows,
+    decay_cols,
+    skip_moment,
+):
+    tp_count = lax.axis_size("tp")
+    seq_index = lax.axis_index("seq")
+    tp_index = lax.axis_index("tp")
+    half_rows, model_dim = block_in.shape
+    row_count = cotangent.shape[0]
+    inner_dim = in_weight.shape[2]
+    channels = inner_dim * tp_count
+    conv_taps = conv_weight.shape[0]
+    states = decay_log.shape[0]
+    step_rank = step_weight.shape[0]
+    row_share = in_weight.shape[0]
+    low_type = jnp.bfloat16
+    id_padded = jnp.concatenate(
+        [
+            jnp.full((conv_taps - 1,), -1, jnp.int32),
+            segment_ids,
+            jnp.full((conv_taps - 1,), -2, jnp.int32),
+        ]
+    )
+    window = lax.dynamic_slice_in_dim(
+        id_padded, seq_index * row_count, row_count + 2 * (conv_taps - 1)
+    )
+    local_ids = window[conv_taps - 1 : conv_taps - 1 + row_count]
+    same_docs = [
+        (window[conv_taps - 1 - lag : conv_taps - 1 - lag + row_count] == local_ids).astype(
+            jnp.float32
+        )[:, None]
+        for lag in range(conv_taps)
+    ]
+    masks = jnp.broadcast_to(jnp.stack(same_docs[1:]), (conv_taps - 1, row_count, 128))
+    ids_after = window[conv_taps - 1 :]
+    same_after = [
+        (ids_after[lag : lag + row_count] == local_ids).astype(jnp.float32)[:, None]
+        for lag in range(1, conv_taps)
+    ]
+    masks_after = jnp.broadcast_to(jnp.stack(same_after), (conv_taps - 1, row_count, 128))
+    lanes = jnp.concatenate(
+        [step_rows, select_rows, decay_rows, conv_rows, jnp.ones((76,), jnp.float32)]
+        + [in_rows, out_rows, jnp.ones((384,), jnp.float32)]
+    ).reshape(8, 128)
+    f = forward_block(
+        0,
+        ForwardIn(
+        in_weight=in_weight,
+        out_weight=out_weight,
+        block=block_in,
+        cot=cotangent,
+        norm_gain=norm_gain,
+        conv_weight=conv_weight,
+        conv_bias=conv_bias,
+        step_bias=step_bias,
+        skip_gain=skip_gain,
+        masks=masks,
+        select_weight=select_weight,
+        step_weight=step_weight,
+        decay_log=decay_log,
+        ),
+    )
+    back = backward_block(
+        1,
+        BackwardIn(
+            block=block_in,
+            masks=masks,
+            masks_after=masks_after,
+            conv_weight=conv_weight,
+            skip_gain=skip_gain,
+            select_weight=select_weight,
+            step_weight=step_weight,
+            decay_log=decay_log,
+            **shared(f, BackwardIn),
+        ),
+    )
+    new = finish(
+        2,
+        channels,
+        FinishIn(
+            hidden_t=f.hidden_t,
+            d_gate=f.d_gate,
+            weights=f.weights,
+            block=block_in,
+            cot=cotangent,
+            lanes=lanes,
+            norm_gain=norm_gain,
+            norm_moment=norm_moment,
+            in_cols=in_cols,
+            out_cols=out_cols,
+            step_cols=step_cols,
+            select_cols=select_cols,
+            decay_cols=decay_cols,
+            conv_cols=conv_cols,
+            bias_moment=bias_moment,
+            step_moment=step_moment,
+            skip_moment=skip_moment,
+            conv_bias=conv_bias,
+            step_bias=step_bias,
+            skip_gain=skip_gain,
+            **shared(back, FinishIn),
+        ),
+    )
+    return renew(
+        RenewIn(
+            value_grad=new.in_grad,
+            gate_grad=new.in_grad,
+            out_grad=back.out_grad,
+            block_out=back.block_out,
+            in_weight=in_weight,
+            out_weight=out_weight,
+            step_weight=step_weight,
+            select_weight=select_weight,
+            decay_log=decay_log,
+            conv_weight=conv_weight,
+            **shared(new, RenewIn),
+        )
+    )
+
+
 def solution(mesh):
+    on_slice = mesh.shape["seq"] == 16 and mesh.shape["tp"] == 2
     return jax.shard_map(
-        on_device,
+        on_block_device if on_slice else on_device,
         mesh=mesh,
         in_specs=(
             P(("seq", "tp"), None),

time: 1350 us -> 403 us (0.30)
  waiting for transfers between devices: 1050 us -> 0 us
  Pallas kernels: 35 us -> 391 us
  matrix products: 71.4 us -> 0 us
  blocking collectives: 59.9 us -> 0 us
  other arithmetic: 51.2 us -> 0.09 us
  local copies, waits for them, and re-layouts: 41.3 us -> 3.15 us
  between operations: 31.4 us -> 1.3 us
    reduce_scatter x4 -> x0, waiting for transfers between devices: 501 us -> none  [the longest x1 335 us: on_device(): lax.psum_scatter(d_in_w, 'seq', scatter_dimension=0, tiled=True)]
    pallas_call x4, Pallas kernels: 35 us -> 391 us  [the longest x1 157 us: forward_block(): pl.pallas_call(forward_block_kernel, in_specs=[vmem] * len(ForwardIn._fie...]
    psum x3 -> x0, waiting for transfers between devices: 291 us -> none  [the longest x2 271 us: on_device(): lax.psum((widen_last(conv_w_grad, tp_index, channels), widen_last(vector_...]
    all_gather x4 -> x0, waiting for transfers between devices: 256 us -> none  [the longest x1 118 us: on_device(): lax.all_gather(in_weight.astype(jnp.bfloat16), 'seq', axis=0, tiled=True)]
    dot_general x12 -> x0, matrix products: 71.4 us -> none  [the longest x1 13.4 us: on_device(): jnp.einsum('td,tke->dke', hidden, d_projected, preferred_element_type=jnp...]
    psum x2 -> x0, blocking collectives: 50 us -> none  [the longest x1 39.6 us: on_device(): lax.psum((widen_last(conv_w_grad, tp_index, channels), widen_last(vector_...]
    reduce_sum x30 -> x0, other arithmetic: 31.4 us -> none  [the longest x9 7.89 us: sum_squares(): return jnp.sum(update * update)]
    unnamed x258 -> x12, local copies, waits for them, and re-layouts: 30.4 us -> 0.03 us
  transfers between devices with their start and end apart: 13 -> 0, of which waited for: 11 -> 0; matrix products, arithmetic and copies ran while one was open for 5% -> 0% of each run, Pallas kernels for 1% -> 0%
where the time goes in v3:
time: 403 us; the launch traced here: 395 us
  Pallas kernels  391 us (97%)
    pallas_call x1, Pallas kernels, forward_block(): pl.pallas_call(forward_block_kernel, in_specs=[vmem] * len(ForwardIn._fie...  157 us
    pallas_call x1, Pallas kernels, finish(): pl.pallas_call(functools.partial(finish_kernel, channels, model), in_spec...  124 us
    pallas_call x1, Pallas kernels, backward_block(): pl.pallas_call(backward_block_kernel, in_specs=[vmem] * len(BackwardIn._f...  98.3 us
    pallas_call x1, Pallas kernels, renew(): pl.pallas_call(renew_kernel, grid=(RENEW_TILES,), in_specs=list(specs), o...  11 us

profile of v3, /device:TPU:0, one launch (start us, length us, event | category | flops | bytes accessed | tf_op | source)
XLA Modules:
  0.0 395.1 jit_solution(14934904024812439218)
XLA Ops:
  0.7 0.8 concatenate.6
  1.5 0.1 dynamic_slice.3
  1.6 0.1 compare_bitcast_fusion.2
  1.7 0.8 broadcast_in_dim.28.refs_9_.refs_21_
  2.5 156.9 %shard_map.652 = (bf16[16,128,128]{2,1,0:T(8,128)(2,1)}, bf16[16,128,128]{2,1,0:T(8,128)(2,1)}, f32[24,2048]{1,0:T(8,128)}, bf16[128,2048]{1,0:T(8,128)(2,1)}, b...) custom-call(f32[128,2,2048]{2,1,0:T(2,128)} %refs_9_.1, ...), custom_call_target="tpu_custom_call" | custom-call | tf_op jit(solution)/shard_map/pallas_call | solution.py:1653
  159.4 0.8 broadcast_in_dim.31.refs_22_
  160.1 0.0 copy-start
  160.1 0.0 copy-start.1
  160.1 0.0 copy-start.2
  160.2 0.0 copy-start.3
  160.2 0.0 copy-start.4
  160.2 0.0 copy-start.5
  160.2 98.3 %shard_map.653 = (f32[128,2048]{1,0:T(8,128)}, f32[128,1024]{1,0:T(8,128)}, f32[64,2048]{1,0:T(8,128)}, bf16[128,2048]{1,0:T(8,128)(2,1)}, bf16[8,2,320,128]{3,2,1,0:T(8,128)(2,1)}) custom-call(bf16[16,128,128]{2,1,0:T(8,128)(2,1)} %get-tuple-element.80.refs_0_, bf16[16,128,128]{2,1,0:T(8,128)(2,1)} %get-tuple-element.81.refs_1_, ...), custom_call_target="tpu_custom_call" | custom-call | tf_op jit(solution)/shard_map/pallas_call | solution.py:2038
  258.5 0.0 copy-done
  258.5 0.0 copy-done.1
  258.5 0.0 copy-done.2
  258.5 0.0 copy-done.3
  258.5 0.0 copy-done.4
  258.5 0.0 copy-done.5
  258.5 0.7 concatenate.7
  259.2 124.4 %shard_map.654 = (f32[128,4096]{1,0:T(8,128)}, f32[64,2048]{1,0:T(8,128)}, f32[320,2048]{1,0:T(8,128)}, f32[5,128,128]{2,1,0:T(8,128)}, f32[8,128]{1,0:T(8,128)}, /*index=5*/f32[32,2048]{1,0:T(8,128)}) custom-call(bf16[16,128,128]{2,1,0:T(8,128)(2,1)} %get-tuple-element.80.refs_0_, bf16[128,2048]{1,0:T(8,128)(2,1)} %get-tuple-element.100.refs_1_, ...), custom_call_target="tpu_custom_call" | custom-call | tf_op jit(solution)/shard_map/pallas_call | solution.py:988
  383.7 11.0 %shard_map.655 = (f32[64,2048]{1,0:T(8,128)}, f32[64,2048]{1,0:T(8,128)}, f32[2048]{0:T(1024)}, f32[2048]{0:T(1024)}, bf16[2048]{0:T(1024)(128)(2,1)}, /*index=5...) custom-call(f32[128,4096]{1,0:T(8,128)} %get-tuple-element.105.refs_, ...), custom_call_target="tpu_custom_call" | custom-call | tf_op jit(solution)/shard_map/pallas_call | solution.py:1156
  (5 shorter events, 0.0 us)
Async XLA Ops:
  160.1 98.3 %copy-start = (f32[160]{0:T(256)S(1)}, f32[160]{0:T(256)}, u32[]{:S(2)}) copy-start(f32[160]{0:T(256)} %param.50) | copy-start | bytes 1924
  160.1 98.3 %copy-start.1 = (f32[128]{0:T(128)S(1)}, f32[128]{0:T(128)}, u32[]{:S(2)}) copy-start(f32[128]{0:T(128)} %param.52) | copy-start | bytes 1540
  160.1 98.4 %copy-start.2 = (f32[16]{0:T(128)S(1)}, f32[16]{0:T(128)}, u32[]{:S(2)}) copy-start(f32[16]{0:T(128)} %param.55) | copy-start | bytes 196
  160.2 98.4 %copy-start.3 = (f32[4]{0:T(128)S(1)}, f32[4]{0:T(128)}, u32[]{:S(2)}) copy-start(f32[4]{0:T(128)} %param.47) | copy-start | bytes 52
  160.2 98.4 %copy-start.4 = (f32[128]{0:T(128)S(1)}, f32[128]{0:T(128)}, u32[]{:S(2)}) copy-start(f32[128]{0:T(128)} %param.43) | copy-start | bytes 1540
  160.2 98.4 %copy-start.5 = (f32[128]{0:T(128)S(1)}, f32[128]{0:T(128)}, u32[]{:S(2)}) copy-start(f32[128]{0:T(128)} %param.45) | copy-start | bytes 1540

commit v4 on v3

--- a/solution.py
+++ b/solution.py
@@ -20,7 +20,7 @@
 TILE = 512
 X_FIRST = (4, 8)
 SHARE_WIDTH = 256
-GATE_EARLY = 1024
+SLOTS = 8
 RENEW_TILES = 4
 VMEM_LIMIT = 48 * 1024 * 1024
 FINISH_LIMIT = 63 * 1024 * 1024
@@ -417,7 +417,7 @@
         self.send, self.come = refs[:3], refs[3:6]
         self.sent, self.got, self.total = refs[6:9], refs[9:12], refs[12]
         self.z, self.x, self.core = position()
-        self.chunks, self.width = self.come[2].shape[0], self.come[2].shape[3]
+        self.chunks, self.width = len(jobs), self.come[2].shape[3]
         self.peers = [
             [device(self.z, self.x, 1 - self.core)],
             [device(self.z, 1 - self.x, self.core)],
@@ -430,7 +430,7 @@
             return [
                 remote(
                     self.send[level].at[slot],
-                    self.come[level].at[chunk],
+                    self.come[level].at[chunk % SLOTS],
                     self.sent[level].at[chunk],
                     self.got[level].at[chunk],
                     self.peers[level][0],
@@ -439,7 +439,7 @@
         return [
             remote(
                 self.send[2].at[slot, 0, lax.rem(self.z + 1 + at, 4)],
-                self.come[2].at[chunk, at],
+                self.come[2].at[chunk % SLOTS, at],
                 self.sent[2].at[chunk, at],
                 self.got[2].at[chunk, at],
                 self.peers[2][at],
@@ -468,7 +468,7 @@
         out[:, here] = out[:, here] + value if more else value
 
     def after_core(self, chunk, x):
-        come = self.come[0][chunk, x].astype(jnp.float32)
+        come = self.come[0][chunk % SLOTS, x].astype(jnp.float32)
         return self.product(chunk, self.core * 8 + x * 4, 4) + come
 
     def fill(self, level, chunk, values):
@@ -492,12 +492,12 @@
         elif level == 1:
             self.fill(1, chunk, [lambda: self.after_core(chunk, 1 - self.x)])
         elif level == 2:
-            come = self.come[1][chunk, 0].astype(jnp.float32)
+            come = self.come[1][chunk % SLOTS, 0].astype(jnp.float32)
             self.total[...] = self.after_core(chunk, self.x) + come
             self.fill(2, chunk, [lambda: self.total[...]])
             self.put(chunk, self.total[self.z], False)
         else:
-            come = [self.come[2][chunk, at].astype(jnp.float32) for at in range(3)]
+            come = [self.come[2][chunk % SLOTS, at].astype(jnp.float32) for at in range(3)]
             self.put(chunk, (come[0] + come[1]) + come[2], True)
 
     def step(self, step):
@@ -524,9 +524,9 @@
         pltpu.VMEM((4, 2, 4, share, width), low),
         pltpu.VMEM((4, 1, 4, share, width), low),
         pltpu.VMEM((4, 1, 4, share, width), low),
-        pltpu.VMEM((chunks, 2, 4, share, width), low),
-        pltpu.VMEM((chunks, 1, 4, share, width), low),
-        pltpu.VMEM((chunks, 3, share, width), low),
+        pltpu.VMEM((SLOTS, 2, 4, share, width), low),
+        pltpu.VMEM((SLOTS, 1, 4, share, width), low),
+        pltpu.VMEM((SLOTS, 3, share, width), low),
         dma((chunks,)),
         dma((chunks,)),
         dma((chunks, 3)),
@@ -545,78 +545,11 @@
     return jnp.broadcast_to(row, (128, 128)).T
 
 
-class FinishIn(NamedTuple):
-    hidden_t: object
-    d_value: object
-    d_gate: object
-    gate_grad: object
-    extra: object
-    weights: object
-    block: object
-    cot: object
-    lanes: object
-    out_grad: object
-    norm_gain: object
-    norm_moment: object
-    in_cols: object
-    out_cols: object
-    step_cols: object
-    select_cols: object
-    decay_cols: object
-    conv_cols: object
-    bias_moment: object
-    step_moment: object
-    skip_moment: object
-    conv_bias: object
-    step_bias: object
-    skip_gain: object
-
-
-class FinishOut(NamedTuple):
-    in_grad: object
-    input_grad: object
-    small: object
-    scales: object
-    lanes_new: object
-    vectors_new: object
-
-
-class FinishWork(NamedTuple):
-    come_core: object
-    send_x: object
-    come_x: object
-    send_z: object
-    come_z: object
-    full: object
-    mine: object
-    acc: object
-    far: object
-    pair: object
-    pair_far: object
-    totals: object
-    totals_acc: object
-    totals_far: object
-    come_half: object
-    d_hidden: object
-    held: object
-    held_sems: object
-    extra_sent: object
-    extra_got: object
-    sums_sent: object
-    sums_got: object
-    half_sems: object
-
-
-def finish_kernel(channels, model, *refs):
-    r, rest = gathered(refs, FinishIn, FinishOut, FinishWork)
+def finish_part(channels, model, r, main):
     z, x, core = position()
     place, tp = lax.axis_index("seq"), lax.axis_index("tp")
     core_peer, x_peer = device(z, x, 1 - core), device(z, 1 - x, core)
     z_peers = [device(lax.rem(z + step, 4), x, core) for step in (1, 2, 3)]
-    others = [
-        (lax.rem(z + step, 4) * 4 + x * 2 + core, 1 - lax.axis_index("tp")) for step in range(4)
-    ]
-    greet([core_peer, x_peer, device(z, 1 - x, 1 - core)] + z_peers + others)
     low = jnp.bfloat16
     half_rows = r.block.shape[0]
     own_half = pl.ds(pl.multiple_of(tp * half_rows, half_rows), half_rows)
@@ -626,20 +559,11 @@
         d_hidden.at[far_half], r.come_half, r.half_sems.at[0], r.half_sems.at[1], other_half()
     )
     sides = [r.d_value, r.d_gate]
-    inner = r.out_grad.shape[1]
-    early = r.gate_grad.shape[1]
-    r.in_grad[:, inner : inner + early] = r.gate_grad[...]
-    main = Reducer(
-        [(r.hidden_t, r.d_value, at, r.in_grad, at) for at in range(0, inner, SHARE_WIDTH)]
-        + [(r.hidden_t, r.d_gate, at, r.in_grad, inner + at) for at in range(early, inner, SHARE_WIDTH)],
-        rest,
-    )
-
     kept_chunks, _, kept_width = r.weights.shape
 
     def fetch(chunk):
         return pltpu.make_async_copy(
-            r.weights.at[chunk], r.held.at[chunk % 2], r.held_sems.at[chunk]
+            r.weights.at[chunk], r.fetched.at[chunk % 2], r.fetched_sems.at[chunk]
         )
 
     def hidden_stage(chunk):
@@ -648,7 +572,7 @@
         at = chunk % per_side
         part = lax.dot_general(
             sides[chunk // per_side][:, at * kept_width : (at + 1) * kept_width],
-            r.held[chunk % 2],
+            r.fetched[chunk % 2],
             (((1,), (1,)), ((), ())),
             preferred_element_type=jnp.float32,
         )
@@ -800,7 +724,7 @@
     extra_core.start()
     extra_steps = {1: extra_stage_x, 3: extra_stage_z, 5: extra_stage_last, 7: extra_back_x, 9: extra_back_core}
     extra_steps.update({14: residual_stage, 12: out_stage, 11: small_stage})
-    for step in range(max(main.chunks + 5, 16)):
+    for step in range(max(main.chunks + 5 - main.at, 16)):
         main.advance()
         if step < kept_chunks:
             hidden_stage(step)
@@ -968,68 +892,8 @@
     vectors_new[10:18, :] = jnp.zeros((8, half), jnp.float32)
     vectors_new[27:32, :] = jnp.zeros((5, half), jnp.float32)
 
-    main.drain()
     for copy in [extra_core, extra_x] + extra_z + back_z + [back_x, back_core]:
         copy.wait_send()
-
-
-def finish(ident, channels, given):
-    half_rows, model = given.block.shape
-    share, inner = given.out_grad.shape
-    columns = 2 * inner
-    f32, low = jnp.float32, jnp.bfloat16
-    small_rows = given.extra.shape[2]
-    vmem = pl.BlockSpec(memory_space=pltpu.VMEM)
-    dma = pltpu.SemaphoreType.DMA
-    shape = jax.ShapeDtypeStruct
-    seq_rows = columns // 128 + inner // 128 + model // 128 + 16
-    kept_chunks, _, kept_width = given.weights.shape
-    block = (small_rows, 128)
-    outs = pl.pallas_call(
-        functools.partial(finish_kernel, channels, model),
-        in_specs=[
-            pl.BlockSpec(memory_space=pltpu.HBM) if value is given.weights else vmem for value in given
-        ],
-        out_specs=[vmem] * len(FinishOut._fields),
-        out_shape=[
-            shape((share, columns), f32),
-            shape((half_rows, model), f32),
-            shape((small_rows, inner), f32),
-            shape((5, 128, 128), f32),
-            shape((8, 128), f32),
-            shape((32, inner), f32),
-        ],
-        scratch_shapes=[
-            pltpu.VMEM((8,) + block, low),
-            pltpu.VMEM((4,) + block, low),
-            pltpu.VMEM((4,) + block, low),
-            pltpu.VMEM((3,) + block, low),
-            pltpu.VMEM((3,) + block, low),
-            pltpu.VMEM((4, 2, 2) + block, low),
-            pltpu.VMEM((seq_rows, 128), f32),
-            pltpu.VMEM((8, seq_rows, 128), f32),
-            pltpu.VMEM((4, model // 128 + 16, 128), f32),
-            pltpu.VMEM((8, 128), f32),
-            pltpu.VMEM((8, 128), f32),
-            pltpu.VMEM((16, 128), f32),
-            pltpu.VMEM((8, 16, 128), f32),
-            pltpu.VMEM((4, 16, 128), f32),
-            pltpu.VMEM((half_rows, model), f32),
-            pltpu.VMEM((2 * half_rows, model), f32),
-            pltpu.VMEM((2, model, kept_width), low),
-            dma((kept_chunks,)),
-            dma((10,)),
-            dma((10,)),
-            dma((21,)),
-            dma((21,)),
-            dma((2,)),
-        ]
-        + reducer_scratch(columns - given.gate_grad.shape[1], share, SHARE_WIDTH),
-        compiler_params=pltpu.CompilerParams(
-            collective_id=ident, has_side_effects=True, vmem_limit_bytes=FINISH_LIMIT
-        ),
-    )(*given)
-    return FinishOut(*outs)
 
 
 class RenewIn(NamedTuple):
@@ -1705,84 +1569,12 @@
     return out._replace(weights=out.weights.reshape(-1, model, width))
 
 
-class BackwardIn(NamedTuple):
-    hidden_t: object
-    cot_t: object
-    gated: object
-    d_gate: object
-    piece: object
-    d_mixed: object
-    held: object
-    drive: object
-    enter: object
-    leave: object
-    start: object
-    conv_out: object
-    step_pre: object
-    step_size: object
-    conv_pre: object
-    conv_in: object
-    rim: object
-    select_out: object
-    branch: object
-    block: object
-    skip_grad: object
-    masks: object
-    masks_after: object
-    conv_weight: object
-    skip_gain: object
-    select_weight: object
-    step_weight: object
-    decay_log: object
-
-
-class BackwardOut(NamedTuple):
-    out_grad: object
-    gate_grad: object
-    block_out: object
-    d_value: object
-    extra: object
-
-
-class BackwardWork(NamedTuple):
-    come: object
-    back: object
-    follow: object
-    kept: object
-    state: object
-    drive_grad: object
-    d_step_pre: object
-    decay_grad: object
-    enter_grad: object
-    leave_grad: object
-    select_grad: object
-    select_far: object
-    conv_grad: object
-    rim_next: object
-    ext: object
-    branch_send: object
-    branch_far: object
-    chain_sems: object
-    pair_sems: object
-    rim_sems: object
-
-
-def backward_block_kernel(*refs):
-    r, rest = gathered(refs, BackwardIn, BackwardOut, BackwardWork)
+def backward_part(r, main):
     z, x, core = position()
     place, tp = lax.axis_index("seq"), lax.axis_index("tp")
     low = jnp.bfloat16
     seq_peers = [(lax.rem(place + step, 16), tp) for step in range(1, 16)]
-    greet(seq_peers + [other_half()])
     rows, inner = r.held.shape
-    main = Reducer(
-        [(r.cot_t, r.gated, at, r.out_grad, at) for at in range(0, inner, SHARE_WIDTH)]
-        + [
-            (r.hidden_t, r.d_gate, at, r.gate_grad, at)
-            for at in range(0, r.gate_grad.shape[1], SHARE_WIDTH)
-        ],
-        rest,
-    )
     states = r.decay_log.shape[0]
     width = 512
     tiles = inner // width
@@ -2019,61 +1811,226 @@
     for tile in range(tiles):
         conv_tile(tile)
         main.advance()
-    main.advance(main.chunks + 5)
-    chain_end()
+
+    def end():
+        chain_end()
+        for tile in range(tiles):
+            rim_copy(tile).wait_send()
+
+    return end
+
+
+def rest_kernel(channels, model, *refs):
+    r, reducer_refs = gathered(refs, RestIn, RestOut, RestWork)
+    z, x, core = position()
+    place, tp = lax.axis_index("seq"), lax.axis_index("tp")
+    seq_peers = [(lax.rem(place + step, 16), tp) for step in range(1, 16)]
+    across = [(lax.rem(z + step, 4) * 4 + x * 2 + core, 1 - tp) for step in range(4)]
+    greet(seq_peers + across)
+    inner = r.out_grad.shape[1]
+    starts = range(0, inner, SHARE_WIDTH)
+    main = Reducer(
+        [(r.cot_t, r.gated, at, r.out_grad, at) for at in starts]
+        + [(r.hidden_t, r.d_gate, at, r.in_grad, inner + at) for at in starts]
+        + [(r.hidden_t, r.d_value, at, r.in_grad, at) for at in starts],
+        reducer_refs,
+    )
+    end = backward_part(r, main)
+    finish_part(channels, model, r, main)
+    end()
     main.drain()
-    for tile in range(tiles):
-        rim_copy(tile).wait_send()
-
-
-def backward_block(ident, given):
+
+
+class RestIn(NamedTuple):
+    hidden_t: object
+    cot_t: object
+    gated: object
+    d_gate: object
+    piece: object
+    d_mixed: object
+    held: object
+    drive: object
+    enter: object
+    leave: object
+    start: object
+    conv_out: object
+    step_pre: object
+    step_size: object
+    conv_pre: object
+    conv_in: object
+    rim: object
+    select_out: object
+    branch: object
+    block: object
+    skip_grad: object
+    masks: object
+    masks_after: object
+    conv_weight: object
+    skip_gain: object
+    select_weight: object
+    step_weight: object
+    decay_log: object
+    weights: object
+    cot: object
+    lanes: object
+    norm_gain: object
+    norm_moment: object
+    in_cols: object
+    out_cols: object
+    step_cols: object
+    select_cols: object
+    decay_cols: object
+    conv_cols: object
+    bias_moment: object
+    step_moment: object
+    skip_moment: object
+    conv_bias: object
+    step_bias: object
+
+
+class RestOut(NamedTuple):
+    out_grad: object
+    block_out: object
+    in_grad: object
+    input_grad: object
+    small: object
+    scales: object
+    lanes_new: object
+    vectors_new: object
+
+
+class RestWork(NamedTuple):
+    d_value: object
+    extra: object
+    come: object
+    back: object
+    follow: object
+    kept: object
+    state: object
+    drive_grad: object
+    d_step_pre: object
+    decay_grad: object
+    enter_grad: object
+    leave_grad: object
+    select_grad: object
+    select_far: object
+    conv_grad: object
+    rim_next: object
+    ext: object
+    branch_send: object
+    branch_far: object
+    chain_sems: object
+    pair_sems: object
+    rim_sems: object
+    come_core: object
+    send_x: object
+    come_x: object
+    send_z: object
+    come_z: object
+    full: object
+    mine: object
+    acc: object
+    far: object
+    pair: object
+    pair_far: object
+    totals: object
+    totals_acc: object
+    totals_far: object
+    come_half: object
+    d_hidden: object
+    fetched: object
+    fetched_sems: object
+    extra_sent: object
+    extra_got: object
+    sums_sent: object
+    sums_got: object
+    half_sems: object
+
+
+def rest_block(ident, channels, given):
     rows, inner = given.held.shape
     half_rows, model = given.block.shape
     states = given.decay_log.shape[0]
     small_rows = given.step_weight.shape[0] + given.select_weight.shape[0] + states + 16
+    columns = 2 * inner
     f32, low = jnp.float32, jnp.bfloat16
-    vmem = pl.BlockSpec(memory_space=pltpu.VMEM)
     dma = pltpu.SemaphoreType.DMA
     share = model // 16
+    seq_rows = columns // 128 + inner // 128 + model // 128 + 16
+    kept_chunks, _, kept_width = given.weights.shape
+    block = (small_rows, 128)
+    shape, space = jax.ShapeDtypeStruct, pltpu.VMEM
+    vmem = pl.BlockSpec(memory_space=pltpu.VMEM)
+    specs = RestIn(*[vmem] * len(given))._replace(
+        weights=pl.BlockSpec(memory_space=pltpu.HBM)
+    )
     outs = pl.pallas_call(
-        backward_block_kernel,
-        in_specs=[vmem] * len(BackwardIn._fields),
-        out_specs=[vmem] * len(BackwardOut._fields),
+        functools.partial(rest_kernel, channels, model),
+        in_specs=list(specs),
+        out_specs=[vmem] * len(RestOut._fields),
         out_shape=[
-            jax.ShapeDtypeStruct((share, inner), f32),
-            jax.ShapeDtypeStruct((share, GATE_EARLY), f32),
-            jax.ShapeDtypeStruct((half_rows, model), f32),
-            jax.ShapeDtypeStruct((rows, inner), low),
-            jax.ShapeDtypeStruct((8, 2, small_rows, 128), low),
+            shape((share, inner), f32),
+            shape((half_rows, model), f32),
+            shape((share, columns), f32),
+            shape((half_rows, model), f32),
+            shape((small_rows, inner), f32),
+            shape((5, 128, 128), f32),
+            shape((8, 128), f32),
+            shape((32, inner), f32),
         ],
         scratch_shapes=[
-            pltpu.VMEM((16, states + 8, 128), f32),
-            pltpu.VMEM((16, states, 128), f32),
-            pltpu.VMEM((states, inner), f32),
-            pltpu.VMEM((rows, states, 512), f32),
-            pltpu.VMEM((rows + 1, states, 512), f32),
-            pltpu.VMEM((rows, inner), f32),
-            pltpu.VMEM((rows, inner), low),
-            pltpu.VMEM((states, inner), f32),
-            pltpu.VMEM((rows, states, 128), f32),
-            pltpu.VMEM((rows, states, 128), f32),
-            pltpu.VMEM((rows, 256), f32),
-            pltpu.VMEM((rows, 256), f32),
-            pltpu.VMEM((rows, inner), f32),
-            pltpu.VMEM((8, inner), f32),
-            pltpu.VMEM((rows + 8, 512), f32),
-            pltpu.VMEM((half_rows, model), low),
-            pltpu.VMEM((half_rows, model), low),
+            space((rows, inner), low),
+            space((8, 2, small_rows, 128), low),
+            space((16, states + 8, 128), f32),
+            space((16, states, 128), f32),
+            space((states, inner), f32),
+            space((rows, states, 512), f32),
+            space((rows + 1, states, 512), f32),
+            space((rows, inner), f32),
+            space((rows, inner), low),
+            space((states, inner), f32),
+            space((rows, states, 128), f32),
+            space((rows, states, 128), f32),
+            space((rows, 256), f32),
+            space((rows, 256), f32),
+            space((rows, inner), f32),
+            space((8, inner), f32),
+            space((rows + 8, 512), f32),
+            space((half_rows, model), low),
+            space((half_rows, model), low),
             dma((4, 15)),
             dma((4,)),
             dma((2, inner // 512)),
+            space((8,) + block, low),
+            space((4,) + block, low),
+            space((4,) + block, low),
+            space((3,) + block, low),
+            space((3,) + block, low),
+            space((4, 2, 2) + block, low),
+            space((seq_rows, 128), f32),
+            space((8, seq_rows, 128), f32),
+            space((4, model // 128 + 16, 128), f32),
+            space((8, 128), f32),
+            space((8, 128), f32),
+            space((16, 128), f32),
+            space((8, 16, 128), f32),
+            space((4, 16, 128), f32),
+            space((half_rows, model), f32),
+            space((2 * half_rows, model), f32),
+            space((2, model, kept_width), low),
+            dma((kept_chunks,)),
+            dma((10,)),
+            dma((10,)),
+            dma((21,)),
+            dma((21,)),
+            dma((2,)),
         ]
-        + reducer_scratch(inner + GATE_EARLY, share, SHARE_WIDTH),
+        + reducer_scratch(inner + columns, share, SHARE_WIDTH),
         compiler_params=pltpu.CompilerParams(
             collective_id=ident, has_side_effects=True, vmem_limit_bytes=FINISH_LIMIT
         ),
     )(*given)
-    return BackwardOut(*outs)
+    return RestOut(*outs)
 
 
 def on_device(
@@ -2517,30 +2474,19 @@
         decay_log=decay_log,
         ),
     )
-    back = backward_block(
+    rest = rest_block(
         1,
-        BackwardIn(
+        channels,
+        RestIn(
             block=block_in,
+            cot=cotangent,
+            lanes=lanes,
             masks=masks,
             masks_after=masks_after,
             conv_weight=conv_weight,
-            skip_gain=skip_gain,
             select_weight=select_weight,
             step_weight=step_weight,
             decay_log=decay_log,
-            **shared(f, BackwardIn),
-        ),
-    )
-    new = finish(
-        2,
-        channels,
-        FinishIn(
-            hidden_t=f.hidden_t,
-            d_gate=f.d_gate,
-            weights=f.weights,
-            block=block_in,
-            cot=cotangent,
-            lanes=lanes,
             norm_gain=norm_gain,
             norm_moment=norm_moment,
             in_cols=in_cols,
@@ -2555,22 +2501,20 @@
             conv_bias=conv_bias,
             step_bias=step_bias,
             skip_gain=skip_gain,
-            **shared(back, FinishIn),
+            **shared(f, RestIn),
         ),
     )
     return renew(
         RenewIn(
-            value_grad=new.in_grad,
-            gate_grad=new.in_grad,
-            out_grad=back.out_grad,
-            block_out=back.block_out,
+            value_grad=rest.in_grad,
+            gate_grad=rest.in_grad,
             in_weight=in_weight,
             out_weight=out_weight,
             step_weight=step_weight,
             select_weight=select_weight,
             decay_log=decay_log,
             conv_weight=conv_weight,
-            **shared(new, RenewIn),
+            **shared(rest, RenewIn),
         )
     )
 

time: 403 us -> 386 us (0.958)
  Pallas kernels: 391 us -> 374 us
    pallas_call x2 -> x1, Pallas kernels: 223 us -> 206 us  [rest_block(): pl.pallas_call(functools.partial(rest_kernel, channels, model), in_specs=...]
where the time goes in v4:
time: 386 us; the launch traced here: 379 us
  Pallas kernels  374 us (97%)
    pallas_call x1, Pallas kernels, rest_block(): pl.pallas_call(functools.partial(rest_kernel, channels, model), in_specs=...  206 us
    pallas_call x1, Pallas kernels, forward_block(): pl.pallas_call(forward_block_kernel, in_specs=[vmem] * len(ForwardIn._fie...  157 us
    pallas_call x1, Pallas kernels, renew(): pl.pallas_call(renew_kernel, grid=(RENEW_TILES,), in_specs=list(specs), o...  11 us

profile of v4, /device:TPU:0, one launch (start us, length us, event | category | flops | bytes accessed | tf_op | source)
XLA Modules:
  0.0 378.7 jit_solution(6294122436761532837)
XLA Ops:
  0.7 1.4 concatenate.7
  2.1 0.8 concatenate.6
  2.9 0.1 dynamic_slice.3
  3.0 0.1 compare_bitcast_fusion.2
  3.1 0.8 broadcast_in_dim.31.refs_22_
  3.9 0.8 broadcast_in_dim.28.refs_9_.refs_21_
  4.7 156.9 %shard_map.652 = (bf16[16,128,128]{2,1,0:T(8,128)(2,1)}, bf16[16,128,128]{2,1,0:T(8,128)(2,1)}, f32[24,2048]{1,0:T(8,128)}, bf16[128,2048]{1,0:T(8,128)(2,1)}, b...) custom-call(f32[128,2,2048]{2,1,0:T(2,128)} %refs_9_.1, ...), custom_call_target="tpu_custom_call" | custom-call | tf_op jit(solution)/shard_map/pallas_call | solution.py:1517
  161.6 205.6 %shard_map.653 = (f32[128,2048]{1,0:T(8,128)}, f32[64,2048]{1,0:T(8,128)}, f32[128,4096]{1,0:T(8,128)}, f32[64,2048]{1,0:T(8,128)}, f32[320,2048]{1,0:T(8,128)},...) custom-call(bf16[16,128,128]{2,1,0:T(8,128)(2,1)} %get-tuple-element.77.refs_0_, ...), custom_call_target="tpu_custom_call" | custom-call | tf_op jit(solution)/shard_map/pallas_call | solution.py:1967
  367.2 11.0 %shard_map.654 = (f32[64,2048]{1,0:T(8,128)}, f32[64,2048]{1,0:T(8,128)}, f32[2048]{0:T(1024)}, f32[2048]{0:T(1024)}, bf16[2048]{0:T(1024)(128)(2,1)}, /*index=5...) custom-call(f32[128,4096]{1,0:T(8,128)} %get-tuple-element.98.refs_0, ...), custom_call_target="tpu_custom_call" | custom-call | tf_op jit(solution)/shard_map/pallas_call | solution.py:1020
  (5 shorter events, 0.0 us)

commit v5 on v4

--- a/solution.py
+++ b/solution.py
@@ -21,7 +21,7 @@
 X_FIRST = (4, 8)
 SHARE_WIDTH = 256
 SLOTS = 8
-RENEW_TILES = 4
+RENEW_TILES = 2
 VMEM_LIMIT = 48 * 1024 * 1024
 FINISH_LIMIT = 63 * 1024 * 1024
 
@@ -407,6 +407,31 @@
     return SimpleNamespace(**named), list(refs[at:])
 
 
+def mirrored(r, group, near, sems, outward):
+    copies = []
+    for at, name in enumerate(group._fields):
+        ends = (near[at], getattr(r, name)) if outward else (getattr(r, name), near[at])
+        copies.append(pltpu.make_async_copy(*ends, sems.at[at]))
+        setattr(r, name, near[at])
+    return group(*copies)
+
+
+def mirrors(group, shapes):
+    named = shapes._asdict()
+    picked = [named[name] for name in group._fields]
+    return [pltpu.VMEM(ref.shape, ref.dtype) for ref in picked] + [
+        pltpu.SemaphoreType.DMA((len(picked),))
+    ]
+
+
+def placed(group, *lazy):
+    names = [name for other in lazy for name in other._fields]
+    return [
+        pl.BlockSpec(memory_space=pltpu.HBM if name in names else pltpu.VMEM)
+        for name in group._fields
+    ]
+
+
 def shared(source, group):
     return {name: value for name, value in source._asdict().items() if name in group._fields}
 
@@ -545,7 +570,7 @@
     return jnp.broadcast_to(row, (128, 128)).T
 
 
-def finish_part(channels, model, r, main):
+def finish_part(channels, model, r, main, stores):
     z, x, core = position()
     place, tp = lax.axis_index("seq"), lax.axis_index("tp")
     core_peer, x_peer = device(z, x, 1 - core), device(z, 1 - x, core)
@@ -648,8 +673,8 @@
     def line(ref):
         return ref[...].reshape(1, -1)
 
-    in_tiles, out_tiles = r.in_grad.shape[1] // 128, r.out_grad.shape[1] // 128
-    seq_rows = in_tiles + out_tiles
+    half = r.out_grad.shape[1]
+    tiles = half // 128
     gain_tiles = model // 128
 
     def put(base, row):
@@ -665,7 +690,7 @@
         residual = r.block[...].astype(jnp.float32)
         inv_rms = lax.rsqrt(jnp.mean(residual * residual, axis=1, keepdims=True) + EPS_NORM)
         normed = residual * inv_rms
-        put(seq_rows, jnp.sum(total * normed, axis=0, keepdims=True))
+        put(2 * tiles, jnp.sum(total * normed, axis=0, keepdims=True))
         scaled = total * line(r.norm_gain)
         mean = jnp.mean(scaled * normed, axis=1, keepdims=True)
         r.input_grad[...] = r.cot[own_half, :].astype(jnp.float32) + inv_rms * (scaled - normed * mean)
@@ -704,48 +729,42 @@
                 )
             put_rows(at, partial)
 
-    def column_sums(ref, base):
-        def one(index, partial):
-            columns = pl.ds(pl.multiple_of(index * span, span), span)
-            value = ref[:, columns]
-            sums = jnp.sum(value * value, axis=0, keepdims=True)
-            for at in range(wide_span):
-                mine[pl.ds(base + index * wide_span + at, 1), :] = sums[:, at * 128 : (at + 1) * 128]
-            return partial + fold_square(value)
-
-        return lax.fori_loop(
-            0, ref.shape[1] // span, one, jnp.zeros((ref.shape[0], 128), jnp.float32)
-        )
+    late = 2 * tiles + gain_tiles + 8
+    row_sums = r.row_sums
+
+    def square_sums(ref, start, width, base):
+        value = ref[:, start : start + width]
+        put(base, jnp.sum(value * value, axis=0, keepdims=True))
+        return fold_square(value)
+
+    def in_stage(chunk):
+        start = (chunk - main.chunks // 3) * main.width
+        if start < 0 or chunk >= main.chunks:
+            return
+        gate = start < half
+        base = start // 128 if gate else late + (start - half) // 128
+        start = half + start if gate else start - half
+        part = square_sums(r.in_grad, start, main.width, base)
+        row_sums[...] = part if base == 0 else row_sums[...] + part
 
     def out_stage():
-        put_rows(4, column_sums(r.out_grad, in_tiles))
-
-    pair[...] = jnp.zeros(pair.shape, jnp.float32)
-    extra_core.start()
-    extra_steps = {1: extra_stage_x, 3: extra_stage_z, 5: extra_stage_last, 7: extra_back_x, 9: extra_back_core}
-    extra_steps.update({14: residual_stage, 12: out_stage, 11: small_stage})
-    for step in range(max(main.chunks + 5 - main.at, 16)):
-        main.advance()
-        if step < kept_chunks:
-            hidden_stage(step)
-        if step in extra_steps:
-            extra_steps[step]()
-    put_rows(3, column_sums(r.in_grad, 0))
+        part = jnp.zeros((r.out_grad.shape[0], 128), jnp.float32)
+        for start in range(0, half, span):
+            part = part + square_sums(r.out_grad, start, span, tiles + start // 128)
+        put_rows(4, part)
 
     lanes = r.lanes
     row_at = lax.broadcasted_iota(jnp.int32, lanes.shape, 0)
     lane_at = lax.broadcasted_iota(jnp.int32, lanes.shape, 1)
     counts = jnp.where(row_at == 3, 2.0 * channels, 1.0 * channels)
     held_lanes = DECAY * lanes[...] + (1.0 - DECAY) * EPS_FACTOR
-    part = jnp.where(tp == 0, held_lanes, 0.0) + (1.0 - DECAY) * pair[...] / counts
-
     def total(value):
         return jnp.sum(jnp.sum(value, axis=1, keepdims=True), axis=0, keepdims=True)
 
-    base = seq_rows + gain_tiles
-    for at in range(2):
-        mean = total(jnp.where(row_at == 3 + at, part, 0.0)) / model
-        mine[base + 8 * at : base + 8 * at + 8, :] = jnp.broadcast_to(mean, (8, 128))
+    def put_mean(at, sums, first):
+        part = jnp.where(tp == 0, held_lanes, 0.0) + (1.0 - DECAY) * sums[...] / counts
+        mean = total(jnp.where(row_at == at, part, 0.0)) / model
+        mine[first : first + 8, :] = jnp.broadcast_to(mean, (8, 128))
 
     sums_sent, sums_got = r.sums_sent, r.sums_got
 
@@ -757,54 +776,55 @@
     across = [(lax.rem(z + step, 4) * 4 + plane, 1 - tp) for step in range(4)]
 
     def sum_hops(first, value, acc, far, shared):
-        acc[plane] = value[...]
-        copies = [hop(first + at, acc.at[plane], acc.at[plane], mates[at]) for at in range(3)]
-        for copy in copies:
-            copy.start()
-        for copy in copies:
-            copy.wait()
-        acc[4 + z] = (acc[0] + acc[1]) + (acc[2] + acc[3])
+        plane_copies = [hop(first + at, acc.at[plane], acc.at[plane], mates[at]) for at in range(3)]
         part = acc.at[4 + z]
-        copies = [hop(first + 3 + at, part, part, z_peers[at]) for at in range(3)]
-        copies += [
-            hop(first + 6 + at, part.at[shared:], far.at[z], across[at]) for at in range(4)
-        ]
-        for copy in copies:
-            copy.start()
-        for copy in copies:
-            copy.wait()
-        value[...] = (acc[4] + acc[5]) + (acc[6] + acc[7])
-        value[shared:] = value[shared:] + ((far[0] + far[1]) + (far[2] + far[3]))
-
-    pair_copy = hop(20, pair, r.pair_far, other_half())
-    pair_copy.start()
-    sum_hops(0, mine, r.acc, r.far, seq_rows)
-    pair_copy.wait()
-
-    lanes_new = held_lanes + (1.0 - DECAY) * (pair[...] + r.pair_far[...]) / counts
-    r.lanes_new[...] = lanes_new
-    flat = row_at * 128 + lane_at
-    means = jnp.where(row_at == 3, mine[base : base + 8, :], mine[base + 8 : base + 16, :])
-    for low_edge, high_edge in groups.values():
-        member = (flat >= low_edge) & (flat < high_edge)
-        mean = total(jnp.where(member, lanes_new, 0.0)) / (high_edge - low_edge)
-        means = jnp.where(member, mean, means)
-    scale = lax.rsqrt(lanes_new / means)
-    scales = [lanes_to_rows(scale[at : at + 1, :]) for at in range(5)]
-    small_scale = jnp.concatenate(scales[:3], axis=0)
-    in_scale, out_scale = scales[3], scales[4]
+        z_copies = [hop(first + 3 + at, part, part, z_peers[at]) for at in range(3)]
+        z_copies += [hop(first + 6 + at, part.at[shared:], far.at[z], across[at]) for at in range(4)]
+
+        def begin():
+            acc[plane] = value[...]
+            for copy in plane_copies:
+                copy.start()
+
+        def middle():
+            for copy in plane_copies:
+                copy.wait()
+            acc[4 + z] = (acc[0] + acc[1]) + (acc[2] + acc[3])
+            for copy in z_copies:
+                copy.start()
+
+        def end():
+            for copy in z_copies:
+                copy.wait()
+            value[...] = (acc[4] + acc[5]) + (acc[6] + acc[7])
+            value[shared:] = value[shared:] + ((far[0] + far[1]) + (far[2] + far[3]))
+
+        return begin, middle, end
 
     def cols_new(old, sums, count):
         return DECAY * old + (1.0 - DECAY) * (sums / count + EPS_FACTOR)
 
-    in_cols = cols_new(
-        jnp.concatenate([r.in_cols[0:1, :], r.in_cols[1:2, :]], axis=1), take(mine, 0, in_tiles), model
-    )
-    half = in_cols.shape[1] // 2
-    out_cols = cols_new(line(r.out_cols), take(mine, in_tiles, out_tiles), model)
-    vectors_new[3:4, :] = in_cols[:, :half]
-    vectors_new[4:5, :] = in_cols[:, half:]
-    vectors_new[5:6, :] = out_cols
+    def part_hops(first, low_row, high_row, low_far, high_far):
+        return sum_hops(
+            first,
+            mine.at[low_row:high_row],
+            r.acc.at[:, low_row:high_row],
+            r.far.at[:, low_far:high_far],
+            high_row - low_row - (high_far - low_far),
+        )
+
+    shared_rows = gain_tiles + 8
+    early_hops = part_hops(0, 0, late, 0, shared_rows)
+    late_hops = part_hops(20, late, late + tiles + 8, shared_rows, shared_rows + 8)
+    pair_copy = hop(30, pair, r.pair_far, other_half())
+    last_copy = hop(31, r.pair_last, r.pair_last_far, other_half())
+    scales_out = r.scales
+    sums = {}
+
+    def early_begin():
+        put_mean(4, pair, 2 * tiles + gain_tiles)
+        pair_copy.start()
+        early_hops[0]()
 
     def squares(ref, row_scale, first_row):
         def one(index, partial):
@@ -818,43 +838,102 @@
             lax.fori_loop(0, ref.shape[1] // span, one, jnp.zeros((ref.shape[0], 128), jnp.float32))
         )
 
-    sums = [squares(r.in_grad, in_scale, 3), squares(r.out_grad, out_scale, 5)]
     group_cols = {
-        "step": (line(r.step_cols), 8),
-        "select": (line(r.select_cols), 7),
-        "decay": (line(r.decay_cols), 9),
-        "conv": (line(r.conv_cols), 6),
+        "step": (r.step_cols, 8),
+        "select": (r.select_cols, 7),
+        "decay": (r.decay_cols, 9),
+        "conv": (r.conv_cols, 6),
     }
-    for name, (low_edge, high_edge) in groups.items():
-        old_cols, new_row = group_cols[name]
-        partial = jnp.zeros((high_edge - low_edge, 128), jnp.float32)
-        for at in range(0, small.shape[1], span):
-            columns = slice(at, at + span)
-            value = small[low_edge:high_edge, columns]
-            col = cols_new(
-                old_cols[:, columns],
-                jnp.sum(value * value, axis=0, keepdims=True),
-                high_edge - low_edge,
-            )
-            vectors_new[new_row : new_row + 1, columns] = col
-            row_scale = small_scale[low_edge:high_edge]
-            partial = partial + fold_square(value * wide(row_scale, span) * lax.rsqrt(col))
-        sums.append(total(partial))
-    updates = []
-    for at in range(3):
-        value = small[308 + at : 309 + at, :]
-        old = line((r.bias_moment, r.step_moment, r.skip_moment)[at])
-        moment = DECAY * old + (1.0 - DECAY) * (value * value + EPS_FACTOR)
-        vectors_new[24 + at : 25 + at, :] = moment
-        vectors_new[18 + at : 19 + at, :] = value
-        update = value * lax.rsqrt(moment)
-        updates.append(update)
-        sums.append(jnp.sum(update * update, axis=1, keepdims=True))
+
+    def early_end():
+        early_hops[2]()
+        pair_copy.wait()
+        lanes_new = held_lanes + (1.0 - DECAY) * (pair[...] + r.pair_far[...]) / counts
+        r.lanes_new[...] = lanes_new
+        flat = row_at * 128 + lane_at
+        base = 2 * tiles + gain_tiles
+        means = mine[base : base + 8, :]
+        for low_edge, high_edge in groups.values():
+            member = (flat >= low_edge) & (flat < high_edge)
+            mean = total(jnp.where(member, lanes_new, 0.0)) / (high_edge - low_edge)
+            means = jnp.where(member, mean, means)
+        scale = lax.rsqrt(lanes_new / means)
+        for at in (0, 1, 2, 4):
+            scales_out[at] = lanes_to_rows(scale[at : at + 1, :])
+        vectors_new[4:5, :] = cols_new(r.in_cols[1:2, :], take(mine, 0, tiles), model)
+        vectors_new[5:6, :] = cols_new(line(r.out_cols), take(mine, tiles, tiles), model)
+        sums["out"] = squares(r.out_grad, scales_out[4], 5)
+        small_scale = jnp.concatenate([scales_out[0], scales_out[1], scales_out[2]], axis=0)
+        for name, (low_edge, high_edge) in groups.items():
+            old_cols, new_row = line(group_cols[name][0]), group_cols[name][1]
+            partial = jnp.zeros((high_edge - low_edge, 128), jnp.float32)
+            for at in range(0, small.shape[1], span):
+                columns = slice(at, at + span)
+                value = small[low_edge:high_edge, columns]
+                col = cols_new(
+                    old_cols[:, columns],
+                    jnp.sum(value * value, axis=0, keepdims=True),
+                    high_edge - low_edge,
+                )
+                vectors_new[new_row : new_row + 1, columns] = col
+                row_scale = small_scale[low_edge:high_edge]
+                partial = partial + fold_square(value * wide(row_scale, span) * lax.rsqrt(col))
+            sums[name] = total(partial)
+        for at in range(3):
+            value = small[308 + at : 309 + at, :]
+            old = line((r.bias_moment, r.step_moment, r.skip_moment)[at])
+            moment = DECAY * old + (1.0 - DECAY) * (value * value + EPS_FACTOR)
+            vectors_new[24 + at : 25 + at, :] = moment
+            vectors_new[18 + at : 19 + at, :] = value
+            update = value * lax.rsqrt(moment)
+            vectors_new[21 + at : 22 + at, :] = update
+            sums[at] = jnp.sum(update * update, axis=1, keepdims=True)
+        gain_grad = take(mine, 2 * tiles, gain_tiles)
+        moment = DECAY * line(r.norm_moment) + (1.0 - DECAY) * (gain_grad * gain_grad + EPS_FACTOR)
+        update = gain_grad * lax.rsqrt(moment)
+        root = jnp.sqrt(jnp.mean(update * update, axis=1, keepdims=True))
+        vectors_new[0:1, :] = gain_grad
+        vectors_new[1:2, :] = line(r.norm_gain) - RATES[0] / jnp.maximum(1.0, root / CLIP) * update
+        vectors_new[2:3, :] = moment
+        vectors_new[10:18, :] = jnp.zeros((8, half), jnp.float32)
+        vectors_new[27:32, :] = jnp.zeros((5, half), jnp.float32)
+
+    pair[...] = jnp.zeros(pair.shape, jnp.float32)
+    r.pair_last[...] = jnp.zeros(pair.shape, jnp.float32)
+    extra_core.start()
+    extra_steps = {1: extra_stage_x, 3: extra_stage_z, 5: extra_stage_last, 7: extra_back_x, 9: extra_back_core}
+    extra_steps.update({2: out_stage, 10: residual_stage, 11: small_stage})
+    extra_steps.update({12: early_begin, 13: early_hops[1], 14: early_end})
+    for step in range(max(main.chunks + 5 - main.at, 15)):
+        main.advance()
+        in_stage(main.at - 6)
+        if step < kept_chunks:
+            hidden_stage(step)
+        if step in extra_steps:
+            extra_steps[step]()
+        if step == 11:
+            for copy in stores:
+                copy.start()
+
+    r.pair_last[3:4, :] = rows_to_lanes(row_sums[...])
+    last_copy.start()
+    put_mean(3, r.pair_last, late + tiles)
+    for action in late_hops:
+        action()
+    last_copy.wait()
+    sums_in = (r.pair_last[...] + r.pair_last_far[...]) / counts
+    lanes_new = jnp.where(row_at == 3, held_lanes + (1.0 - DECAY) * sums_in, r.lanes_new[...])
+    r.lanes_new[...] = lanes_new
+    in_mean = mine[late + tiles : late + tiles + 1, :]
+    in_scale = lanes_to_rows(lax.rsqrt(lanes_new[3:4, :] / in_mean))
+    vectors_new[3:4, :] = cols_new(r.in_cols[0:1, :], take(mine, late, tiles), model)
+    in_sum = squares(r.in_grad, in_scale, 3)
     totals = r.totals
-    for at in range(9):
-        totals[at : at + 1, :] = jnp.broadcast_to(sums[at], (1, 128))
+    for at, value in enumerate([in_sum, *sums.values()]):
+        totals[at : at + 1, :] = jnp.broadcast_to(value, (1, 128))
     totals[9:16, :] = jnp.zeros((7, 128), jnp.float32)
-    sum_hops(10, totals, r.totals_acc, r.totals_far, 0)
+    for action in sum_hops(10, totals, r.totals_acc, r.totals_far, 0):
+        action()
 
     def rate(at, count, step_rate, copies):
         root = jnp.sqrt(totals[at : at + 1, :] / (copies * count))
@@ -863,9 +942,9 @@
     in_rate = rate(0, 2.0 * channels * model, RATES[1], 1)
     out_rate = rate(1, 1.0 * channels * model, RATES[2], 1)
 
-    scales_out = r.scales
     scales_out[3] = in_scale * in_rate
-    scales_out[4] = out_scale * out_rate
+    scales_out[4] = scales_out[4] * out_rate
+    small_scale = jnp.concatenate([scales_out[0], scales_out[1], scales_out[2]], axis=0)
     small_rates = {"step": RATES[6], "select": RATES[5], "decay": RATES[8], "conv": RATES[3]}
     at_total = {"step": 2, "select": 3, "decay": 4, "conv": 5}
     row_number = lax.broadcasted_iota(jnp.int32, small_scale.shape, 0)
@@ -880,17 +959,9 @@
     for at, step_rate in enumerate((RATES[4], RATES[7], RATES[9])):
         step_rate = rate(6 + at, 1.0 * channels, step_rate, 16)
         vectors_new[21 + at : 22 + at, :] = (
-            line((r.conv_bias, r.step_bias, r.skip_gain)[at]) - wide(step_rate, half) * updates[at]
+            line((r.conv_bias, r.step_bias, r.skip_gain)[at])
+            - wide(step_rate, half) * vectors_new[21 + at : 22 + at, :]
         )
-    gain_grad = take(mine, seq_rows, gain_tiles)
-    moment = DECAY * line(r.norm_moment) + (1.0 - DECAY) * (gain_grad * gain_grad + EPS_FACTOR)
-    update = gain_grad * lax.rsqrt(moment)
-    root = jnp.sqrt(jnp.mean(update * update, axis=1, keepdims=True))
-    vectors_new[0:1, :] = gain_grad
-    vectors_new[1:2, :] = line(r.norm_gain) - RATES[0] / jnp.maximum(1.0, root / CLIP) * update
-    vectors_new[2:3, :] = moment
-    vectors_new[10:18, :] = jnp.zeros((8, half), jnp.float32)
-    vectors_new[27:32, :] = jnp.zeros((5, half), jnp.float32)
 
     for copy in [extra_core, extra_x] + extra_z + back_z + [back_x, back_core]:
         copy.wait_send()
@@ -1068,6 +1139,31 @@
     weights: object
 
 
+class ForwardLazy(NamedTuple):
+    in_weight: object
+    masks: object
+    select_weight: object
+    cot: object
+    out_weight: object
+    step_weight: object
+    decay_log: object
+
+
+class ForwardEarly(NamedTuple):
+    hidden_t: object
+    cot_t: object
+    conv_in: object
+    conv_pre: object
+    conv_out: object
+    step_pre: object
+    step_size: object
+    held: object
+    drive: object
+    enter: object
+    leave: object
+    start: object
+
+
 class ForwardWork(NamedTuple):
     hidden: object
     full: object
@@ -1090,7 +1186,12 @@
 
 
 def forward_block_kernel(*refs):
-    r, _ = gathered(refs, ForwardIn, ForwardOut, ForwardWork)
+    r, left = gathered(refs, ForwardIn, ForwardOut, ForwardWork)
+    lazy, early = len(ForwardLazy._fields), len(ForwardEarly._fields)
+    loads = mirrored(r, ForwardLazy, left[:lazy], left[lazy], False)
+    stores = mirrored(r, ForwardEarly, left[lazy + 1 :], left[lazy + 1 + early], True)
+    for copy in loads:
+        copy.start()
     z, x, core = position()
     place, tp = lax.axis_index("seq"), lax.axis_index("tp")
     full, hidden = r.full, r.hidden
@@ -1223,6 +1324,7 @@
     pair_sems = r.pair_sems
     swap = remote(hidden.at[mine], hidden.at[mine], pair_sems.at[0], pair_sems.at[1], other_half())
     swap.start()
+    loads.in_weight.wait()
 
     rows = hidden.shape[0]
     conv_in, conv_pre, conv_out, rim, ext = (
@@ -1387,11 +1489,10 @@
 
     for step in range(third + 5):
         pump(step)
-        if step == 0:
-            turn(r.cot, r.cot_t)
         if step == 2:
             swap.wait()
-            turn(hidden, r.hidden_t)
+            for copy in loads[1:]:
+                copy.wait()
         if step >= 5:
             value_tile(step - 5)
         if step >= 6:
@@ -1408,7 +1509,9 @@
     for tile in range(third):
         state_tile(tile)
     chain_out()
+    turn(r.cot, r.cot_t)
     chain_middle()
+    turn(hidden, r.hidden_t)
     pump(third + 7)
     gate_tile(2)
     chain_home()
@@ -1416,6 +1519,8 @@
         scan_tile(tile)
     pump(third + 8)
     gate_tile(3)
+    for copy in stores:
+        copy.start()
     for tile in range(third):
         pump(2 * third + 5 + tile)
         out_tile(tile)
@@ -1435,6 +1540,8 @@
             keep(chunk).wait()
     for tile in range(third):
         rim_copy(tile).wait_send()
+    for copy in stores:
+        copy.wait()
 
 
 def own_lanes(at):
@@ -1514,33 +1621,37 @@
         return jax.ShapeDtypeStruct((rows, columns), dtype)
 
     lanes = jax.ShapeDtypeStruct((rows, states, 128), f32)
+    shapes = ForwardOut(*[
+        jax.ShapeDtypeStruct((16, share, rows), low),
+        jax.ShapeDtypeStruct((16, share, rows), low),
+        jax.ShapeDtypeStruct((states + 8, inner), f32),
+        like(inner, low),
+        jax.ShapeDtypeStruct((16, inner), low),
+        like(inner, f32),
+        like(inner, low),
+        like(select_rows, f32),
+        like(inner, f32),
+        like(inner, f32),
+        like(inner, f32),
+        like(inner, f32),
+        lanes,
+        lanes,
+        jax.ShapeDtypeStruct((states, inner), f32),
+        like(inner, low),
+        like(inner, f32),
+        like(inner, low),
+        like(model, f32),
+        jax.ShapeDtypeStruct((1, inner), f32),
+        jax.ShapeDtypeStruct((chunks * 2 // 3, 4, 2, 2, share, width), low),
+    ])
+    specs = ForwardOut(*placed(ForwardOut, ForwardEarly))._replace(
+        weights=pl.BlockSpec(memory_space=pltpu.HBM)
+    )
     outs = pl.pallas_call(
         forward_block_kernel,
-        in_specs=[vmem] * len(ForwardIn._fields),
-        out_specs=[vmem] * (len(ForwardOut._fields) - 1) + [pl.BlockSpec(memory_space=pltpu.HBM)],
-        out_shape=[
-            jax.ShapeDtypeStruct((16, share, rows), low),
-            jax.ShapeDtypeStruct((16, share, rows), low),
-            jax.ShapeDtypeStruct((states + 8, inner), f32),
-            like(inner, low),
-            jax.ShapeDtypeStruct((16, inner), low),
-            like(inner, f32),
-            like(inner, low),
-            like(select_rows, f32),
-            like(inner, f32),
-            like(inner, f32),
-            like(inner, f32),
-            like(inner, f32),
-            lanes,
-            lanes,
-            jax.ShapeDtypeStruct((states, inner), f32),
-            like(inner, low),
-            like(inner, f32),
-            like(inner, low),
-            like(model, f32),
-            jax.ShapeDtypeStruct((1, inner), f32),
-            jax.ShapeDtypeStruct((chunks * 2 // 3, 4, 2, 2, share, width), low),
-        ],
+        in_specs=placed(ForwardIn, ForwardLazy),
+        out_specs=list(specs),
+        out_shape=list(shapes),
         scratch_shapes=[
             pltpu.VMEM((rows, model), low),
             pltpu.VMEM((chunks, 4, 2, 2, share, width), low),
@@ -1560,7 +1671,9 @@
             dma((2, chunks // 3)),
             dma((4, 15)),
             dma((4,)),
-        ],
+        ]
+        + mirrors(ForwardLazy, given)
+        + mirrors(ForwardEarly, shapes),
         compiler_params=pltpu.CompilerParams(
             collective_id=ident, has_side_effects=True, vmem_limit_bytes=FINISH_LIMIT
         ),
@@ -1569,7 +1682,7 @@
     return out._replace(weights=out.weights.reshape(-1, model, width))
 
 
-def backward_part(r, main):
+def backward_part(r, main, loads):
     z, x, core = position()
     place, tp = lax.axis_index("seq"), lax.axis_index("tp")
     low = jnp.bfloat16
@@ -1597,11 +1710,9 @@
     half_rows = r.block.shape[0]
     own_half = pl.ds(pl.multiple_of(tp * half_rows, half_rows), half_rows)
     far_half = pl.ds(pl.multiple_of((1 - tp) * half_rows, half_rows), half_rows)
-    r.branch_send[...] = r.branch[far_half, :].astype(low)
     branch_swap = remote(
         r.branch_send, r.branch_far, pair_sems.at[0], pair_sems.at[1], other_half()
     )
-    branch_swap.start()
 
     held, drive, grad = r.held, r.drive, r.d_mixed
     enter, leave, piece = r.enter, r.leave, r.piece
@@ -1750,7 +1861,7 @@
             sigmoid = jax.nn.sigmoid(pre)
             conv_grad[:, here] = d_conv * (sigmoid * (1.0 + pre * (1.0 - sigmoid)))
             rim_copy(tile).start()
-            if tile % 2:
+            if tile == 1:
                 main.advance()
 
     masks, masks_after = r.masks, r.masks_after
@@ -1786,8 +1897,15 @@
             )
         r.d_value[:, here] = total.astype(low)
 
+    for copy in loads[:3]:
+        copy.wait()
+    main.advance()
     chain_out()
-    main.advance(2)
+    main.advance()
+    for copy in loads[3:]:
+        copy.wait()
+    r.branch_send[...] = r.branch[far_half, :].astype(low)
+    branch_swap.start()
     chain_middle()
     again_tile(0)
     main.advance(1)
@@ -1795,7 +1913,6 @@
     for tile in range(tiles):
         if tile > 0:
             again_tile(tile)
-            main.advance()
         reverse_tile(tile)
         main.advance()
     select_start()
@@ -1810,7 +1927,8 @@
     main.advance()
     for tile in range(tiles):
         conv_tile(tile)
-        main.advance()
+        if tile % 2:
+            main.advance()
 
     def end():
         chain_end()
@@ -1821,7 +1939,14 @@
 
 
 def rest_kernel(channels, model, *refs):
-    r, reducer_refs = gathered(refs, RestIn, RestOut, RestWork)
+    r, left = gathered(refs, RestIn, RestOut, RestWork)
+    lazy, early = len(RestLazy._fields), len(RestEarly._fields)
+    loads = mirrored(r, RestLazy, left, left[lazy], False)
+    left = left[lazy + 1 :]
+    stores = mirrored(r, RestEarly, left, left[early], True)
+    for copy in loads:
+        copy.start()
+    reducer_refs = left[early + 1 :]
     z, x, core = position()
     place, tp = lax.axis_index("seq"), lax.axis_index("tp")
     seq_peers = [(lax.rem(place + step, 16), tp) for step in range(1, 16)]
@@ -1835,10 +1960,12 @@
         + [(r.hidden_t, r.d_value, at, r.in_grad, at) for at in starts],
         reducer_refs,
     )
-    end = backward_part(r, main)
-    finish_part(channels, model, r, main)
+    end = backward_part(r, main, loads)
+    finish_part(channels, model, r, main, stores)
     end()
     main.drain()
+    for copy in stores:
+        copy.wait()
 
 
 class RestIn(NamedTuple):
@@ -1899,6 +2026,37 @@
     vectors_new: object
 
 
+class RestLazy(NamedTuple):
+    cot_t: object
+    gated: object
+    piece: object
+    branch: object
+    held: object
+    drive: object
+    enter: object
+    start: object
+    leave: object
+    d_mixed: object
+    conv_out: object
+    step_pre: object
+    step_weight: object
+    select_weight: object
+    step_size: object
+    conv_pre: object
+    conv_in: object
+    hidden_t: object
+    d_gate: object
+    masks: object
+    masks_after: object
+
+
+class RestEarly(NamedTuple):
+    out_grad: object
+    block_out: object
+    input_grad: object
+    small: object
+
+
 class RestWork(NamedTuple):
     d_value: object
     extra: object
@@ -1931,8 +2089,11 @@
     mine: object
     acc: object
     far: object
+    row_sums: object
     pair: object
     pair_far: object
+    pair_last: object
+    pair_last_far: object
     totals: object
     totals_acc: object
     totals_far: object
@@ -1961,23 +2122,24 @@
     block = (small_rows, 128)
     shape, space = jax.ShapeDtypeStruct, pltpu.VMEM
     vmem = pl.BlockSpec(memory_space=pltpu.VMEM)
-    specs = RestIn(*[vmem] * len(given))._replace(
+    specs = RestIn(*placed(RestIn, RestLazy))._replace(
         weights=pl.BlockSpec(memory_space=pltpu.HBM)
+    )
+    shapes = RestOut(
+        shape((share, inner), f32),
+        shape((half_rows, model), f32),
+        shape((share, columns), f32),
+        shape((half_rows, model), f32),
+        shape((small_rows, inner), f32),
+        shape((5, 128, 128), f32),
+        shape((8, 128), f32),
+        shape((32, inner), f32),
     )
     outs = pl.pallas_call(
         functools.partial(rest_kernel, channels, model),
         in_specs=list(specs),
-        out_specs=[vmem] * len(RestOut._fields),
-        out_shape=[
-            shape((share, inner), f32),
-            shape((half_rows, model), f32),
-            shape((share, columns), f32),
-            shape((half_rows, model), f32),
-            shape((small_rows, inner), f32),
-            shape((5, 128, 128), f32),
-            shape((8, 128), f32),
-            shape((32, inner), f32),
-        ],
+        out_specs=placed(RestOut, RestEarly),
+        out_shape=list(shapes),
         scratch_shapes=[
             space((rows, inner), low),
             space((8, 2, small_rows, 128), low),
@@ -2010,6 +2172,9 @@
             space((seq_rows, 128), f32),
             space((8, seq_rows, 128), f32),
             space((4, model // 128 + 16, 128), f32),
+            space((share, 128), f32),
+            space((8, 128), f32),
+            space((8, 128), f32),
             space((8, 128), f32),
             space((8, 128), f32),
             space((16, 128), f32),
@@ -2021,10 +2186,12 @@
             dma((kept_chunks,)),
             dma((10,)),
             dma((10,)),
-            dma((21,)),
-            dma((21,)),
+            dma((32,)),
+            dma((32,)),
             dma((2,)),
         ]
+        + mirrors(RestLazy, given)
+        + mirrors(RestEarly, shapes)
         + reducer_scratch(inner + columns, share, SHARE_WIDTH),
         compiler_params=pltpu.CompilerParams(
             collective_id=ident, has_side_effects=True, vmem_limit_bytes=FINISH_LIMIT

time: 386 us -> 370 us (0.959)
  Pallas kernels: 374 us -> 358 us
    pallas_call x1, Pallas kernels: 206 us -> 196 us  [rest_block(): pl.pallas_call(functools.partial(rest_kernel, channels, model), in_specs=...]
    pallas_call x1, Pallas kernels: 157 us -> 152 us  [forward_block(): pl.pallas_call(forward_block_kernel, in_specs=placed(ForwardIn, ForwardLa...]
where the time goes in v5:
time: 370 us; the launch traced here: 363 us
  Pallas kernels  358 us (97%)
  local copies, waits for them, and re-layouts  3.85 us (1%)
    pallas_call x1, Pallas kernels, rest_block(): pl.pallas_call(functools.partial(rest_kernel, channels, model), in_specs=...  196 us
    pallas_call x1, Pallas kernels, forward_block(): pl.pallas_call(forward_block_kernel, in_specs=placed(ForwardIn, ForwardLa...  152 us
    pallas_call x1, Pallas kernels, renew(): pl.pallas_call(renew_kernel, grid=(RENEW_TILES,), in_specs=list(specs), o...  9.64 us

profile of v5, /device:TPU:0, one launch (start us, length us, event | category | flops | bytes accessed | tf_op | source)
XLA Modules:
  0.0 363.1 jit_solution(17816094455607754270)
XLA Ops:
  0.7 1.4 concatenate.7
  2.1 0.8 concatenate.6
  2.9 0.1 dynamic_slice.3
  3.0 0.1 compare_bitcast_fusion.2
  3.1 0.8 broadcast_in_dim.31.refs_22_
  3.9 0.8 broadcast_in_dim.28.refs_9_.refs_21_
  4.7 151.9 %shard_map.652 = (bf16[16,128,128]{2,1,0:T(8,128)(2,1)}, bf16[16,128,128]{2,1,0:T(8,128)(2,1)}, f32[24,2048]{1,0:T(8,128)}, bf16[128,2048]{1,0:T(8,128)(2,1)}, b...) custom-call(f32[128,2,2048]{2,1,0:T(2,128)} %refs_9_.1, ...), custom_call_target="tpu_custom_call" | custom-call | tf_op jit(solution)/shard_map/pallas_call | solution.py:1650
  156.5 196.4 %shard_map.653 = (f32[128,2048]{1,0:T(8,128)}, f32[64,2048]{1,0:T(8,128)}, f32[128,4096]{1,0:T(8,128)}, f32[64,2048]{1,0:T(8,128)}, f32[320,2048]{1,0:T(8,128)},...) custom-call(bf16[16,128,128]{2,1,0:T(8,128)(2,1)} %get-tuple-element.77.refs_0_, ...), custom_call_target="tpu_custom_call" | custom-call | tf_op jit(solution)/shard_map/pallas_call | solution.py:2138
  353.0 9.6 %shard_map.654 = (f32[64,2048]{1,0:T(8,128)}, f32[64,2048]{1,0:T(8,128)}, f32[2048]{0:T(1024)}, f32[2048]{0:T(1024)}, bf16[2048]{0:T(1024)(128)(2,1)}, /*index=5...) custom-call(f32[128,4096]{1,0:T(8,128)} %get-tuple-element.98.refs_0, ...), custom_call_target="tpu_custom_call" | custom-call | tf_op jit(solution)/shard_map/pallas_call | solution.py:1091
  (5 shorter events, 0.0 us)

commit v6 on v5

--- a/solution.py
+++ b/solution.py
@@ -21,6 +21,7 @@
 X_FIRST = (4, 8)
 SHARE_WIDTH = 256
 SLOTS = 8
+LAGS = (0, 1, 3, 5)
 RENEW_TILES = 2
 VMEM_LIMIT = 48 * 1024 * 1024
 FINISH_LIMIT = 63 * 1024 * 1024
@@ -526,12 +527,12 @@
             self.put(chunk, (come[0] + come[1]) + come[2], True)
 
     def step(self, step):
-        for level, lag in enumerate((0, 1, 3, 5)):
+        for level, lag in enumerate(LAGS):
             self.stage(level, step - lag)
 
     def advance(self, count=1):
         for _ in range(count):
-            if self.at < self.chunks + 5:
+            if self.at < self.chunks + LAGS[3]:
                 self.step(self.at)
                 self.at += 1
 
@@ -754,6 +755,16 @@
         put_rows(4, part)
 
     lanes = r.lanes
+    ones = jnp.ones((3, 128), jnp.float32)
+    packed = jnp.concatenate(
+        [line(r.select_rows), line(r.decay_rows), line(r.conv_rows), ones[:1, :76]], axis=1
+    )
+    lanes[0:1, :] = line(r.step_rows)
+    lanes[1:2, :] = packed[:, :128]
+    lanes[2:3, :] = packed[:, 128:]
+    lanes[3:4, :] = line(r.in_rows)
+    lanes[4:5, :] = line(r.out_rows)
+    lanes[5:8, :] = ones
     row_at = lax.broadcasted_iota(jnp.int32, lanes.shape, 0)
     lane_at = lax.broadcasted_iota(jnp.int32, lanes.shape, 1)
     counts = jnp.where(row_at == 3, 2.0 * channels, 1.0 * channels)
@@ -904,9 +915,9 @@
     extra_steps = {1: extra_stage_x, 3: extra_stage_z, 5: extra_stage_last, 7: extra_back_x, 9: extra_back_core}
     extra_steps.update({2: out_stage, 10: residual_stage, 11: small_stage})
     extra_steps.update({12: early_begin, 13: early_hops[1], 14: early_end})
-    for step in range(max(main.chunks + 5 - main.at, 15)):
+    for step in range(max(main.chunks + LAGS[3] - main.at, 15)):
         main.advance()
-        in_stage(main.at - 6)
+        in_stage(main.at - 1 - LAGS[3])
         if step < kept_chunks:
             hidden_stage(step)
         if step in extra_steps:
@@ -1864,7 +1875,7 @@
             if tile == 1:
                 main.advance()
 
-    masks, masks_after = r.masks, r.masks_after
+    masks = r.masks
 
     def conv_tile(tile):
         here = columns(tile)
@@ -1893,7 +1904,7 @@
         total = weight[0:1, here] * value
         for lag in range(1, 4):
             total = total + weight[lag : lag + 1, here] * (
-                ext[lag : lag + rows, :] * wide(masks_after[lag - 1], width)
+                ext[lag : lag + rows, :] * wide(masks[2 + lag], width)
             )
         r.d_value[:, here] = total.astype(low)
 
@@ -1991,7 +2002,6 @@
     block: object
     skip_grad: object
     masks: object
-    masks_after: object
     conv_weight: object
     skip_gain: object
     select_weight: object
@@ -1999,7 +2009,12 @@
     decay_log: object
     weights: object
     cot: object
-    lanes: object
+    step_rows: object
+    select_rows: object
+    decay_rows: object
+    conv_rows: object
+    in_rows: object
+    out_rows: object
     norm_gain: object
     norm_moment: object
     in_cols: object
@@ -2047,7 +2062,6 @@
     hidden_t: object
     d_gate: object
     masks: object
-    masks_after: object
 
 
 class RestEarly(NamedTuple):
@@ -2094,6 +2108,7 @@
     pair_far: object
     pair_last: object
     pair_last_far: object
+    lanes: object
     totals: object
     totals_acc: object
     totals_far: object
@@ -2173,6 +2188,7 @@
             space((8, seq_rows, 128), f32),
             space((4, model // 128 + 16, 128), f32),
             space((share, 128), f32),
+            space((8, 128), f32),
             space((8, 128), f32),
             space((8, 128), f32),
             space((8, 128), f32),
@@ -2612,17 +2628,14 @@
         )[:, None]
         for lag in range(conv_taps)
     ]
-    masks = jnp.broadcast_to(jnp.stack(same_docs[1:]), (conv_taps - 1, row_count, 128))
     ids_after = window[conv_taps - 1 :]
     same_after = [
         (ids_after[lag : lag + row_count] == local_ids).astype(jnp.float32)[:, None]
         for lag in range(1, conv_taps)
     ]
-    masks_after = jnp.broadcast_to(jnp.stack(same_after), (conv_taps - 1, row_count, 128))
-    lanes = jnp.concatenate(
-        [step_rows, select_rows, decay_rows, conv_rows, jnp.ones((76,), jnp.float32)]
-        + [in_rows, out_rows, jnp.ones((384,), jnp.float32)]
-    ).reshape(8, 128)
+    masks = jnp.broadcast_to(
+        jnp.stack(same_docs[1:] + same_after), (2 * (conv_taps - 1), row_count, 128)
+    )
     f = forward_block(
         0,
         ForwardIn(
@@ -2647,9 +2660,13 @@
         RestIn(
             block=block_in,
             cot=cotangent,
-            lanes=lanes,
+            step_rows=step_rows,
+            select_rows=select_rows,
+            decay_rows=decay_rows,
+            conv_rows=conv_rows,
+            in_rows=in_rows,
+            out_rows=out_rows,
             masks=masks,
-            masks_after=masks_after,
             conv_weight=conv_weight,
             select_weight=select_weight,
             step_weight=step_weight,

time: 370 us -> 368 us (level)
  no operation moved by 1% of the time
where the time goes in v6:
time: 368 us; the launch traced here: 361 us
  Pallas kernels  358 us (97%)
    pallas_call x1, Pallas kernels, rest_block(): pl.pallas_call(functools.partial(rest_kernel, channels, model), in_specs=...  197 us
    pallas_call x1, Pallas kernels, forward_block(): pl.pallas_call(forward_block_kernel, in_specs=placed(ForwardIn, ForwardLa...  152 us
    pallas_call x1, Pallas kernels, renew(): pl.pallas_call(renew_kernel, grid=(RENEW_TILES,), in_specs=list(specs), o...  9.64 us

profile of v6, /device:TPU:0, one launch (start us, length us, event | category | flops | bytes accessed | tf_op | source)
XLA Modules:
  0.0 361.2 jit_solution(3443956249659973620)
XLA Ops:
  0.7 0.8 concatenate.3
  1.5 0.1 dynamic_slice.3
  1.6 0.1 compare_bitcast_fusion
  1.7 0.9 broadcast_in_dim.12.refs_9_.refs_21_
  2.6 151.9 %shard_map.652 = (bf16[16,128,128]{2,1,0:T(8,128)(2,1)}, bf16[16,128,128]{2,1,0:T(8,128)(2,1)}, f32[24,2048]{1,0:T(8,128)}, bf16[128,2048]{1,0:T(8,128)(2,1)}, b...) custom-call(f32[128,2,2048]{2,1,0:T(2,128)} %refs_9_.1, ...), custom_call_target="tpu_custom_call" | custom-call | tf_op jit(solution)/shard_map/pallas_call | solution.py:1661
  154.5 196.6 %shard_map.653 = (f32[128,2048]{1,0:T(8,128)}, f32[64,2048]{1,0:T(8,128)}, f32[128,4096]{1,0:T(8,128)}, f32[64,2048]{1,0:T(8,128)}, f32[320,2048]{1,0:T(8,128)},...) custom-call(bf16[16,128,128]{2,1,0:T(8,128)(2,1)} %get-tuple-element.77.refs_0_, ...), custom_call_target="tpu_custom_call" | custom-call | tf_op jit(solution)/shard_map/pallas_call | solution.py:2153
  351.1 9.6 %shard_map.654 = (f32[64,2048]{1,0:T(8,128)}, f32[64,2048]{1,0:T(8,128)}, f32[2048]{0:T(1024)}, f32[2048]{0:T(1024)}, bf16[2048]{0:T(1024)(128)(2,1)}, /*index=5...) custom-call(f32[128,4096]{1,0:T(8,128)} %get-tuple-element.98.refs_0, ...), custom_call_target="tpu_custom_call" | custom-call | tf_op jit(solution)/shard_map/pallas_call | solution.py:1102
  (4 shorter events, 0.0 us)
